TPU v7x, 512 devices: a whole 4x4x16 slice. The times are simulated.
512 devices in a mesh: view: 8 (over y, x_lo), slab: 32 (over z, core), row: 2 (over x_hi).
Axes of the slice: x: 4 (x_hi: 2, x_lo: 2; x = x_hi * 2 + x_lo), y: 4, z: 16, core: 2. Of those that a mesh axis runs over, the one named last changes fastest.
Arguments:
- data: float32 [8, 256, 128, 256], P('view', 'slab', 'row'), may hold values from 0.2 to 5
- estimate: float32 [256, 128, 256], P('slab', 'row'), may hold values from 0.5 to 2
- profile: float32 [8, 3, 5], P('view'), may hold values from 0.1 to 1
- band: int32 [8, 3], P('view'), may hold values from 1 to 4, as said below
- axes_perm: int32 [8, 3], P('view'), may hold values from 0 to 2, each once within a row
Outputs:
- updated: float32 [256, 128, 256], P('slab', 'row')
Inputs may be any that keep to these rules, and one draw needn't show every extreme that they name: Some view's detection band (profile 0) is exactly 4.
All inputs are finite; a program needn't handle non-finite values.
Results may differ from a plain program's by a relative error of at most 0.0001.
Values sent between devices are 32-bit elements; how exact they have to be, the bound alone decides.
No kernel may reach another device: no remote copies, remote signals or barrier semaphores. Data moves between devices by JAX's collectives and lax.ppermute only.
A program may use at most 64 MiB of HBM per device.

v0:
```python
import jax
import jax.numpy as jnp
import numpy as np
from jax import lax
from jax.sharding import PartitionSpec as P

PASSES = 3


TAU = 0.05
EPS2 = 0.25


def padded_2(block, sides, width):
    for axis, dim in sides:
        count = lax.axis_size(axis)
        forward = [(i, i + 1) for i in range(count - 1)]
        backward = [(target, source) for source, target in forward]
        low = lax.ppermute(
            lax.slice_in_dim(block, block.shape[dim] - width, None, axis=dim), axis, forward
        )
        high = lax.ppermute(lax.slice_in_dim(block, 0, width, axis=dim), axis, backward)
        block = jnp.concatenate([low, block, high], axis=dim)
    return block


def kernels(prof, band_row, perm_row):
    width = prof.shape[1] - 1
    taps = np.abs(np.arange(-width, width + 1))
    select = perm_row[:, None] == jnp.arange(3, dtype=jnp.int32)[None, :]
    chosen = jnp.dot(select.astype(jnp.float32), prof, precision=lax.Precision.HIGHEST)
    reach = jnp.sum(jnp.where(select, band_row[None, :], 0), axis=1)
    weights = chosen[:, taps] * (
        jnp.asarray(taps, dtype=jnp.int32)[None, :] <= reach[:, None]
    ).astype(jnp.float32)
    return weights / jnp.sum(weights, axis=1, keepdims=True)


def blur_valid(block, weights, axis_num, width):
    length = block.shape[axis_num] - 2 * width
    total = jnp.zeros(block.shape[:axis_num] + (length,) + block.shape[axis_num + 1 :], jnp.float32)
    for offset in range(-width, width + 1):
        total = total + weights[axis_num, offset + width] * lax.slice_in_dim(
            block, width + offset, width + offset + length, axis=axis_num
        )
    return total


def blur_block(near, weights, width):
    padded = jnp.pad(near, ((0, 0), (0, 0), (width, width)))
    for axis_num in range(3):
        padded = blur_valid(padded, weights, axis_num, width)
    return padded


def tv_step(padded, mask):
    base = padded[:-1, :-1, :-1]
    grad_z = padded[1:, :-1, :-1] - base
    grad_y = padded[:-1, 1:, :-1] - base
    grad_x = padded[:-1, :-1, 1:] - base
    scale = mask[:-1, :-1, :-1] / jnp.sqrt(
        grad_z * grad_z + grad_y * grad_y + grad_x * grad_x + EPS2
    )
    flux_z = grad_z * scale
    flux_y = grad_y * scale
    flux_x = grad_x * scale
    spread = flux_z[1:, 1:, 1:] - flux_z[:-1, 1:, 1:]
    spread = spread + flux_y[1:, 1:, 1:] - flux_y[1:, :-1, 1:]
    spread = spread + flux_x[1:, 1:, 1:] - flux_x[1:, 1:, :-1]
    return (padded[1:-1, 1:-1, 1:-1] + TAU * spread) * mask[1:-1, 1:-1, 1:-1]


def body(data, estimate, profile, band, axes_perm):
    width = profile.shape[2] - 1
    weights = kernels(profile[0], band[0], axes_perm[0])
    near = padded_2(estimate, (("slab", 0), ("row", 1)), width)
    blurred = blur_block(near, weights, width)
    ratio = data[0] / blurred
    near = padded_2(ratio, (("slab", 0), ("row", 1)), width)
    back = blur_block(near, weights, width)
    views = lax.axis_size("view")
    planes, rows, full_x = estimate.shape
    z_start = lax.axis_index("slab") * planes
    y_start = lax.axis_index("row") * rows
    z_limit = planes * lax.axis_size("slab")
    y_limit = rows * lax.axis_size("row")
    total = lax.psum(back, "view")
    field = estimate * (total * (1.0 / views))
    x_start = 0
    for step in range(PASSES):
        padded = jnp.pad(padded_2(field, (("slab", 0), ("row", 1)), 1), ((0, 0), (0, 0), (1, 1)))
        shape = padded.shape
        z_index = z_start - 1 + jnp.arange(shape[0])
        y_index = y_start - 1 + jnp.arange(shape[1])
        x_index = x_start - 1 + jnp.arange(shape[2])
        inside_z = (z_index >= 0) & (z_index < z_limit)
        inside_y = (y_index >= 0) & (y_index < y_limit)
        inside_x = (x_index >= 0) & (x_index < full_x)
        field = tv_step(
            padded,
            (inside_z[:, None, None] & inside_y[None, :, None] & inside_x[None, None, :]).astype(
                jnp.float32
            ),
        )
    return field


def solution(mesh):
    placed = (
        P("view", "slab", "row", None),
        P("slab", "row", None),
        P("view", None, None),
        P("view", None),
        P("view", None),
    )
    return jax.shard_map(
        body, mesh=mesh, in_specs=placed, out_specs=P("slab", "row", None), check_vma=False
    )
```

profile of v0, /device:TPU:97, one launch (start us, length us, event | category | flops | bytes accessed | tf_op | source)
XLA Modules:
  0.0 257.0 jit_solution(13747692929972099418)
XLA Ops:
  7.7 2.6 %collective-permute-start.1 = (f32[4,64,256]{2,1,0:T(8,128)S(1)}, f32[4,64,256]{2,1,0:T(8,128)S(1)}, u32[]{:S(2)}, u32[]{:S(2)}) collective-permute-start(f32[4,64,256]{2,1,0:T(8,128)S(1)} %get-tuple-element.35), channel_id=1, source_target_pairs={{2,0},{4,2},{6,4},{8,6},{10,8},{12,10},{14,12},{16,14},{18,16},{20... | collective-permute-start | bytes 786440 | tf_op jit(solution)/shard_map/ppermute | solution.py:22
  10.3 4.7 %collective-permute-start = (f32[4,64,256]{2,1,0:T(8,128)S(1)}, f32[4,64,256]{2,1,0:T(8,128)S(1)}, u32[]{:S(2)}, u32[]{:S(2)}) collective-permute-start(f32[4,64,256]{2,1,0:T(8,128)S(1)} %get-tuple-element.36), channel_id=1, source_target_pairs={{0,2},{2,4},{4,6},{6,8},{8,10},{10,12},{12,14},{14,16},{16,18},{18... | collective-permute-start | bytes 786440 | tf_op jit(solution)/shard_map/ppermute | solution.py:19
  18.4 4.7 %collective-permute-start.2 = (f32[16,4,256]{2,1,0:T(4,128)S(1)}, f32[16,4,256]{2,1,0:T(4,128)S(1)}, u32[]{:S(2)}, u32[]{:S(2)}) collective-permute-start(f32[16,4,256]{2,1,0:T(4,128)S(1)} %get-tuple-element.19), channel_id=1, source_target_pairs={{0,1},{2,3},{4,5},{6,7},{8,9},{10,11},{12,13},{14,15},{16,17},{18,... | collective-permute-start | bytes 196616 | tf_op jit(solution)/shard_map/ppermute | solution.py:19
  24.9 5.2 %collective-permute-done.3 = f32[16,4,256]{2,1,0:T(4,128)S(1)} collective-permute-done((f32[16,4,256]{2,1,0:T(4,128)S(1)}, f32[16,4,256]{2,1,0:T(4,128)S(1)}, u32[]{:S(2)}, u32[]{:S(2)}) %collective-permute-start.3) | collective-permute-done | bytes 65568 | tf_op jit(solution)/shard_map/ppermute | solution.py:22
  30.8 6.2 %fusion.10 = f32[8,72,264]{2,1,0:T(8,128)S(1)} fusion(f32[16,72,264]{2,1,0:T(8,128)S(1)} %select_maximum_fusion.4, f32[]{:T(128)} %bitcast.14, f32[]{:T(128)} %bitcast.13, f32[]{:T(128)} %bitcast.12, f32[]{:T(128)} %bitcast.11, f32[]{:T(128)} %bitcast.10, f32[]{:T(128)} %bitcast.9, f32[]{:T(128)} %bitcast.8, f32[]{:T(128)} %bitcast.7, f32[]{:T(128)} %bitcast.5), kind=kLoop, calls=%fused_computation.56 | loop fusion | flops 2585088 | bytes 6082596 | tf_op jit(solution)/shard_map/add | solution.py:43
  37.0 6.3 %fusion.26 = f32[8,64,264]{2,1,0:T(8,128)S(1)} fusion(f32[8,72,264]{2,1,0:T(8,128)S(1)} %fusion.10, f32[]{:T(128)} %bitcast.22, f32[]{:T(128)} %bitcast.21, f32[]{:T(128)} %bitcast.20, f32[]{:T(128)} %bitcast.19, f32[]{:T(128)} %bitcast.18, f32[]{:T(128)} %bitcast.17, f32[]{:T(128)} %bitcast.16, f32[]{:T(128)} %bitcast.15, f32[]{:T(128)} %bitcast.4), kind=kLoop, calls=%fused_computation.90 | loop fusion | flops 2297856 | bytes 5406756 | tf_op jit(solution)/shard_map/add | solution.py:43
  43.3 6.7 %fusion.52 = f32[8,64,256]{2,1,0:T(8,128)S(1)} fusion(f32[8,64,264]{2,1,0:T(8,128)S(1)} %fusion.26, f32[1,8,64,256]{3,2,1,0:T(8,128)S(1)} %copy-done.1, f32[]{:T(128)} %bitcast.30, f32[]{:T(128)} %bitcast.29, f32[]{:T(128)} %bitcast.28, f32[]{:T(128)} %bitcast.27, f32[]{:T(128)} %bitcast.26, f32[]{:T(128)} %bitcast.25, f32[]{:T(128)} %bitcast.24, ...), kind=kLoop, calls=%fused_computation.149 | loop fusion | flops 2359296 | bytes 5767204 | tf_op jit(solution)/shard_map/div | solution.py:78
  50.1 6.4 %collective-permute-start.4 = (f32[4,64,256]{2,1,0:T(8,128)S(1)}, f32[4,64,256]{2,1,0:T(8,128)S(1)}, u32[]{:S(2)}, u32[]{:S(2)}) collective-permute-start(f32[4,64,256]{2,1,0:T(8,128)S(1)} %get-tuple-element.33), channel_id=1, source_target_pairs={{0,2},{2,4},{4,6},{6,8},{8,10},{10,12},{12,14},{14,16},{16,18},{18... | collective-permute-start | bytes 786440 | tf_op jit(solution)/shard_map/ppermute | solution.py:19
  59.8 5.6 %collective-permute-done.5 = f32[4,64,256]{2,1,0:T(8,128)S(1)} collective-permute-done((f32[4,64,256]{2,1,0:T(8,128)S(1)}, f32[4,64,256]{2,1,0:T(8,128)S(1)}, u32[]{:S(2)}, u32[]{:S(2)}) %collective-permute-start.5) | collective-permute-done | bytes 262176 | tf_op jit(solution)/shard_map/ppermute | solution.py:22
  68.1 5.2 %collective-permute-done.7 = f32[16,4,256]{2,1,0:T(4,128)S(1)} collective-permute-done((f32[16,4,256]{2,1,0:T(4,128)S(1)}, f32[16,4,256]{2,1,0:T(4,128)S(1)}, u32[]{:S(2)}, u32[]{:S(2)}) %collective-permute-start.7) | collective-permute-done | bytes 65568 | tf_op jit(solution)/shard_map/ppermute | solution.py:22
  74.0 6.2 %fusion.2 = f32[8,72,264]{2,1,0:T(8,128)S(1)} fusion(f32[16,72,264]{2,1,0:T(8,128)S(1)} %select_maximum_fusion, f32[]{:T(128)} %bitcast.14, f32[]{:T(128)} %bitcast.13, f32[]{:T(128)} %bitcast.12, f32[]{:T(128)} %bitcast.11, f32[]{:T(128)} %bitcast.10, f32[]{:T(128)} %bitcast.9, f32[]{:T(128)} %bitcast.8, f32[]{:T(128)} %bitcast.7, f32[]{:T(128)} %bitcast.5), kind=kLoop, calls=%fused_computation.39 | loop fusion | flops 2585088 | bytes 6082596 | tf_op jit(solution)/shard_map/add | solution.py:43
  80.1 6.3 %fusion.18 = f32[8,64,264]{2,1,0:T(8,128)S(1)} fusion(f32[8,72,264]{2,1,0:T(8,128)S(1)} %fusion.2, f32[]{:T(128)} %bitcast.22, f32[]{:T(128)} %bitcast.21, f32[]{:T(128)} %bitcast.20, f32[]{:T(128)} %bitcast.19, f32[]{:T(128)} %bitcast.18, f32[]{:T(128)} %bitcast.17, f32[]{:T(128)} %bitcast.16, f32[]{:T(128)} %bitcast.15, f32[]{:T(128)} %bitcast.4), kind=kLoop, calls=%fused_computation.73 | loop fusion | flops 2297856 | bytes 5406756 | tf_op jit(solution)/shard_map/add | solution.py:43
  86.4 7.5 %fusion.43 = f32[8,64,256]{2,1,0:T(8,128)} fusion(f32[8,64,264]{2,1,0:T(8,128)S(1)} %fusion.18, f32[]{:T(128)} %bitcast.30, f32[]{:T(128)} %bitcast.29, f32[]{:T(128)} %bitcast.28, f32[]{:T(128)} %bitcast.27, f32[]{:T(128)} %bitcast.26, f32[]{:T(128)} %bitcast.25, f32[]{:T(128)} %bitcast.24, f32[]{:T(128)} %bitcast.23, f32[]{:T(128)} %bitcast.3), kind=kLoop, calls=%fused_computation.131 | loop fusion | flops 2228224 | bytes 5242916 | tf_op jit(solution)/shard_map/add | solution.py:43
  94.0 85.5 %all-reduce.7.cloned.1.call-done = f32[8,64,256]{2,1,0:T(8,128)} async-done(((f32[8,64,256]{2,1,0:T(8,128)}), f32[8,64,256]{2,1,0:T(8,128)}) %all-reduce.7.cloned.1.call-update) | async-done | bytes 524304 | tf_op jit(solution)/shard_map/psum | solution.py:87
  180.6 9.5 %collective-permute-start.8 = (f32[1,64,256]{2,1,0:T(8,128)S(1)}, f32[1,64,256]{2,1,0:T(8,128)S(1)}, u32[]{:S(2)}, u32[]{:S(2)}) collective-permute-start(f32[1,64,256]{2,1,0:T(8,128)S(1)} %get-tuple-element.31), channel_id=1, source_target_pairs={{0,2},{2,4},{4,6},{6,8},{8,10},{10,12},{12,14},{14,16},{16,18},{18... | collective-permute-start | bytes 196616 | tf_op jit(solution)/shard_map/ppermute | solution.py:19
  192.1 4.8 %collective-permute-done.9 = f32[1,64,256]{2,1,0:T(8,128)S(1)} collective-permute-done((f32[1,64,256]{2,1,0:T(8,128)S(1)}, f32[1,64,256]{2,1,0:T(8,128)S(1)}, u32[]{:S(2)}, u32[]{:S(2)}) %collective-permute-start.9) | collective-permute-done | bytes 65568 | tf_op jit(solution)/shard_map/ppermute | solution.py:22
  197.0 4.3 %collective-permute-start.10 = (f32[10,1,256]{2,1,0:T(1,128)S(1)}, f32[10,1,256]{2,1,0:T(1,128)S(1)}, u32[]{:S(2)}, u32[]{:S(2)}) collective-permute-start(f32[10,1,256]{2,1,0:T(1,128)S(1)} %get-tuple-element.25), channel_id=1, source_target_pairs={{0,1},{2,3},{4,5},{6,7},{8,9},{10,11},{12,13},{14,15},{16,17},{18,... | collective-permute-start | bytes 30728 | tf_op jit(solution)/shard_map/ppermute | solution.py:19
  202.8 4.4 %collective-permute-done.11 = f32[10,1,256]{2,1,0:T(1,128)S(1)} collective-permute-done((f32[10,1,256]{2,1,0:T(1,128)S(1)}, f32[10,1,256]{2,1,0:T(1,128)S(1)}, u32[]{:S(2)}, u32[]{:S(2)}) %collective-permute-start.11) | collective-permute-done | bytes 10272 | tf_op jit(solution)/shard_map/ppermute | solution.py:22
  209.7 3.3 %collective-permute-start.12 = (f32[1,64,256]{2,1,0:T(8,128)S(1)}, f32[1,64,256]{2,1,0:T(8,128)S(1)}, u32[]{:S(2)}, u32[]{:S(2)}) collective-permute-start(f32[1,64,256]{2,1,0:T(8,128)S(1)} %get-tuple-element.29), channel_id=1, source_target_pairs={{0,2},{2,4},{4,6},{6,8},{8,10},{10,12},{12,14},{14,16},{16,18},{18... | collective-permute-start | bytes 196616 | tf_op jit(solution)/shard_map/ppermute | solution.py:19
  214.9 4.9 %collective-permute-done.13 = f32[1,64,256]{2,1,0:T(8,128)S(1)} collective-permute-done((f32[1,64,256]{2,1,0:T(8,128)S(1)}, f32[1,64,256]{2,1,0:T(8,128)S(1)}, u32[]{:S(2)}, u32[]{:S(2)}) %collective-permute-start.13) | collective-permute-done | bytes 65568 | tf_op jit(solution)/shard_map/ppermute | solution.py:22
  222.7 4.4 %collective-permute-done.15 = f32[10,1,256]{2,1,0:T(1,128)S(1)} collective-permute-done((f32[10,1,256]{2,1,0:T(1,128)S(1)}, f32[10,1,256]{2,1,0:T(1,128)S(1)}, u32[]{:S(2)}, u32[]{:S(2)}) %collective-permute-start.15) | collective-permute-done | bytes 10272 | tf_op jit(solution)/shard_map/ppermute | solution.py:22
  229.5 3.3 %collective-permute-start.16 = (f32[1,64,256]{2,1,0:T(8,128)S(1)}, f32[1,64,256]{2,1,0:T(8,128)S(1)}, u32[]{:S(2)}, u32[]{:S(2)}) collective-permute-start(f32[1,64,256]{2,1,0:T(8,128)S(1)} %get-tuple-element.27), channel_id=1, source_target_pairs={{0,2},{2,4},{4,6},{6,8},{8,10},{10,12},{12,14},{14,16},{16,18},{18... | collective-permute-start | bytes 196616 | tf_op jit(solution)/shard_map/ppermute | solution.py:19
  234.8 4.9 %collective-permute-done.17 = f32[1,64,256]{2,1,0:T(8,128)S(1)} collective-permute-done((f32[1,64,256]{2,1,0:T(8,128)S(1)}, f32[1,64,256]{2,1,0:T(8,128)S(1)}, u32[]{:S(2)}, u32[]{:S(2)}) %collective-permute-start.17) | collective-permute-done | bytes 65568 | tf_op jit(solution)/shard_map/ppermute | solution.py:22
  242.3 4.6 %collective-permute-done.19 = f32[10,1,256]{2,1,0:T(1,128)S(1)} collective-permute-done((f32[10,1,256]{2,1,0:T(1,128)S(1)}, f32[10,1,256]{2,1,0:T(1,128)S(1)}, u32[]{:S(2)}, u32[]{:S(2)}) %collective-permute-start.19) | collective-permute-done | bytes 10272 | tf_op jit(solution)/shard_map/ppermute | solution.py:22
  (72 shorter events, 35.7 us)
Async XLA Ops:
  6.5 10.1 %copy-start.2 = (s32[9]{0:T(128)S(1)}, s32[9]{0:T(128)}, u32[]{:S(2)}) copy-start(s32[9]{0:T(128)} %constant.43.clone) | copy-start | bytes 112
  6.5 11.7 %copy-start = (f32[8,64,256]{2,1,0:T(8,128)S(1)}, f32[8,64,256]{2,1,0:T(8,128)}, u32[]{:S(2)}) copy-start(f32[8,64,256]{2,1,0:T(8,128)} %param.9) | copy-start | bytes 1572868
  6.5 173.0 %all-reduce.7.cloned.1.call-start = ((), (), s32[]{:S(2)}) async-start(), calls=%async_computation | async-start | bytes 1048576 | tf_op jit(solution)/shard_map/psum | solution.py:87
  7.7 10.6 %collective-permute-start.1 = (f32[4,64,256]{2,1,0:T(8,128)S(1)}, f32[4,64,256]{2,1,0:T(8,128)S(1)}, u32[]{:S(2)}, u32[]{:S(2)}) collective-permute-start(f32[4,64,256]{2,1,0:T(8,128)S(1)} %get-tuple-element.35), channel_id=1, source_target_pairs={{2,0},{4,2},{6,4},{8,6},{10,8},{12,10},{14,12},{16,14},{18,16},{20... | collective-permute-start | bytes 786440 | tf_op jit(solution)/shard_map/ppermute | solution.py:22
  10.3 8.0 %collective-permute-start = (f32[4,64,256]{2,1,0:T(8,128)S(1)}, f32[4,64,256]{2,1,0:T(8,128)S(1)}, u32[]{:S(2)}, u32[]{:S(2)}) collective-permute-start(f32[4,64,256]{2,1,0:T(8,128)S(1)} %get-tuple-element.36), channel_id=1, source_target_pairs={{0,2},{2,4},{4,6},{6,8},{8,10},{10,12},{12,14},{14,16},{16,18},{18... | collective-permute-start | bytes 786440 | tf_op jit(solution)/shard_map/ppermute | solution.py:19
  18.4 6.6 %collective-permute-start.2 = (f32[16,4,256]{2,1,0:T(4,128)S(1)}, f32[16,4,256]{2,1,0:T(4,128)S(1)}, u32[]{:S(2)}, u32[]{:S(2)}) collective-permute-start(f32[16,4,256]{2,1,0:T(4,128)S(1)} %get-tuple-element.19), channel_id=1, source_target_pairs={{0,1},{2,3},{4,5},{6,7},{8,9},{10,11},{12,13},{14,15},{16,17},{18,... | collective-permute-start | bytes 196616 | tf_op jit(solution)/shard_map/ppermute | solution.py:19
  23.0 7.1 %collective-permute-start.3 = (f32[16,4,256]{2,1,0:T(4,128)S(1)}, f32[16,4,256]{2,1,0:T(4,128)S(1)}, u32[]{:S(2)}, u32[]{:S(2)}) collective-permute-start(f32[16,4,256]{2,1,0:T(4,128)S(1)} %get-tuple-element.20), channel_id=1, source_target_pairs={{1,0},{3,2},{5,4},{7,6},{9,8},{11,10},{13,12},{15,14},{17,16},{19,... | collective-permute-start | bytes 196616 | tf_op jit(solution)/shard_map/ppermute | solution.py:22
  37.0 6.3 %copy-start.1 = (f32[1,8,64,256]{3,2,1,0:T(8,128)S(1)}, f32[1,8,64,256]{3,2,1,0:T(8,128)}, u32[]{:S(2)}) copy-start(f32[1,8,64,256]{3,2,1,0:T(8,128)} %param.8) | copy-start | bytes 1572868
  50.1 9.7 %collective-permute-start.4 = (f32[4,64,256]{2,1,0:T(8,128)S(1)}, f32[4,64,256]{2,1,0:T(8,128)S(1)}, u32[]{:S(2)}, u32[]{:S(2)}) collective-permute-start(f32[4,64,256]{2,1,0:T(8,128)S(1)} %get-tuple-element.33), channel_id=1, source_target_pairs={{0,2},{2,4},{4,6},{6,8},{8,10},{10,12},{12,14},{14,16},{16,18},{18... | collective-permute-start | bytes 786440 | tf_op jit(solution)/shard_map/ppermute | solution.py:19
  56.5 8.9 %collective-permute-start.5 = (f32[4,64,256]{2,1,0:T(8,128)S(1)}, f32[4,64,256]{2,1,0:T(8,128)S(1)}, u32[]{:S(2)}, u32[]{:S(2)}) collective-permute-start(f32[4,64,256]{2,1,0:T(8,128)S(1)} %get-tuple-element.34), channel_id=1, source_target_pairs={{2,0},{4,2},{6,4},{8,6},{10,8},{12,10},{14,12},{16,14},{18,16},{20... | collective-permute-start | bytes 786440 | tf_op jit(solution)/shard_map/ppermute | solution.py:22
  65.5 2.6 %collective-permute-start.6 = (f32[16,4,256]{2,1,0:T(4,128)S(1)}, f32[16,4,256]{2,1,0:T(4,128)S(1)}, u32[]{:S(2)}, u32[]{:S(2)}) collective-permute-start(f32[16,4,256]{2,1,0:T(4,128)S(1)} %get-tuple-element.17), channel_id=1, source_target_pairs={{0,1},{2,3},{4,5},{6,7},{8,9},{10,11},{12,13},{14,15},{16,17},{18,... | collective-permute-start | bytes 196616 | tf_op jit(solution)/shard_map/ppermute | solution.py:19
  66.8 6.5 %collective-permute-start.7 = (f32[16,4,256]{2,1,0:T(4,128)S(1)}, f32[16,4,256]{2,1,0:T(4,128)S(1)}, u32[]{:S(2)}, u32[]{:S(2)}) collective-permute-start(f32[16,4,256]{2,1,0:T(4,128)S(1)} %get-tuple-element.18), channel_id=1, source_target_pairs={{1,0},{3,2},{5,4},{7,6},{9,8},{11,10},{13,12},{15,14},{17,16},{19,... | collective-permute-start | bytes 196616 | tf_op jit(solution)/shard_map/ppermute | solution.py:22
  180.6 11.5 %collective-permute-start.8 = (f32[1,64,256]{2,1,0:T(8,128)S(1)}, f32[1,64,256]{2,1,0:T(8,128)S(1)}, u32[]{:S(2)}, u32[]{:S(2)}) collective-permute-start(f32[1,64,256]{2,1,0:T(8,128)S(1)} %get-tuple-element.31), channel_id=1, source_target_pairs={{0,2},{2,4},{4,6},{6,8},{8,10},{10,12},{12,14},{14,16},{16,18},{18... | collective-permute-start | bytes 196616 | tf_op jit(solution)/shard_map/ppermute | solution.py:19
  190.2 6.8 %collective-permute-start.9 = (f32[1,64,256]{2,1,0:T(8,128)S(1)}, f32[1,64,256]{2,1,0:T(8,128)S(1)}, u32[]{:S(2)}, u32[]{:S(2)}) collective-permute-start(f32[1,64,256]{2,1,0:T(8,128)S(1)} %get-tuple-element.32), channel_id=1, source_target_pairs={{2,0},{4,2},{6,4},{8,6},{10,8},{12,10},{14,12},{16,14},{18,16},{20... | collective-permute-start | bytes 196616 | tf_op jit(solution)/shard_map/ppermute | solution.py:22
  197.0 5.8 %collective-permute-start.10 = (f32[10,1,256]{2,1,0:T(1,128)S(1)}, f32[10,1,256]{2,1,0:T(1,128)S(1)}, u32[]{:S(2)}, u32[]{:S(2)}) collective-permute-start(f32[10,1,256]{2,1,0:T(1,128)S(1)} %get-tuple-element.25), channel_id=1, source_target_pairs={{0,1},{2,3},{4,5},{6,7},{8,9},{10,11},{12,13},{14,15},{16,17},{18,... | collective-permute-start | bytes 30728 | tf_op jit(solution)/shard_map/ppermute | solution.py:19
  201.3 5.9 %collective-permute-start.11 = (f32[10,1,256]{2,1,0:T(1,128)S(1)}, f32[10,1,256]{2,1,0:T(1,128)S(1)}, u32[]{:S(2)}, u32[]{:S(2)}) collective-permute-start(f32[10,1,256]{2,1,0:T(1,128)S(1)} %get-tuple-element.26), channel_id=1, source_target_pairs={{1,0},{3,2},{5,4},{7,6},{9,8},{11,10},{13,12},{15,14},{17,16},{19,... | collective-permute-start | bytes 30728 | tf_op jit(solution)/shard_map/ppermute | solution.py:22
  209.7 5.2 %collective-permute-start.12 = (f32[1,64,256]{2,1,0:T(8,128)S(1)}, f32[1,64,256]{2,1,0:T(8,128)S(1)}, u32[]{:S(2)}, u32[]{:S(2)}) collective-permute-start(f32[1,64,256]{2,1,0:T(8,128)S(1)} %get-tuple-element.29), channel_id=1, source_target_pairs={{0,2},{2,4},{4,6},{6,8},{8,10},{10,12},{12,14},{14,16},{16,18},{18... | collective-permute-start | bytes 196616 | tf_op jit(solution)/shard_map/ppermute | solution.py:19
  213.0 6.8 %collective-permute-start.13 = (f32[1,64,256]{2,1,0:T(8,128)S(1)}, f32[1,64,256]{2,1,0:T(8,128)S(1)}, u32[]{:S(2)}, u32[]{:S(2)}) collective-permute-start(f32[1,64,256]{2,1,0:T(8,128)S(1)} %get-tuple-element.30), channel_id=1, source_target_pairs={{2,0},{4,2},{6,4},{8,6},{10,8},{12,10},{14,12},{16,14},{18,16},{20... | collective-permute-start | bytes 196616 | tf_op jit(solution)/shard_map/ppermute | solution.py:22
  219.8 2.9 %collective-permute-start.14 = (f32[10,1,256]{2,1,0:T(1,128)S(1)}, f32[10,1,256]{2,1,0:T(1,128)S(1)}, u32[]{:S(2)}, u32[]{:S(2)}) collective-permute-start(f32[10,1,256]{2,1,0:T(1,128)S(1)} %get-tuple-element.23), channel_id=1, source_target_pairs={{0,1},{2,3},{4,5},{6,7},{8,9},{10,11},{12,13},{14,15},{16,17},{18,... | collective-permute-start | bytes 30728 | tf_op jit(solution)/shard_map/ppermute | solution.py:19
  221.2 5.9 %collective-permute-start.15 = (f32[10,1,256]{2,1,0:T(1,128)S(1)}, f32[10,1,256]{2,1,0:T(1,128)S(1)}, u32[]{:S(2)}, u32[]{:S(2)}) collective-permute-start(f32[10,1,256]{2,1,0:T(1,128)S(1)} %get-tuple-element.24), channel_id=1, source_target_pairs={{1,0},{3,2},{5,4},{7,6},{9,8},{11,10},{13,12},{15,14},{17,16},{19,... | collective-permute-start | bytes 30728 | tf_op jit(solution)/shard_map/ppermute | solution.py:22
  229.5 5.2 %collective-permute-start.16 = (f32[1,64,256]{2,1,0:T(8,128)S(1)}, f32[1,64,256]{2,1,0:T(8,128)S(1)}, u32[]{:S(2)}, u32[]{:S(2)}) collective-permute-start(f32[1,64,256]{2,1,0:T(8,128)S(1)} %get-tuple-element.27), channel_id=1, source_target_pairs={{0,2},{2,4},{4,6},{6,8},{8,10},{10,12},{12,14},{14,16},{16,18},{18... | collective-permute-start | bytes 196616 | tf_op jit(solution)/shard_map/ppermute | solution.py:19
  232.8 6.8 %collective-permute-start.17 = (f32[1,64,256]{2,1,0:T(8,128)S(1)}, f32[1,64,256]{2,1,0:T(8,128)S(1)}, u32[]{:S(2)}, u32[]{:S(2)}) collective-permute-start(f32[1,64,256]{2,1,0:T(8,128)S(1)} %get-tuple-element.28), channel_id=1, source_target_pairs={{2,0},{4,2},{6,4},{8,6},{10,8},{12,10},{14,12},{16,14},{18,16},{20... | collective-permute-start | bytes 196616 | tf_op jit(solution)/shard_map/ppermute | solution.py:22
  239.6 2.7 %collective-permute-start.18 = (f32[10,1,256]{2,1,0:T(1,128)S(1)}, f32[10,1,256]{2,1,0:T(1,128)S(1)}, u32[]{:S(2)}, u32[]{:S(2)}) collective-permute-start(f32[10,1,256]{2,1,0:T(1,128)S(1)} %get-tuple-element.21), channel_id=1, source_target_pairs={{0,1},{2,3},{4,5},{6,7},{8,9},{10,11},{12,13},{14,15},{16,17},{18,... | collective-permute-start | bytes 30728 | tf_op jit(solution)/shard_map/ppermute | solution.py:19
  241.0 5.9 %collective-permute-start.19 = (f32[10,1,256]{2,1,0:T(1,128)S(1)}, f32[10,1,256]{2,1,0:T(1,128)S(1)}, u32[]{:S(2)}, u32[]{:S(2)}) collective-permute-start(f32[10,1,256]{2,1,0:T(1,128)S(1)} %get-tuple-element.22), channel_id=1, source_target_pairs={{1,0},{3,2},{5,4},{7,6},{9,8},{11,10},{13,12},{15,14},{17,16},{19,... | collective-permute-start | bytes 30728 | tf_op jit(solution)/shard_map/ppermute | solution.py:22
Sparse Core Ops, SparseCore 0:
  94.0 85.4 all-reduce.6
where the time goes:
time: 258 us; the launch traced here: 257 us
  waiting for transfers between devices  131 us (51%)
  starting transfers between devices  57.1 us (22%)
  other arithmetic  50.9 us (20%)
  between operations  13.9 us (5%)
  local copies, waits for them, and re-layouts  3.19 us (1%)
    psum x1, waiting for transfers between devices, body(): total = lax.psum(back, 'view')  85.5 us
    ppermute x10, waiting for transfers between devices, padded_2(): lax.ppermute(lax.slice_in_dim(block, 0, width, axis=dim), axis, backward)  44 us
    ppermute x10, starting transfers between devices, padded_2(): lax.ppermute(lax.slice_in_dim(block, block.shape[dim] - width, None, axis...  40.2 us
    add x5, other arithmetic, blur_valid(): total + weights[axis_num, offset + width] * lax.slice_in_dim(block, width...  32.4 us
    ppermute x10, starting transfers between devices, padded_2(): lax.ppermute(lax.slice_in_dim(block, 0, width, axis=dim), axis, backward)  16.9 us
    div x1, other arithmetic, body(): ratio = data[0] / blurred  6.7 us
  transfers between devices with their start and end apart: 21, of which 12 were waited for; matrix products, arithmetic and copies ran while one was open for 2% of the time, Pallas kernels for 0%

commit v1 on v0

v1 whole, which is shorter than its diff:
```python
import functools

import jax
import jax.numpy as jnp
from jax import lax
from jax.experimental import pallas as pl
from jax.experimental.pallas import tpu as pltpu
from jax.sharding import PartitionSpec as P

PASSES = 3
TAU = 0.05
EPS2 = 0.25
WIDTH = 4
EST_STRIP = 16
DATA_STRIP = 8
TV_HALO = 3
VMEM = pl.BlockSpec(memory_space=pltpu.VMEM)
SMEM = pl.BlockSpec(memory_space=pltpu.SMEM)
F32 = jnp.float32
BF16 = jnp.bfloat16


def split(x):
    high = x.astype(BF16)
    return high, (x - high.astype(F32)).astype(BF16)


def dot3(a_high, a_low, b_high, b_low):
    dot = functools.partial(jnp.dot, preferred_element_type=F32)
    return dot(a_high, b_high) + (dot(a_low, b_high) + dot(a_high, b_low))


def weights_kernel(rows, place, band, perm, prof, taps_z, wx_h, wx_l, wy1_h, wy1_l, wy2_h, wy2_l):
    row = place[2]
    pitch = wy1_h.shape[0] // 3
    halo1, halo2 = pitch - rows, pitch - rows - DATA_STRIP

    def taps(axis, shape):
        k = perm[axis]
        reach = band[k]
        parts = [jnp.where(t <= reach, prof[k * (WIDTH + 1) + t], 0.0) for t in range(WIDTH + 1)]
        total = parts[0]
        for part in parts[1:]:
            total = total + 2.0 * part
        return [jnp.full(shape, part, F32) / jnp.full(shape, total, F32) for part in parts]

    def banded(axis, shape, distance, keep, high, low):
        small = (8, shape[1])
        for start in range(0, shape[0], 16):
            pieces = []
            for t, tap in enumerate(taps(axis, small)):
                pieces.append(jnp.concatenate([tap, tap], axis=0))
            i = start + lax.broadcasted_iota(jnp.int32, (16, shape[1]), 0)
            j = lax.broadcasted_iota(jnp.int32, (16, shape[1]), 1)
            d = jnp.abs(distance(i, j))
            value = jnp.zeros((16, shape[1]), F32)
            for t in range(WIDTH + 1):
                value = jnp.where((d == t) & keep(i, j), pieces[t], value)
            high[start : start + 16, :], low[start : start + 16, :] = split(value)

    for t, tap in enumerate(taps(0, taps_z.shape[1:])):
        taps_z[t] = tap
    banded(2, wx_h.shape, lambda i, j: i - j, lambda i, j: (i >= 0), wx_h, wx_l)

    def plane_of(i):
        return (i >= pitch).astype(jnp.int32) + (i >= 2 * pitch).astype(jnp.int32)

    def halo_place(i, strip):
        i = i - pitch * plane_of(i)
        return jnp.where((i >= rows) & (row == 1), i - rows - strip, i)

    def ascending(i):
        return i - pitch * plane_of(i) - DATA_STRIP * row

    def same(i, j):
        return plane_of(i) == plane_of(j)

    def used(i):
        return i - pitch * plane_of(i) < rows + DATA_STRIP

    banded(
        1,
        wy1_h.shape,
        lambda i, j: halo_place(i, DATA_STRIP) - halo_place(j, EST_STRIP),
        lambda i, j: same(i, j) & used(i),
        wy1_h,
        wy1_l,
    )
    banded(
        1,
        wy2_h.shape,
        lambda i, j: ascending(i) - halo_place(j, DATA_STRIP),
        lambda i, j: same(i, j) & used(i) & used(j),
        wy2_h,
        wy2_l,
    )


def blur_z(read, taps_z, lanes):
    total = taps_z[0] * read(WIDTH)
    for t in range(1, WIDTH + 1):
        total = total + taps_z[t] * (read(WIDTH - t) + read(WIDTH + t))
    return total


def views_kernel(
    slabs, place, est, data, strip, below, above, strip_below, strip_above,
    taps_z, wx_h, wx_l, wy1_h, wy1_l, wy2_h, wy2_l, out, flat1, ratio, flat2,
):
    planes, rows, lanes = est.shape
    slab = place[1]
    pitch = rows + EST_STRIP
    used = rows + DATA_STRIP
    wide = planes + 2 * WIDTH

    def est_plane(q, first, count):
        if q < planes:
            return below[q, first : first + count, :]
        if q < 2 * planes:
            return est[q - planes, first : first + count, :]
        return above[q - 2 * planes, first : first + count, :]

    def est_strip(q):
        ref = (strip_below, strip, strip_above)[q // planes]
        return ref[q % planes, 0:EST_STRIP, :]

    for p in range(wide):
        for first in range(0, rows, 16):
            flat1[p * pitch + first : p * pitch + first + 16, :] = blur_z(
                lambda t: est_plane(p + t, first, 16), taps_z, lanes
            )
        flat1[p * pitch + rows : (p + 1) * pitch, :] = blur_z(
            lambda t: est_strip(p + t), taps_z, lanes
        )

    def blur_yx(flat, start, count, w_h, w_l):
        n = count * pitch
        x_h, x_l = split(flat[start * pitch : start * pitch + n, :])
        mid = dot3(w_h[0:n, 0:n], w_l[0:n, 0:n], x_h, x_l)
        m_h, m_l = split(mid)
        return dot3(m_h, m_l, wx_h[...], wx_l[...])

    for start in range(0, wide, 3):
        count = min(3, wide - start)
        blurred = blur_yx(flat1, start, count, wy1_h, wy1_l)
        for p in range(start, start + count):
            own = blurred[(p - start) * pitch : (p - start) * pitch + rows, :]
            rim = blurred[(p - start) * pitch + rows : (p - start) * pitch + used, :]
            strip_rows = slice(EST_STRIP, EST_STRIP + DATA_STRIP)
            if p < WIDTH:
                top, low = below[planes + p], strip_below[planes - WIDTH + p, strip_rows, :]
                inside = slab > 0
            elif p < WIDTH + planes:
                top, low = data[p - WIDTH], strip[p - WIDTH, strip_rows, :]
                inside = None
            else:
                q = p - WIDTH - planes
                top, low = above[planes + q], strip_above[q, strip_rows, :]
                inside = slab < slabs - 1
            top, low = top / own, low / rim
            if inside is not None:
                top, low = jnp.where(inside, top, 0.0), jnp.where(inside, low, 0.0)
            ratio[p, 0:rows, :] = top
            ratio[p, rows:used, :] = low

    for p in range(planes):
        for first in range(0, used, 8):
            flat2[p * pitch + first : p * pitch + first + 8, :] = blur_z(
                lambda t: ratio[p + t, first : first + 8, :], [taps_z[t, 0:8, :] for t in range(5)], lanes
            )
        flat2[p * pitch + used : (p + 1) * pitch, :] = jnp.zeros((pitch - used, lanes), F32)
    for start in range(0, planes, 3):
        count = min(3, planes - start)
        back = blur_yx(flat2, start, count, wy2_h, wy2_l)
        for p in range(start, start + count):
            out[p] = back[(p - start) * pitch : (p - start) * pitch + used, :]


def field_kernel(views, rows, place, parts, est, strip, out):
    view, row = place[0], place[2]
    total = parts[0]
    for v in range(1, views):
        total = total + parts[v]
    total = total * (1.0 / views)
    own, rim = est[view], strip[view, 0:EST_STRIP, :]

    @pl.when(row == 0)
    def _():
        value = jnp.concatenate([own * total[0:rows], rim[0:DATA_STRIP] * total[rows:]], axis=0)
        for v in range(views):
            out[v] = value

    @pl.when(row == 1)
    def _():
        value = jnp.concatenate(
            [rim[DATA_STRIP:] * total[0:DATA_STRIP], own * total[DATA_STRIP:]], axis=0
        )
        for v in range(views):
            out[v] = value


def variation_kernel(slabs, rows, place, field, below, above, out, first, second):
    planes, used, lanes = field.shape
    slab, row = place[1], place[2]
    lane = lax.broadcasted_iota(jnp.int32, (used, lanes), 1)
    line = lax.broadcasted_iota(jnp.int32, (used, lanes), 0)

    def up(x, axis, index, last):
        return jnp.where(index == last, 0.0, pltpu.roll(x, x.shape[axis] - 1, axis))

    def down(x, axis, index):
        return jnp.where(index == 0, 0.0, pltpu.roll(x, 1, axis))

    def one_pass(read, low, high, write):
        before = None
        current = read(low - 1)
        for z in range(low - 1, high):
            after = read(z + 1)
            g_z = after - current
            g_y = up(current, 0, line, used - 1) - current
            g_x = up(current, 1, lane, lanes - 1) - current
            scale = lax.rsqrt(g_z * g_z + g_y * g_y + g_x * g_x + EPS2)
            if z < 0:
                scale = jnp.where(slab > 0, scale, 0.0)
            f_z = g_z * scale
            if z >= low:
                f_y, f_x = g_y * scale, g_x * scale
                spread = f_z - before + f_y - down(f_y, 0, line) + f_x - down(f_x, 1, lane)
                value = current + TAU * spread
                if z < 0:
                    value = jnp.where(slab > 0, value, 0.0)
                if z >= planes:
                    value = jnp.where(slab < slabs - 1, value, 0.0)
                write(z, value)
            before, current = f_z, after

    def read_field(z):
        if z < 0:
            return below[z + TV_HALO]
        if z >= planes:
            return above[z - planes]
        return field[z]

    def into(ref):
        def write(z, value):
            ref[z + TV_HALO] = value

        return write

    def last(z, value):
        @pl.when(row == 0)
        def _():
            out[z] = value[0:rows]

        @pl.when(row == 1)
        def _():
            out[z] = value[used - rows :]

    one_pass(read_field, -2, planes + 2, into(first))
    one_pass(lambda z: first[z + TV_HALO], -1, planes + 1, into(second))
    one_pass(lambda z: second[z + TV_HALO], 0, planes, last)


def call(kernel, shapes, scratch, *args):
    specs = [SMEM if jnp.ndim(a) == 1 else VMEM for a in args]
    return pl.pallas_call(
        kernel,
        out_shape=shapes,
        in_specs=specs,
        out_specs=jax.tree.map(lambda _: VMEM, shapes),
        scratch_shapes=scratch,
        compiler_params=pltpu.CompilerParams(vmem_limit_bytes=40 * 2**20),
    )(*args)


def body(data, estimate, profile, band, axes_perm):
    data = data[0]
    planes, rows, lanes = estimate.shape
    views, slabs = lax.axis_size("view"), lax.axis_size("slab")
    view, slab, row = lax.axis_index("view"), lax.axis_index("slab"), lax.axis_index("row")
    place = jnp.stack([view, slab, row]).astype(jnp.int32)
    shape = functools.partial(jax.ShapeDtypeStruct, dtype=F32)
    half = functools.partial(jax.ShapeDtypeStruct, dtype=BF16)
    up = [(i, i + 1) for i in range(slabs - 1)]
    down = [(i + 1, i) for i in range(slabs - 1)]

    start_e = jnp.where(row == 0, rows - EST_STRIP, 0)
    start_d = jnp.where(row == 0, rows - DATA_STRIP, 0)
    edge = jnp.concatenate(
        [
            lax.dynamic_slice_in_dim(estimate, start_e, EST_STRIP, 1),
            lax.dynamic_slice_in_dim(data, start_d, DATA_STRIP, 1),
        ],
        axis=1,
    )
    strip = lax.ppermute(edge, "row", [(0, 1), (1, 0)])
    below = lax.ppermute(jnp.concatenate([estimate, data[planes - WIDTH :]], axis=0), "slab", up)
    above = lax.ppermute(jnp.concatenate([estimate, data[:WIDTH]], axis=0), "slab", down)
    strip_below = lax.ppermute(strip, "slab", up)
    strip_above = lax.ppermute(strip, "slab", down)

    pitch, used = rows + EST_STRIP, rows + DATA_STRIP
    matrices = call(
        functools.partial(weights_kernel, rows),
        [shape((WIDTH + 1, 16, lanes))]
        + [half((lanes, lanes))] * 2
        + [half((3 * pitch, 3 * pitch))] * 4,
        [],
        place, band[0], axes_perm[0], profile.reshape(-1),
    )
    back = call(
        functools.partial(views_kernel, slabs),
        shape((planes, used, lanes)),
        [
            pltpu.VMEM(((planes + 2 * WIDTH) * pitch, lanes), F32),
            pltpu.VMEM((planes + 2 * WIDTH, used, lanes), F32),
            pltpu.VMEM((planes * pitch, lanes), F32),
        ],
        place, estimate, data, strip, below, above, strip_below, strip_above, *matrices,
    )
    parts = lax.all_to_all(back, "view", 0, 0, tiled=True)
    copies = call(
        functools.partial(field_kernel, views, rows),
        shape((views, used, lanes)),
        [],
        place, parts, estimate, strip,
    )
    field = lax.all_to_all(copies, "view", 0, 0, tiled=True)
    field_below = lax.ppermute(field[planes - TV_HALO :], "slab", up)
    field_above = lax.ppermute(field[:TV_HALO], "slab", down)
    deep = pltpu.VMEM((planes + 2 * TV_HALO, used, lanes), F32)
    return call(
        functools.partial(variation_kernel, slabs, rows),
        shape((planes, rows, lanes)),
        [deep, deep],
        place, field, field_below, field_above,
    )


def solution(mesh):
    placed = (
        P("view", "slab", "row", None),
        P("slab", "row", None),
        P("view", None, None),
        P("view", None),
        P("view", None),
    )
    return jax.shard_map(
        body, mesh=mesh, in_specs=placed, out_specs=P("slab", "row", None), check_vma=False
    )
```

time: 258 us -> 82.7 us (0.32)
  waiting for transfers between devices: 131 us -> 15.1 us
  other arithmetic: 50.9 us -> 1.45 us
  starting transfers between devices: 57.1 us -> 28.3 us
  blocking collectives: 0 us -> 24.6 us
  between operations: 13.9 us -> 0.16 us
  Pallas kernels: 0 us -> 9.96 us
    psum x1 -> x0, waiting for transfers between devices: 85.5 us -> none  [body(): total = lax.psum(back, 'view')]
    add x5 -> x0, other arithmetic: 32.4 us -> none  [blur_valid(): total + weights[axis_num, offset + width] * lax.slice_in_dim(block, width...]
    ppermute x20 -> x7, waiting for transfers between devices: 45.5 us -> 15.1 us  [the longest x1 5.61 us: body(): field_above = lax.ppermute(field[:TV_HALO], 'slab', down)]
    ppermute x20 -> x7, starting transfers between devices: 57.1 us -> 28.3 us  [the longest x1 7.92 us: body(): field_below = lax.ppermute(field[planes - TV_HALO:], 'slab', up)]
    all_to_all x0 -> x2, blocking collectives: none -> 24.6 us  [the longest x1 12.9 us: body(): parts = lax.all_to_all(back, 'view', 0, 0, tiled=True)]
    pallas_call x0 -> x4, Pallas kernels: none -> 9.96 us  [call(): pl.pallas_call(kernel, out_shape=shapes, in_specs=specs, out_specs=jax.tr...]
    mul x10 -> x0, other arithmetic: 7.71 us -> none  [the longest x3 3.75 us: tv_step(): return (padded[1:-1, 1:-1, 1:-1] + TAU * spread) * mask[1:-1, 1:-1, 1:-1]]
    div x2 -> x0, other arithmetic: 6.77 us -> none  [the longest x1 6.7 us: body(): ratio = data[0] / blurred]
  transfers between devices with their start and end apart: 21 -> 7, of which waited for: 12 -> 4; matrix products, arithmetic and copies ran while one was open for 2% -> 0% of each run, Pallas kernels for 0% -> 1%
where the time goes in v1:
time: 82.7 us; the launch traced here: 82.3 us
  starting transfers between devices  28.3 us (34%)
  blocking collectives  24.6 us (30%)
  waiting for transfers between devices  15.1 us (18%)
  Pallas kernels  9.96 us (12%)
  local copies, waits for them, and re-layouts  2.69 us (3%)
  other arithmetic  1.45 us (2%)
    all_to_all x1, blocking collectives, body(): parts = lax.all_to_all(back, 'view', 0, 0, tiled=True)  12.9 us
    all_to_all x1, blocking collectives, body(): field = lax.all_to_all(copies, 'view', 0, 0, tiled=True)  11.7 us
    pallas_call x4, Pallas kernels, call(): pl.pallas_call(kernel, out_shape=shapes, in_specs=specs, out_specs=jax.tr...  9.96 us
    ppermute x1, starting transfers between devices, body(): field_below = lax.ppermute(field[planes - TV_HALO:], 'slab', up)  7.92 us
    ppermute x1, waiting for transfers between devices, body(): field_above = lax.ppermute(field[:TV_HALO], 'slab', down)  5.61 us
    ppermute x1, starting transfers between devices, body(): lax.ppermute(jnp.concatenate([estimate, data[planes - WIDTH:]], axis=0),...  5.3 us
    ppermute x1, waiting for transfers between devices, body(): strip = lax.ppermute(edge, 'row', [(0, 1), (1, 0)])  4.83 us
    ppermute x1, starting transfers between devices, body(): strip = lax.ppermute(edge, 'row', [(0, 1), (1, 0)])  4.65 us
  transfers between devices with their start and end apart: 7, of which 4 were waited for; matrix products, arithmetic and copies ran while one was open for 0% of the time, Pallas kernels for 1%

profile of v1, /device:TPU:97, one launch (start us, length us, event | category | flops | bytes accessed | tf_op | source)
XLA Modules:
  0.0 82.3 jit_solution(16028732100616559869)
XLA Ops:
  0.0 1.1 %slice_bitcast_fusion = (f32[4,64,256]{2,1,0:T(8,128)S(1)}, f32[4,64,256]{2,1,0:T(8,128)S(1)}) fusion(f32[1,8,64,256]{3,2,1,0:T(8,128)} %param.5), kind=kLoop, calls=%fused_computation.2 | loop fusion | bytes 1048576 | tf_op jit(solution)/shard_map/slice | solution.py:298
  1.1 0.1 copy-done
  1.2 1.3 %pad_maximum_fusion = (f32[12,64,256]{2,1,0:T(8,128)}, f32[12,64,256]{2,1,0:T(8,128)}) fusion(f32[8,64,256]{2,1,0:T(8,128)S(1)} %copy-done, f32[4,64,256]{2,1,0:T(8,128)S(1)} %get-tuple-element.23, f32[4,64,256]{2,1,0:T(8,128)S(1)} %get-tuple-element.24), kind=kLoop, calls=%fused_computation | loop fusion | flops 393216 | bytes 2621440 | tf_op jit(solution)/shard_map/concatenate | solution.py:298
  2.5 5.3 %collective-permute-start.1 = (f32[12,64,256]{2,1,0:T(8,128)}, f32[12,64,256]{2,1,0:T(8,128)S(1)}, u32[]{:S(2)}, u32[]{:S(2)}) collective-permute-start(f32[12,64,256]{2,1,0:T(8,128)} %get-tuple-element.22), channel_id=1, source_target_pairs={{0,2},{2,4},{4,6},{6,8},{8,10},{10,12},{12,14},{14,16},{16,18},{18... | collective-permute-start | bytes 2359304 | tf_op jit(solution)/shard_map/ppermute | solution.py:297
  7.9 1.9 %collective-permute-start.2 = (f32[12,64,256]{2,1,0:T(8,128)}, f32[12,64,256]{2,1,0:T(8,128)S(1)}, u32[]{:S(2)}, u32[]{:S(2)}) collective-permute-start(f32[12,64,256]{2,1,0:T(8,128)} %get-tuple-element.21), channel_id=1, source_target_pairs={{2,0},{4,2},{6,4},{8,6},{10,8},{12,10},{14,12},{16,14},{18,16},{20... | collective-permute-start | bytes 2359304 | tf_op jit(solution)/shard_map/ppermute | solution.py:298
  9.9 4.7 %collective-permute-start = (f32[8,24,256]{2,1,0:T(8,128)S(1)}, f32[8,24,256]{2,1,0:T(8,128)S(1)}, u32[]{:S(2)}, u32[]{:S(2)}) collective-permute-start(f32[8,24,256]{2,1,0:T(8,128)S(1)} %pad_maximum_fusion.2), channel_id=1, source_target_pairs={{0,1},{1,0},{2,3},{3,2},{4,5},{5,4},{6,7},{7,6},{8,9},{9,8},{10,11... | collective-permute-start | bytes 589832 | tf_op jit(solution)/shard_map/ppermute | solution.py:296
  14.5 4.8 %collective-permute-done.strip = f32[8,24,256]{2,1,0:T(8,128)S(1)} collective-permute-done((f32[8,24,256]{2,1,0:T(8,128)S(1)}, f32[8,24,256]{2,1,0:T(8,128)S(1)}, u32[]{:S(2)}, u32[]{:S(2)}) %collective-permute-start) | collective-permute-done | bytes 196640 | tf_op jit(solution)/shard_map/ppermute | solution.py:296
  19.4 4.6 %collective-permute-start.3 = (f32[8,24,256]{2,1,0:T(8,128)S(1)}, f32[8,24,256]{2,1,0:T(8,128)S(1)}, u32[]{:S(2)}, u32[]{:S(2)}) collective-permute-start(f32[8,24,256]{2,1,0:T(8,128)S(1)} %collective-permute-done.strip), channel_id=1, source_target_pairs={{0,2},{2,4},{4,6},{6,8},{8,10},{10,12},{12,14},{14,16},{16,18},{18... | collective-permute-start | bytes 589832 | tf_op jit(solution)/shard_map/ppermute | solution.py:299
  24.0 1.9 %collective-permute-start.4 = (f32[8,24,256]{2,1,0:T(8,128)S(1)}, f32[8,24,256]{2,1,0:T(8,128)S(1)}, u32[]{:S(2)}, u32[]{:S(2)}) collective-permute-start(f32[8,24,256]{2,1,0:T(8,128)S(1)} %collective-permute-done.strip), channel_id=1, source_target_pairs={{2,0},{4,2},{6,4},{8,6},{10,8},{12,10},{14,12},{16,14},{18,16},{20... | collective-permute-start | bytes 589832 | tf_op jit(solution)/shard_map/ppermute | solution.py:300
  26.0 0.7 copy-done.4
  26.7 0.1 reshape.6.prof
  26.7 0.1 pad_add_fusion.place
  26.8 0.7 copy-done.2
  27.5 1.0 %shard_map.55 = (f32[5,16,256]{2,1,0:T(8,128)S(1)}, bf16[256,256]{1,0:T(8,128)(2,1)S(1)}, bf16[256,256]{1,0:T(8,128)(2,1)S(1)}, bf16[240,240]{1,0:T(8,128)(2,1)S...) custom-call(s32[3]{0:T(128)S(1)} %pad_add_fusion.place, ...), custom_call_target="tpu_custom_call" | custom-call | tf_op jit(solution)/shard_map/pallas_call | solution.py:266
  28.5 3.7 %collective-permute-done.4.strip_above = f32[8,24,256]{2,1,0:T(8,128)S(1)} collective-permute-done((f32[8,24,256]{2,1,0:T(8,128)S(1)}, f32[8,24,256]{2,1,0:T(8,128)S(1)}, u32[]{:S(2)}, u32[]{:S(2)}) %collective-permute-start.4) | collective-permute-done | bytes 196640 | tf_op jit(solution)/shard_map/ppermute | solution.py:300
  32.2 3.1 %shard_map.56 = f32[8,72,256]{2,1,0:T(8,128)S(1)} custom-call(s32[3]{0:T(128)S(1)} %pad_add_fusion.place, f32[8,64,256]{2,1,0:T(8,128)S(1)} %copy-done, f32[8,64,256]{2,1,0:T(8,128)S(1)} %bitcast.12, f32[8,24,256]{2,1,0:T(8,128)S(1)} %collective-permute-done.strip, f32[12,64,256]{2,1,0:T(8,128)S(1)} %collective-permute-done.1.below, ...), custom_call_target="tpu_custom_call" | custom-call | tf_op jit(solution)/shard_map/pallas_call | solution.py:266
  35.3 12.9 %all_to_all.10.parts = f32[8,72,256]{2,1,0:T(8,128)S(1)} all-to-all(f32[8,72,256]{2,1,0:T(8,128)S(1)} %shard_map.56), channel_id=1, replica_groups=mesh['view'=8,'slab'=32,'row'=2] {'view'}, dimensions={0} | all-to-all | bytes 1179648 | tf_op jit(solution)/shard_map/all_to_all | solution.py:321
  48.3 0.6 shard_map.57
  48.9 11.7 %all_to_all.11.field = f32[8,72,256]{2,1,0:T(8,128)S(1)} all-to-all(f32[8,72,256]{2,1,0:T(8,128)S(1)} %shard_map.57), channel_id=1, replica_groups=mesh['view'=8,'slab'=32,'row'=2] {'view'}, dimensions={0} | all-to-all | bytes 1179648 | tf_op jit(solution)/shard_map/all_to_all | solution.py:328
  60.6 7.9 %collective-permute-start.5 = (f32[3,72,256]{2,1,0:T(8,128)S(1)}, f32[3,72,256]{2,1,0:T(8,128)S(1)}, u32[]{:S(2)}, u32[]{:S(2)}) collective-permute-start(f32[3,72,256]{2,1,0:T(8,128)S(1)} %get-tuple-element.20), channel_id=1, source_target_pairs={{0,2},{2,4},{4,6},{6,8},{8,10},{10,12},{12,14},{14,16},{16,18},{18... | collective-permute-start | bytes 663560 | tf_op jit(solution)/shard_map/ppermute | solution.py:329
  68.6 1.9 %collective-permute-start.6 = (f32[3,72,256]{2,1,0:T(8,128)S(1)}, f32[3,72,256]{2,1,0:T(8,128)S(1)}, u32[]{:S(2)}, u32[]{:S(2)}) collective-permute-start(f32[3,72,256]{2,1,0:T(8,128)S(1)} %get-tuple-element.19), channel_id=1, source_target_pairs={{2,0},{4,2},{6,4},{8,6},{10,8},{12,10},{14,12},{16,14},{18,16},{20... | collective-permute-start | bytes 663560 | tf_op jit(solution)/shard_map/ppermute | solution.py:330
  70.5 0.9 %collective-permute-done.5.below = f32[3,72,256]{2,1,0:T(8,128)S(1)} collective-permute-done((f32[3,72,256]{2,1,0:T(8,128)S(1)}, f32[3,72,256]{2,1,0:T(8,128)S(1)}, u32[]{:S(2)}, u32[]{:S(2)}) %collective-permute-start.5) | collective-permute-done | bytes 221216 | tf_op jit(solution)/shard_map/ppermute | solution.py:329
  71.4 5.6 %collective-permute-done.6.above = f32[3,72,256]{2,1,0:T(8,128)S(1)} collective-permute-done((f32[3,72,256]{2,1,0:T(8,128)S(1)}, f32[3,72,256]{2,1,0:T(8,128)S(1)}, u32[]{:S(2)}, u32[]{:S(2)}) %collective-permute-start.6) | collective-permute-done | bytes 221216 | tf_op jit(solution)/shard_map/ppermute | solution.py:330
  77.0 5.2 %shard_map.58 = f32[8,64,256]{2,1,0:T(8,128)} custom-call(s32[3]{0:T(128)S(1)} %pad_add_fusion.place, f32[8,72,256]{2,1,0:T(8,128)S(1)} %all_to_all.11.field, f32[3,72,256]{2,1,0:T(8,128)S(1)} %collective-permute-done.5.below, f32[3,72,256]{2,1,0:T(8,128)S(1)} %collective-permute-done.6.above), custom_call_target="tpu_custom_call" | custom-call | tf_op jit(solution)/shard_map/pallas_call | solution.py:266
  (15 shorter events, 0.1 us)
Async XLA Ops:
  0.0 1.2 %copy-start = (f32[8,64,256]{2,1,0:T(8,128)S(1)}, f32[8,64,256]{2,1,0:T(8,128)}, u32[]{:S(2)}) copy-start(f32[8,64,256]{2,1,0:T(8,128)} %est.3) | copy-start | bytes 1572868
  1.2 8.6 %copy-start.1 = (f32[1,8,64,256]{3,2,1,0:T(8,128)S(1)}, f32[1,8,64,256]{3,2,1,0:T(8,128)}, u32[]{:S(2)}) copy-start(f32[1,8,64,256]{3,2,1,0:T(8,128)} %param.5) | copy-start | bytes 1572868
  2.5 29.7 %collective-permute-start.1 = (f32[12,64,256]{2,1,0:T(8,128)}, f32[12,64,256]{2,1,0:T(8,128)S(1)}, u32[]{:S(2)}, u32[]{:S(2)}) collective-permute-start(f32[12,64,256]{2,1,0:T(8,128)} %get-tuple-element.22), channel_id=1, source_target_pairs={{0,2},{2,4},{4,6},{6,8},{8,10},{10,12},{12,14},{14,16},{16,18},{18... | collective-permute-start | bytes 2359304 | tf_op jit(solution)/shard_map/ppermute | solution.py:297
  7.9 24.4 %collective-permute-start.2 = (f32[12,64,256]{2,1,0:T(8,128)}, f32[12,64,256]{2,1,0:T(8,128)S(1)}, u32[]{:S(2)}, u32[]{:S(2)}) collective-permute-start(f32[12,64,256]{2,1,0:T(8,128)} %get-tuple-element.21), channel_id=1, source_target_pairs={{2,0},{4,2},{6,4},{8,6},{10,8},{12,10},{14,12},{16,14},{18,16},{20... | collective-permute-start | bytes 2359304 | tf_op jit(solution)/shard_map/ppermute | solution.py:298
  9.9 9.5 %collective-permute-start = (f32[8,24,256]{2,1,0:T(8,128)S(1)}, f32[8,24,256]{2,1,0:T(8,128)S(1)}, u32[]{:S(2)}, u32[]{:S(2)}) collective-permute-start(f32[8,24,256]{2,1,0:T(8,128)S(1)} %pad_maximum_fusion.2), channel_id=1, source_target_pairs={{0,1},{1,0},{2,3},{3,2},{4,5},{5,4},{6,7},{7,6},{8,9},{9,8},{10,11... | collective-permute-start | bytes 589832 | tf_op jit(solution)/shard_map/ppermute | solution.py:296
  19.4 9.2 %collective-permute-start.3 = (f32[8,24,256]{2,1,0:T(8,128)S(1)}, f32[8,24,256]{2,1,0:T(8,128)S(1)}, u32[]{:S(2)}, u32[]{:S(2)}) collective-permute-start(f32[8,24,256]{2,1,0:T(8,128)S(1)} %collective-permute-done.strip), channel_id=1, source_target_pairs={{0,2},{2,4},{4,6},{6,8},{8,10},{10,12},{12,14},{14,16},{16,18},{18... | collective-permute-start | bytes 589832 | tf_op jit(solution)/shard_map/ppermute | solution.py:299
  24.0 8.2 %collective-permute-start.4 = (f32[8,24,256]{2,1,0:T(8,128)S(1)}, f32[8,24,256]{2,1,0:T(8,128)S(1)}, u32[]{:S(2)}, u32[]{:S(2)}) collective-permute-start(f32[8,24,256]{2,1,0:T(8,128)S(1)} %collective-permute-done.strip), channel_id=1, source_target_pairs={{2,0},{4,2},{6,4},{8,6},{10,8},{12,10},{14,12},{16,14},{18,16},{20... | collective-permute-start | bytes 589832 | tf_op jit(solution)/shard_map/ppermute | solution.py:300
  26.0 0.7 copy-start.4
  26.8 0.7 copy-start.2
  26.8 0.7 copy-start.3
  60.6 10.8 %collective-permute-start.5 = (f32[3,72,256]{2,1,0:T(8,128)S(1)}, f32[3,72,256]{2,1,0:T(8,128)S(1)}, u32[]{:S(2)}, u32[]{:S(2)}) collective-permute-start(f32[3,72,256]{2,1,0:T(8,128)S(1)} %get-tuple-element.20), channel_id=1, source_target_pairs={{0,2},{2,4},{4,6},{6,8},{8,10},{10,12},{12,14},{14,16},{16,18},{18... | collective-permute-start | bytes 663560 | tf_op jit(solution)/shard_map/ppermute | solution.py:329
  68.6 8.5 %collective-permute-start.6 = (f32[3,72,256]{2,1,0:T(8,128)S(1)}, f32[3,72,256]{2,1,0:T(8,128)S(1)}, u32[]{:S(2)}, u32[]{:S(2)}) collective-permute-start(f32[3,72,256]{2,1,0:T(8,128)S(1)} %get-tuple-element.19), channel_id=1, source_target_pairs={{2,0},{4,2},{6,4},{8,6},{10,8},{12,10},{14,12},{16,14},{18,16},{20... | collective-permute-start | bytes 663560 | tf_op jit(solution)/shard_map/ppermute | solution.py:330

commit v2 on v1

--- a/solution.py
+++ b/solution.py
@@ -14,6 +14,7 @@
 EST_STRIP = 16
 DATA_STRIP = 8
 TV_HALO = 3
+COST = 20000000000
 VMEM = pl.BlockSpec(memory_space=pltpu.VMEM)
 SMEM = pl.BlockSpec(memory_space=pltpu.SMEM)
 F32 = jnp.float32
@@ -96,7 +97,7 @@
     )
 
 
-def blur_z(read, taps_z, lanes):
+def blur_z(read, taps_z):
     total = taps_z[0] * read(WIDTH)
     for t in range(1, WIDTH + 1):
         total = total + taps_z[t] * (read(WIDTH - t) + read(WIDTH + t))
@@ -104,7 +105,7 @@
 
 
 def views_kernel(
-    slabs, place, est, data, strip, below, above, strip_below, strip_above,
+    slabs, place, est, data, strip, est_on, est_off, on, off,
     taps_z, wx_h, wx_l, wy1_h, wy1_l, wy2_h, wy2_l, out, flat1, ratio, flat2,
 ):
     planes, rows, lanes = est.shape
@@ -113,25 +114,36 @@
     used = rows + DATA_STRIP
     wide = planes + 2 * WIDTH
 
-    def est_plane(q, first, count):
-        if q < planes:
-            return below[q, first : first + count, :]
-        if q < 2 * planes:
-            return est[q - planes, first : first + count, :]
-        return above[q - 2 * planes, first : first + count, :]
-
-    def est_strip(q):
-        ref = (strip_below, strip, strip_above)[q // planes]
-        return ref[q % planes, 0:EST_STRIP, :]
-
-    for p in range(wide):
-        for first in range(0, rows, 16):
-            flat1[p * pitch + first : p * pitch + first + 16, :] = blur_z(
-                lambda t: est_plane(p + t, first, 16), taps_z, lanes
-            )
-        flat1[p * pitch + rows : (p + 1) * pitch, :] = blur_z(
-            lambda t: est_strip(p + t), taps_z, lanes
-        )
+    odd = lax.rem(slab, 2) == 1
+
+    thick = EST_STRIP + DATA_STRIP
+    base = planes * thick
+
+    def blur_first(below, above, strip_below, strip_above):
+        def est_plane(q, first):
+            ref = (below, est, above)[q // planes]
+            return ref[q % planes, first : first + 16, :]
+
+        def est_strip(q):
+            if q // planes == 1:
+                return strip[q - planes, 0:EST_STRIP, :]
+            at = q % planes * thick
+            return (strip_below, strip_above)[q // planes // 2][at : at + EST_STRIP, :]
+
+        for p in range(wide):
+            for first in range(0, rows, 16):
+                flat1[p * pitch + first : p * pitch + first + 16, :] = blur_z(
+                    lambda t: est_plane(p + t, first), taps_z
+                )
+            flat1[p * pitch + rows : (p + 1) * pitch, :] = blur_z(lambda t: est_strip(p + t), taps_z)
+
+    @pl.when(odd)
+    def _():
+        blur_first(est_on, est_off, on, off)
+
+    @pl.when(jnp.logical_not(odd))
+    def _():
+        blur_first(est_off, est_on, off, on)
 
     def blur_yx(flat, start, count, w_h, w_l):
         n = count * pitch
@@ -148,14 +160,21 @@
             rim = blurred[(p - start) * pitch + rows : (p - start) * pitch + used, :]
             strip_rows = slice(EST_STRIP, EST_STRIP + DATA_STRIP)
             if p < WIDTH:
-                top, low = below[planes + p], strip_below[planes - WIDTH + p, strip_rows, :]
+                top = slice(base + p * rows, base + (p + 1) * rows)
+                low = (planes - WIDTH + p) * thick + EST_STRIP
+                low = slice(low, low + DATA_STRIP)
+                top = jnp.where(odd, on[top, :], off[top, :])
+                low = jnp.where(odd, on[low, :], off[low, :])
                 inside = slab > 0
             elif p < WIDTH + planes:
                 top, low = data[p - WIDTH], strip[p - WIDTH, strip_rows, :]
                 inside = None
             else:
                 q = p - WIDTH - planes
-                top, low = above[planes + q], strip_above[q, strip_rows, :]
+                top = slice(base + q * rows, base + (q + 1) * rows)
+                low = slice(q * thick + EST_STRIP, (q + 1) * thick)
+                top = jnp.where(odd, off[top, :], on[top, :])
+                low = jnp.where(odd, off[low, :], on[low, :])
                 inside = slab < slabs - 1
             top, low = top / own, low / rim
             if inside is not None:
@@ -166,7 +185,7 @@
     for p in range(planes):
         for first in range(0, used, 8):
             flat2[p * pitch + first : p * pitch + first + 8, :] = blur_z(
-                lambda t: ratio[p + t, first : first + 8, :], [taps_z[t, 0:8, :] for t in range(5)], lanes
+                lambda t: ratio[p + t, first : first + 8, :], [taps_z[t, 0:8, :] for t in range(5)]
             )
         flat2[p * pitch + used : (p + 1) * pitch, :] = jnp.zeros((pitch - used, lanes), F32)
     for start in range(0, planes, 3):
@@ -199,11 +218,15 @@
             out[v] = value
 
 
-def variation_kernel(slabs, rows, place, field, below, above, out, first, second):
+def variation_kernel(slabs, rows, place, field, on, off, out, rims, first, second):
     planes, used, lanes = field.shape
     slab, row = place[1], place[2]
     lane = lax.broadcasted_iota(jnp.int32, (used, lanes), 1)
     line = lax.broadcasted_iota(jnp.int32, (used, lanes), 0)
+
+    odd = lax.rem(slab, 2)
+    rims[pl.ds(odd * TV_HALO, TV_HALO)] = off[...]
+    rims[pl.ds((1 - odd) * TV_HALO, TV_HALO)] = on[...]
 
     def up(x, axis, index, last):
         return jnp.where(index == last, 0.0, pltpu.roll(x, x.shape[axis] - 1, axis))
@@ -236,9 +259,9 @@
 
     def read_field(z):
         if z < 0:
-            return below[z + TV_HALO]
+            return rims[z + TV_HALO]
         if z >= planes:
-            return above[z - planes]
+            return rims[z - planes + TV_HALO]
         return field[z]
 
     def into(ref):
@@ -261,7 +284,7 @@
     one_pass(lambda z: second[z + TV_HALO], 0, planes, last)
 
 
-def call(kernel, shapes, scratch, *args):
+def call(kernel, shapes, scratch, *args, cost=None):
     specs = [SMEM if jnp.ndim(a) == 1 else VMEM for a in args]
     return pl.pallas_call(
         kernel,
@@ -269,7 +292,8 @@
         in_specs=specs,
         out_specs=jax.tree.map(lambda _: VMEM, shapes),
         scratch_shapes=scratch,
-        compiler_params=pltpu.CompilerParams(vmem_limit_bytes=40 * 2**20),
+        cost_estimate=cost,
+        compiler_params=pltpu.CompilerParams(vmem_limit_bytes=16 * 2**20),
     )(*args)
 
 
@@ -281,23 +305,30 @@
     place = jnp.stack([view, slab, row]).astype(jnp.int32)
     shape = functools.partial(jax.ShapeDtypeStruct, dtype=F32)
     half = functools.partial(jax.ShapeDtypeStruct, dtype=BF16)
-    up = [(i, i + 1) for i in range(slabs - 1)]
-    down = [(i + 1, i) for i in range(slabs - 1)]
-
-    start_e = jnp.where(row == 0, rows - EST_STRIP, 0)
-    start_d = jnp.where(row == 0, rows - DATA_STRIP, 0)
+    off_pairs = [(i, i + 1) for i in range(1, slabs - 1, 2)]
+    off_pairs += [(target, source) for source, target in off_pairs]
+    on_pairs = [(i, i ^ 1) for i in range(slabs)]
+    odd = lax.rem(slab, 2)
+
+    first_row, is_odd = row == 0, odd == 1
     edge = jnp.concatenate(
         [
-            lax.dynamic_slice_in_dim(estimate, start_e, EST_STRIP, 1),
-            lax.dynamic_slice_in_dim(data, start_d, DATA_STRIP, 1),
+            jnp.where(first_row, estimate[:, rows - EST_STRIP :], estimate[:, :EST_STRIP]),
+            jnp.where(first_row, data[:, rows - DATA_STRIP :], data[:, :DATA_STRIP]),
         ],
         axis=1,
     )
     strip = lax.ppermute(edge, "row", [(0, 1), (1, 0)])
-    below = lax.ppermute(jnp.concatenate([estimate, data[planes - WIDTH :]], axis=0), "slab", up)
-    above = lax.ppermute(jnp.concatenate([estimate, data[:WIDTH]], axis=0), "slab", down)
-    strip_below = lax.ppermute(strip, "slab", up)
-    strip_above = lax.ppermute(strip, "slab", down)
+    held = lax.optimization_barrier((estimate, edge))[0]
+    est_off = lax.ppermute(held, "slab", off_pairs)
+    est_on = lax.ppermute(held, "slab", on_pairs)
+    low = data[:WIDTH].reshape(-1, lanes)
+    high = data[planes - WIDTH :].reshape(-1, lanes)
+    flat = strip.reshape(-1, lanes)
+    off = jnp.concatenate([flat, jnp.where(is_odd, high, low)], axis=0)
+    on = jnp.concatenate([flat, jnp.where(is_odd, low, high)], axis=0)
+    off = lax.ppermute(off, "slab", off_pairs)
+    on = lax.ppermute(on, "slab", on_pairs)
 
     pitch, used = rows + EST_STRIP, rows + DATA_STRIP
     matrices = call(
@@ -307,6 +338,7 @@
         + [half((3 * pitch, 3 * pitch))] * 4,
         [],
         place, band[0], axes_perm[0], profile.reshape(-1),
+        cost=pl.CostEstimate(flops=COST, bytes_accessed=0, transcendentals=0),
     )
     back = call(
         functools.partial(views_kernel, slabs),
@@ -316,7 +348,7 @@
             pltpu.VMEM((planes + 2 * WIDTH, used, lanes), F32),
             pltpu.VMEM((planes * pitch, lanes), F32),
         ],
-        place, estimate, data, strip, below, above, strip_below, strip_above, *matrices,
+        place, estimate, data, strip, est_on, est_off, on, off, *matrices,
     )
     parts = lax.all_to_all(back, "view", 0, 0, tiled=True)
     copies = call(
@@ -326,14 +358,16 @@
         place, parts, estimate, strip,
     )
     field = lax.all_to_all(copies, "view", 0, 0, tiled=True)
-    field_below = lax.ppermute(field[planes - TV_HALO :], "slab", up)
-    field_above = lax.ppermute(field[:TV_HALO], "slab", down)
+    reach = planes - TV_HALO
+    low, high = field[:TV_HALO], field[reach:]
+    off = lax.ppermute(jnp.where(is_odd, high, low), "slab", off_pairs)
+    on = lax.ppermute(jnp.where(is_odd, low, high), "slab", on_pairs)
     deep = pltpu.VMEM((planes + 2 * TV_HALO, used, lanes), F32)
     return call(
         functools.partial(variation_kernel, slabs, rows),
         shape((planes, rows, lanes)),
-        [deep, deep],
-        place, field, field_below, field_above,
+        [pltpu.VMEM((2 * TV_HALO, used, lanes), F32), deep, deep],
+        place, field, on, off,
     )
 
 

time: 82.7 us -> 73.6 us (0.89)
  the two profiles are of different devices: /device:TPU:97 before, /device:TPU:193 now
where the time goes in v2:
time: 73.6 us; the launch traced here: 73.2 us
  blocking collectives  27.5 us (37%)
  starting transfers between devices  26.4 us (36%)
  Pallas kernels  10.2 us (14%)
  waiting for transfers between devices  4.18 us (6%)
  other arithmetic  3.21 us (4%)
  local copies, waits for them, and re-layouts  1.42 us (2%)
    all_to_all x1, blocking collectives, body(): parts = lax.all_to_all(back, 'view', 0, 0, tiled=True)  14.9 us
    all_to_all x1, blocking collectives, body(): field = lax.all_to_all(copies, 'view', 0, 0, tiled=True)  12.6 us
    pallas_call x4, Pallas kernels, call(): pl.pallas_call(kernel, out_shape=shapes, in_specs=specs, out_specs=jax.tr...  10.2 us
    ppermute x1, starting transfers between devices, body(): off = lax.ppermute(jnp.where(is_odd, high, low), 'slab', off_pairs)  6.48 us
    ppermute x1, starting transfers between devices, body(): off = lax.ppermute(off, 'slab', off_pairs)  5.14 us
    ppermute x1, starting transfers between devices, body(): strip = lax.ppermute(edge, 'row', [(0, 1), (1, 0)])  4.65 us
    ppermute x1, starting transfers between devices, body(): est_off = lax.ppermute(held, 'slab', off_pairs)  4.39 us
    ppermute x1, waiting for transfers between devices, body(): off = lax.ppermute(off, 'slab', off_pairs)  2.5 us
  transfers between devices with their start and end apart: 7, of which 2 were waited for; matrix products, arithmetic and copies ran while one was open for 2% of the time, Pallas kernels for 1%

profile of v2, /device:TPU:193, one launch (start us, length us, event | category | flops | bytes accessed | tf_op | source)
XLA Modules:
  0.0 73.2 jit_solution(10349544378282333665)
XLA Ops:
  0.0 0.9 %slice_select_fusion.5 = f32[8,8,256]{2,1,0:T(8,128)S(1)} fusion(f32[8,64,256]{2,1,0:T(8,128)} %bitcast.9, pred[]{:T(512)S(6)} %eq.6), kind=kLoop, calls=%fused_computation.8 | loop fusion | flops 16384 | bytes 196609 | tf_op jit(solution)/shard_map/jit(_where)/select_n | solution.py:317
  0.9 1.0 %slice_select_fusion.4 = f32[8,16,256]{2,1,0:T(8,128)S(1)} fusion(f32[8,64,256]{2,1,0:T(8,128)} %est.3, pred[]{:T(512)S(6)} %eq.6), kind=kLoop, calls=%fused_computation.7 | loop fusion | flops 32768 | bytes 393217 | tf_op jit(solution)/shard_map/jit(_where)/select_n | solution.py:316
  2.0 4.7 %collective-permute-start = (f32[8,24,256]{2,1,0:T(8,128)S(1)}, f32[8,24,256]{2,1,0:T(8,128)S(1)}, u32[]{:S(2)}, u32[]{:S(2)}) collective-permute-start(f32[8,24,256]{2,1,0:T(8,128)S(1)} %pad_maximum_fusion.2), channel_id=1, source_target_pairs={{0,1},{1,0},{2,3},{3,2},{4,5},{5,4},{6,7},{7,6},{8,9},{9,8},{10,11... | collective-permute-start | bytes 589832 | tf_op jit(solution)/shard_map/ppermute | solution.py:321
  6.6 4.4 %collective-permute-start.2 = (f32[8,64,256]{2,1,0:T(8,128)S(1)}, f32[8,64,256]{2,1,0:T(8,128)S(1)}, u32[]{:S(2)}, u32[]{:S(2)}) collective-permute-start(f32[8,64,256]{2,1,0:T(8,128)S(1)} %copy-done), channel_id=1, source_target_pairs={{2,4},{6,8},{10,12},{14,16},{18,20},{22,24},{26,28},{30,32},{34,36... | collective-permute-start | bytes 1572872 | tf_op jit(solution)/shard_map/ppermute | solution.py:323
  11.0 1.9 %collective-permute-start.1 = (f32[8,64,256]{2,1,0:T(8,128)S(1)}, f32[8,64,256]{2,1,0:T(8,128)S(1)}, u32[]{:S(2)}, u32[]{:S(2)}) collective-permute-start(f32[8,64,256]{2,1,0:T(8,128)S(1)} %copy-done), channel_id=1, source_target_pairs={{0,2},{2,0},{4,6},{6,4},{8,10},{10,8},{12,14},{14,12},{16,18},{18,... | collective-permute-start | bytes 1572872 | tf_op jit(solution)/shard_map/ppermute | solution.py:324
  13.0 0.7 copy-done.4
  13.7 0.1 reshape.17.prof
  13.8 0.1 pad_add_fusion.place
  13.8 1.1 %slice_select_fusion = (f32[1,4,64,256]{3,2,1,0:T(8,128)S(1)}, f32[1,4,64,256]{3,2,1,0:T(8,128)S(1)}) fusion(f32[1,8,64,256]{3,2,1,0:T(8,128)} %param.5, pred[]{:T(512)S(6)} %eq.7), kind=kLoop, calls=%fused_computation.2 | loop fusion | flops 131072 | bytes 1048577 | tf_op jit(solution)/shard_map/jit(_where)/select_n | solution.py:328
  14.9 0.1 pad_maximum_fusion
  15.0 5.1 %collective-permute-start.4 = (f32[448,256]{1,0:T(8,128)S(1)}, f32[448,256]{1,0:T(8,128)S(1)}, u32[]{:S(2)}, u32[]{:S(2)}) collective-permute-start(f32[448,256]{1,0:T(8,128)S(1)} %get-tuple-element.25), channel_id=1, source_target_pairs={{2,4},{6,8},{10,12},{14,16},{18,20},{22,24},{26,28},{30,32},{34,36... | collective-permute-start | bytes 1376264 | tf_op jit(solution)/shard_map/ppermute | solution.py:330
  20.1 1.9 %collective-permute-start.3 = (f32[448,256]{1,0:T(8,128)S(1)}, f32[448,256]{1,0:T(8,128)S(1)}, u32[]{:S(2)}, u32[]{:S(2)}) collective-permute-start(f32[448,256]{1,0:T(8,128)S(1)} %get-tuple-element.26), channel_id=1, source_target_pairs={{0,2},{2,0},{4,6},{6,4},{8,10},{10,8},{12,14},{14,12},{16,18},{18,... | collective-permute-start | bytes 1376264 | tf_op jit(solution)/shard_map/ppermute | solution.py:331
  22.1 0.6 copy-done.2
  22.7 0.0 copy-done.3
  22.7 1.0 %shard_map.55 = (f32[5,16,256]{2,1,0:T(8,128)S(1)}, bf16[256,256]{1,0:T(8,128)(2,1)S(1)}, bf16[256,256]{1,0:T(8,128)(2,1)S(1)}, bf16[240,240]{1,0:T(8,128)(2,1)S...) custom-call(s32[3]{0:T(128)S(1)} %pad_add_fusion.place, ...), custom_call_target="tpu_custom_call" | custom-call | flops 20000000000 | tf_op jit(solution)/shard_map/pallas_call | solution.py:289
  23.8 2.5 %collective-permute-done.4.off = f32[448,256]{1,0:T(8,128)S(1)} collective-permute-done((f32[448,256]{1,0:T(8,128)S(1)}, f32[448,256]{1,0:T(8,128)S(1)}, u32[]{:S(2)}, u32[]{:S(2)}) %collective-permute-start.4) | collective-permute-done | bytes 458784 | tf_op jit(solution)/shard_map/ppermute | solution.py:330
  26.3 3.3 %shard_map.56 = f32[8,72,256]{2,1,0:T(8,128)S(1)} custom-call(s32[3]{0:T(128)S(1)} %pad_add_fusion.place, f32[8,64,256]{2,1,0:T(8,128)S(1)} %copy-done, f32[8,64,256]{2,1,0:T(8,128)S(1)} %bitcast.10, f32[8,24,256]{2,1,0:T(8,128)S(1)} %collective-permute-done.strip, f32[8,64,256]{2,1,0:T(8,128)S(1)} %collective-permute-done.1.est_on, ...), custom_call_target="tpu_custom_call" | custom-call | tf_op jit(solution)/shard_map/pallas_call | solution.py:289
  29.6 14.9 %all_to_all.10.parts = f32[8,72,256]{2,1,0:T(8,128)S(1)} all-to-all(f32[8,72,256]{2,1,0:T(8,128)S(1)} %shard_map.56), channel_id=1, replica_groups=mesh['view'=8,'slab'=32,'row'=2] {'view'}, dimensions={0} | all-to-all | bytes 1179648 | tf_op jit(solution)/shard_map/all_to_all | solution.py:353
  44.6 0.6 shard_map.57
  45.2 12.6 %all_to_all.11.field = f32[8,72,256]{2,1,0:T(8,128)S(1)} all-to-all(f32[8,72,256]{2,1,0:T(8,128)S(1)} %shard_map.57), channel_id=1, replica_groups=mesh['view'=8,'slab'=32,'row'=2] {'view'}, dimensions={0} | all-to-all | bytes 1179648 | tf_op jit(solution)/shard_map/all_to_all | solution.py:360
  57.8 6.5 %collective-permute-start.6 = (f32[3,72,256]{2,1,0:T(8,128)S(1)}, f32[3,72,256]{2,1,0:T(8,128)S(1)}, u32[]{:S(2)}, u32[]{:S(2)}) collective-permute-start(f32[3,72,256]{2,1,0:T(8,128)S(1)} %get-tuple-element.21), channel_id=1, source_target_pairs={{2,4},{6,8},{10,12},{14,16},{18,20},{22,24},{26,28},{30,32},{34,36... | collective-permute-start | bytes 663560 | tf_op jit(solution)/shard_map/ppermute | solution.py:363
  64.3 1.9 %collective-permute-start.5 = (f32[3,72,256]{2,1,0:T(8,128)S(1)}, f32[3,72,256]{2,1,0:T(8,128)S(1)}, u32[]{:S(2)}, u32[]{:S(2)}) collective-permute-start(f32[3,72,256]{2,1,0:T(8,128)S(1)} %get-tuple-element.22), channel_id=1, source_target_pairs={{0,2},{2,0},{4,6},{6,4},{8,10},{10,8},{12,14},{14,12},{16,18},{18,... | collective-permute-start | bytes 663560 | tf_op jit(solution)/shard_map/ppermute | solution.py:364
  66.2 1.7 %collective-permute-done.6.off = f32[3,72,256]{2,1,0:T(8,128)S(1)} collective-permute-done((f32[3,72,256]{2,1,0:T(8,128)S(1)}, f32[3,72,256]{2,1,0:T(8,128)S(1)}, u32[]{:S(2)}, u32[]{:S(2)}) %collective-permute-start.6) | collective-permute-done | bytes 221216 | tf_op jit(solution)/shard_map/ppermute | solution.py:363
  67.9 5.3 %shard_map.58 = f32[8,64,256]{2,1,0:T(8,128)} custom-call(s32[3]{0:T(128)S(1)} %pad_add_fusion.place, f32[8,72,256]{2,1,0:T(8,128)S(1)} %all_to_all.11.field, f32[3,72,256]{2,1,0:T(8,128)S(1)} %collective-permute-done.5.on, f32[3,72,256]{2,1,0:T(8,128)S(1)} %collective-permute-done.6.off), custom_call_target="tpu_custom_call" | custom-call | tf_op jit(solution)/shard_map/pallas_call | solution.py:289
  (15 shorter events, 0.1 us)
Async XLA Ops:
  0.0 6.6 %copy-start = (f32[8,64,256]{2,1,0:T(8,128)S(1)}, f32[8,64,256]{2,1,0:T(8,128)}, u32[]{:S(2)}) copy-start(f32[8,64,256]{2,1,0:T(8,128)} %est.3) | copy-start | bytes 1572868
  2.0 12.9 %collective-permute-start = (f32[8,24,256]{2,1,0:T(8,128)S(1)}, f32[8,24,256]{2,1,0:T(8,128)S(1)}, u32[]{:S(2)}, u32[]{:S(2)}) collective-permute-start(f32[8,24,256]{2,1,0:T(8,128)S(1)} %pad_maximum_fusion.2), channel_id=1, source_target_pairs={{0,1},{1,0},{2,3},{3,2},{4,5},{5,4},{6,7},{7,6},{8,9},{9,8},{10,11... | collective-permute-start | bytes 589832 | tf_op jit(solution)/shard_map/ppermute | solution.py:321
  6.6 17.1 %collective-permute-start.2 = (f32[8,64,256]{2,1,0:T(8,128)S(1)}, f32[8,64,256]{2,1,0:T(8,128)S(1)}, u32[]{:S(2)}, u32[]{:S(2)}) collective-permute-start(f32[8,64,256]{2,1,0:T(8,128)S(1)} %copy-done), channel_id=1, source_target_pairs={{2,4},{6,8},{10,12},{14,16},{18,20},{22,24},{26,28},{30,32},{34,36... | collective-permute-start | bytes 1572872 | tf_op jit(solution)/shard_map/ppermute | solution.py:323
  11.0 12.7 %collective-permute-start.1 = (f32[8,64,256]{2,1,0:T(8,128)S(1)}, f32[8,64,256]{2,1,0:T(8,128)S(1)}, u32[]{:S(2)}, u32[]{:S(2)}) collective-permute-start(f32[8,64,256]{2,1,0:T(8,128)S(1)} %copy-done), channel_id=1, source_target_pairs={{0,2},{2,0},{4,6},{6,4},{8,10},{10,8},{12,14},{14,12},{16,18},{18,... | collective-permute-start | bytes 1572872 | tf_op jit(solution)/shard_map/ppermute | solution.py:324
  13.0 0.7 copy-start.4
  15.0 11.3 %collective-permute-start.4 = (f32[448,256]{1,0:T(8,128)S(1)}, f32[448,256]{1,0:T(8,128)S(1)}, u32[]{:S(2)}, u32[]{:S(2)}) collective-permute-start(f32[448,256]{1,0:T(8,128)S(1)} %get-tuple-element.25), channel_id=1, source_target_pairs={{2,4},{6,8},{10,12},{14,16},{18,20},{22,24},{26,28},{30,32},{34,36... | collective-permute-start | bytes 1376264 | tf_op jit(solution)/shard_map/ppermute | solution.py:330
  20.1 6.2 %collective-permute-start.3 = (f32[448,256]{1,0:T(8,128)S(1)}, f32[448,256]{1,0:T(8,128)S(1)}, u32[]{:S(2)}, u32[]{:S(2)}) collective-permute-start(f32[448,256]{1,0:T(8,128)S(1)} %get-tuple-element.26), channel_id=1, source_target_pairs={{0,2},{2,0},{4,6},{6,4},{8,10},{10,8},{12,14},{14,12},{16,18},{18,... | collective-permute-start | bytes 1376264 | tf_op jit(solution)/shard_map/ppermute | solution.py:331
  22.1 0.7 copy-start.2
  22.1 0.7 copy-start.3
  22.7 3.6 %copy-start.1 = (f32[1,8,64,256]{3,2,1,0:T(8,128)S(1)}, f32[1,8,64,256]{3,2,1,0:T(8,128)}, u32[]{:S(2)}) copy-start(f32[1,8,64,256]{3,2,1,0:T(8,128)} %param.5) | copy-start | bytes 1572868
  57.8 10.1 %collective-permute-start.6 = (f32[3,72,256]{2,1,0:T(8,128)S(1)}, f32[3,72,256]{2,1,0:T(8,128)S(1)}, u32[]{:S(2)}, u32[]{:S(2)}) collective-permute-start(f32[3,72,256]{2,1,0:T(8,128)S(1)} %get-tuple-element.21), channel_id=1, source_target_pairs={{2,4},{6,8},{10,12},{14,16},{18,20},{22,24},{26,28},{30,32},{34,36... | collective-permute-start | bytes 663560 | tf_op jit(solution)/shard_map/ppermute | solution.py:363
  64.3 3.6 %collective-permute-start.5 = (f32[3,72,256]{2,1,0:T(8,128)S(1)}, f32[3,72,256]{2,1,0:T(8,128)S(1)}, u32[]{:S(2)}, u32[]{:S(2)}) collective-permute-start(f32[3,72,256]{2,1,0:T(8,128)S(1)} %get-tuple-element.22), channel_id=1, source_target_pairs={{0,2},{2,0},{4,6},{6,4},{8,10},{10,8},{12,14},{14,12},{16,18},{18,... | collective-permute-start | bytes 663560 | tf_op jit(solution)/shard_map/ppermute | solution.py:364

commit v3 on v2

--- a/solution.py
+++ b/solution.py
@@ -37,9 +37,9 @@
     halo1, halo2 = pitch - rows, pitch - rows - DATA_STRIP
 
     def taps(axis, shape):
-        k = perm[axis]
-        reach = band[k]
-        parts = [jnp.where(t <= reach, prof[k * (WIDTH + 1) + t], 0.0) for t in range(WIDTH + 1)]
+        k = perm[0, axis]
+        reach = band[0, k]
+        parts = [jnp.where(t <= reach, prof[0, k, t], 0.0) for t in range(WIDTH + 1)]
         total = parts[0]
         for part in parts[1:]:
             total = total + 2.0 * part
@@ -218,74 +218,90 @@
             out[v] = value
 
 
-def variation_kernel(slabs, rows, place, field, on, off, out, rims, first, second):
+def variation_kernel(slabs, rows, place, field, on, off, out, start, first, second):
     planes, used, lanes = field.shape
     slab, row = place[1], place[2]
-    lane = lax.broadcasted_iota(jnp.int32, (used, lanes), 1)
-    line = lax.broadcasted_iota(jnp.int32, (used, lanes), 0)
-
+    half = lanes // 2
     odd = lax.rem(slab, 2)
-    rims[pl.ds(odd * TV_HALO, TV_HALO)] = off[...]
-    rims[pl.ds((1 - odd) * TV_HALO, TV_HALO)] = on[...]
-
-    def up(x, axis, index, last):
-        return jnp.where(index == last, 0.0, pltpu.roll(x, x.shape[axis] - 1, axis))
-
-    def down(x, axis, index):
-        return jnp.where(index == 0, 0.0, pltpu.roll(x, 1, axis))
-
-    def one_pass(read, low, high, write):
-        before = None
-        current = read(low - 1)
-        for z in range(low - 1, high):
-            after = read(z + 1)
-            g_z = after - current
-            g_y = up(current, 0, line, used - 1) - current
-            g_x = up(current, 1, lane, lanes - 1) - current
-            scale = lax.rsqrt(g_z * g_z + g_y * g_y + g_x * g_x + EPS2)
-            if z < 0:
-                scale = jnp.where(slab > 0, scale, 0.0)
-            f_z = g_z * scale
-            if z >= low:
-                f_y, f_x = g_y * scale, g_x * scale
-                spread = f_z - before + f_y - down(f_y, 0, line) + f_x - down(f_x, 1, lane)
-                value = current + TAU * spread
-                if z < 0:
-                    value = jnp.where(slab > 0, value, 0.0)
-                if z >= planes:
-                    value = jnp.where(slab < slabs - 1, value, 0.0)
-                write(z, value)
-            before, current = f_z, after
-
-    def read_field(z):
-        if z < 0:
-            return rims[z + TV_HALO]
-        if z >= planes:
-            return rims[z - planes + TV_HALO]
-        return field[z]
-
-    def into(ref):
-        def write(z, value):
-            ref[z + TV_HALO] = value
-
-        return write
-
-    def last(z, value):
-        @pl.when(row == 0)
-        def _():
-            out[z] = value[0:rows]
-
-        @pl.when(row == 1)
-        def _():
-            out[z] = value[used - rows :]
-
-    one_pass(read_field, -2, planes + 2, into(first))
-    one_pass(lambda z: first[z + TV_HALO], -1, planes + 1, into(second))
-    one_pass(lambda z: second[z + TV_HALO], 0, planes, last)
-
-
-def call(kernel, shapes, scratch, *args, cost=None):
-    specs = [SMEM if jnp.ndim(a) == 1 else VMEM for a in args]
+    start[pl.ds(odd * (planes + TV_HALO), TV_HALO)] = off[...]
+    start[pl.ds((1 - odd) * (planes + TV_HALO), TV_HALO)] = on[...]
+    start[TV_HALO : TV_HALO + planes] = field[...]
+    lane = lax.broadcasted_iota(jnp.int32, (1, 1, half), 2)
+    line = lax.broadcasted_iota(jnp.int32, (1, 8, half), 1)
+
+    def next_x(x):
+        turned = [pltpu.roll(h, half - 1, 2) for h in x]
+        return [
+            jnp.where(lane == half - 1, turned[1], turned[0]),
+            jnp.where(lane == half - 1, 0.0, turned[1]),
+        ]
+
+    def last_x(x):
+        turned = [pltpu.roll(h, 1, 2) for h in x]
+        return [jnp.where(lane == 0, 0.0, turned[0]), jnp.where(lane == 0, turned[0], turned[1])]
+
+    def next_y(x):
+        turned = pltpu.roll(x, used - 1, 1)
+        last = jnp.where(line == 7, 0.0, turned[:, used - 8 :])
+        return jnp.concatenate([turned[:, : used - 8], last], axis=1)
+
+    def last_y(x):
+        turned = pltpu.roll(x, 1, 1)
+        return jnp.concatenate([jnp.where(line == 0, 0.0, turned[:, :8]), turned[:, 8:]], axis=1)
+
+    def masked(x, z):
+        if z >= TV_HALO and z + x.shape[0] <= TV_HALO + planes:
+            return x
+        parts = []
+        for i in range(x.shape[0]):
+            part = x[i : i + 1]
+            if z + i < TV_HALO:
+                part = jnp.where(slab > 0, part, 0.0)
+            elif z + i >= TV_HALO + planes:
+                part = jnp.where(slab < slabs - 1, part, 0.0)
+            parts.append(part)
+        return jnp.concatenate(parts, axis=0) if len(parts) > 1 else parts[0]
+
+    def flux(source, z, count, only_z):
+        box = [slice(h * half, (h + 1) * half) for h in range(2)]
+        now = [source[z : z + count, :, b] for b in box]
+        after = [source[z + 1 : z + count + 1, :, b] for b in box]
+        side = next_x(now)
+        f_x, f_y, f_z = [], [], []
+        for h in range(2):
+            g_z, g_y, g_x = after[h] - now[h], next_y(now[h]) - now[h], side[h] - now[h]
+            scale = masked(lax.rsqrt(g_z * g_z + g_y * g_y + g_x * g_x + EPS2), z)
+            f_z.append(g_z * scale)
+            if not only_z:
+                f_y.append(g_y * scale)
+                f_x.append(g_x * scale)
+        return now, f_x, f_y, f_z
+
+    def one_pass(source, low, high, group, target):
+        before = flux(source, low - 1, 1, True)[3]
+        for z in range(low, high, group):
+            count = min(group, high - z)
+            now, f_x, f_y, f_z = flux(source, z, count, False)
+            side = last_x(f_x)
+            for h in range(2):
+                below = before[h]
+                if count > 1:
+                    below = jnp.concatenate([below, f_z[h][: count - 1]], axis=0)
+                spread = (f_z[h] - below) + (f_y[h] - last_y(f_y[h])) + (f_x[h] - side[h])
+                target[z : z + count, :, h * half : (h + 1) * half] = masked(now[h] + TAU * spread, z)
+            before = [f[count - 1 : count] for f in f_z]
+
+    deep = planes + 2 * TV_HALO
+    groups = (4, 5, 4)
+    one_pass(start, 1, deep - 1, groups[0], first)
+    one_pass(first, 2, deep - 2, groups[1], second)
+    one_pass(second, 3, deep - 3, groups[2], first)
+    skip = pl.multiple_of(row * (used - rows), 8)
+    out[...] = first[TV_HALO : TV_HALO + planes, pl.ds(skip, rows), :]
+
+
+def call(kernel, shapes, scratch, *args, cost=None, scalars=1):
+    specs = [SMEM if i < scalars else VMEM for i in range(len(args))]
     return pl.pallas_call(
         kernel,
         out_shape=shapes,
@@ -337,7 +353,8 @@
         + [half((lanes, lanes))] * 2
         + [half((3 * pitch, 3 * pitch))] * 4,
         [],
-        place, band[0], axes_perm[0], profile.reshape(-1),
+        place, band, axes_perm, profile,
+        scalars=4,
         cost=pl.CostEstimate(flops=COST, bytes_accessed=0, transcendentals=0),
     )
     back = call(
@@ -366,7 +383,7 @@
     return call(
         functools.partial(variation_kernel, slabs, rows),
         shape((planes, rows, lanes)),
-        [pltpu.VMEM((2 * TV_HALO, used, lanes), F32), deep, deep],
+        [deep, deep, deep],
         place, field, on, off,
     )
 

time: 73.6 us -> 71.9 us (0.977)
  Pallas kernels: 10.2 us -> 8.62 us
    pallas_call x4, Pallas kernels: 10.2 us -> 8.62 us  [call(): pl.pallas_call(kernel, out_shape=shapes, in_specs=specs, out_specs=jax.tr...]
where the time goes in v3:
time: 71.9 us; the launch traced here: 71.5 us
  blocking collectives  27.5 us (38%)
  starting transfers between devices  26.6 us (37%)
  Pallas kernels  8.62 us (12%)
  waiting for transfers between devices  4.66 us (6%)
  other arithmetic  3.19 us (4%)
    all_to_all x1, blocking collectives, body(): parts = lax.all_to_all(back, 'view', 0, 0, tiled=True)  14.9 us
    all_to_all x1, blocking collectives, body(): field = lax.all_to_all(copies, 'view', 0, 0, tiled=True)  12.6 us
    pallas_call x4, Pallas kernels, call(): pl.pallas_call(kernel, out_shape=shapes, in_specs=specs, out_specs=jax.tr...  8.62 us
    ppermute x1, starting transfers between devices, body(): off = lax.ppermute(jnp.where(is_odd, high, low), 'slab', off_pairs)  6.48 us
    ppermute x1, starting transfers between devices, body(): off = lax.ppermute(off, 'slab', off_pairs)  5.14 us
    ppermute x1, starting transfers between devices, body(): strip = lax.ppermute(edge, 'row', [(0, 1), (1, 0)])  4.65 us
    ppermute x1, starting transfers between devices, body(): est_off = lax.ppermute(held, 'slab', off_pairs)  4.39 us
    ppermute x1, waiting for transfers between devices, body(): off = lax.ppermute(off, 'slab', off_pairs)  2.98 us
  transfers between devices with their start and end apart: 7, of which 2 were waited for; matrix products, arithmetic and copies ran while one was open for 2% of the time, Pallas kernels for 1%

profile of v3, /device:TPU:193, one launch (start us, length us, event | category | flops | bytes accessed | tf_op | source)
XLA Modules:
  0.0 71.5 jit_solution(17539612885468997311)
XLA Ops:
  0.0 0.9 %slice_select_fusion.5 = f32[8,8,256]{2,1,0:T(8,128)S(1)} fusion(f32[8,64,256]{2,1,0:T(8,128)} %bitcast.7, pred[]{:T(512)S(6)} %eq.6), kind=kLoop, calls=%fused_computation.8 | loop fusion | flops 16384 | bytes 196609 | tf_op jit(solution)/shard_map/jit(_where)/select_n | solution.py:333
  0.9 1.0 %slice_select_fusion.4 = f32[8,16,256]{2,1,0:T(8,128)S(1)} fusion(f32[8,64,256]{2,1,0:T(8,128)} %est.3, pred[]{:T(512)S(6)} %eq.6), kind=kLoop, calls=%fused_computation.7 | loop fusion | flops 32768 | bytes 393217 | tf_op jit(solution)/shard_map/jit(_where)/select_n | solution.py:332
  2.0 4.7 %collective-permute-start = (f32[8,24,256]{2,1,0:T(8,128)S(1)}, f32[8,24,256]{2,1,0:T(8,128)S(1)}, u32[]{:S(2)}, u32[]{:S(2)}) collective-permute-start(f32[8,24,256]{2,1,0:T(8,128)S(1)} %pad_maximum_fusion.2), channel_id=1, source_target_pairs={{0,1},{1,0},{2,3},{3,2},{4,5},{5,4},{6,7},{7,6},{8,9},{9,8},{10,11... | collective-permute-start | bytes 589832 | tf_op jit(solution)/shard_map/ppermute | solution.py:337
  6.6 4.4 %collective-permute-start.2 = (f32[8,64,256]{2,1,0:T(8,128)S(1)}, f32[8,64,256]{2,1,0:T(8,128)S(1)}, u32[]{:S(2)}, u32[]{:S(2)}) collective-permute-start(f32[8,64,256]{2,1,0:T(8,128)S(1)} %copy-done), channel_id=1, source_target_pairs={{2,4},{6,8},{10,12},{14,16},{18,20},{22,24},{26,28},{30,32},{34,36... | collective-permute-start | bytes 1572872 | tf_op jit(solution)/shard_map/ppermute | solution.py:339
  11.0 1.9 %collective-permute-start.1 = (f32[8,64,256]{2,1,0:T(8,128)S(1)}, f32[8,64,256]{2,1,0:T(8,128)S(1)}, u32[]{:S(2)}, u32[]{:S(2)}) collective-permute-start(f32[8,64,256]{2,1,0:T(8,128)S(1)} %copy-done), channel_id=1, source_target_pairs={{0,2},{2,0},{4,6},{6,4},{8,10},{10,8},{12,14},{14,12},{16,18},{18,... | collective-permute-start | bytes 1572872 | tf_op jit(solution)/shard_map/ppermute | solution.py:340
  13.0 0.0 copy-start.4
  13.0 0.7 copy-done.4
  13.7 0.1 pad_add_fusion.place
  13.7 1.1 %slice_select_fusion = (f32[1,4,64,256]{3,2,1,0:T(8,128)S(1)}, f32[1,4,64,256]{3,2,1,0:T(8,128)S(1)}) fusion(f32[1,8,64,256]{3,2,1,0:T(8,128)} %param.5, pred[]{:T(512)S(6)} %eq.7), kind=kLoop, calls=%fused_computation.2 | loop fusion | flops 131072 | bytes 1048577 | tf_op jit(solution)/shard_map/jit(_where)/select_n | solution.py:344
  14.8 0.1 pad_maximum_fusion
  14.9 0.0 copy-start.2
  14.9 5.1 %collective-permute-start.4 = (f32[448,256]{1,0:T(8,128)S(1)}, f32[448,256]{1,0:T(8,128)S(1)}, u32[]{:S(2)}, u32[]{:S(2)}) collective-permute-start(f32[448,256]{1,0:T(8,128)S(1)} %get-tuple-element.25), channel_id=1, source_target_pairs={{2,4},{6,8},{10,12},{14,16},{18,20},{22,24},{26,28},{30,32},{34,36... | collective-permute-start | bytes 1376264 | tf_op jit(solution)/shard_map/ppermute | solution.py:346
  20.1 0.0 copy-start.1
  20.1 2.1 %collective-permute-start.3 = (f32[448,256]{1,0:T(8,128)S(1)}, f32[448,256]{1,0:T(8,128)S(1)}, u32[]{:S(2)}, u32[]{:S(2)}) collective-permute-start(f32[448,256]{1,0:T(8,128)S(1)} %get-tuple-element.26), channel_id=1, source_target_pairs={{0,2},{2,0},{4,6},{6,4},{8,10},{10,8},{12,14},{14,12},{16,18},{18,... | collective-permute-start | bytes 1376264 | tf_op jit(solution)/shard_map/ppermute | solution.py:347
  22.1 1.1 %shard_map.55 = (f32[5,16,256]{2,1,0:T(8,128)S(1)}, bf16[256,256]{1,0:T(8,128)(2,1)S(1)}, bf16[256,256]{1,0:T(8,128)(2,1)S(1)}, bf16[240,240]{1,0:T(8,128)(2,1)S...) custom-call(s32[3]{0:T(128)S(1)} %pad_add_fusion.place, ...), custom_call_target="tpu_custom_call" | custom-call | flops 20000000000 | tf_op jit(solution)/shard_map/pallas_call | solution.py:305
  23.2 3.0 %collective-permute-done.4.off = f32[448,256]{1,0:T(8,128)S(1)} collective-permute-done((f32[448,256]{1,0:T(8,128)S(1)}, f32[448,256]{1,0:T(8,128)S(1)}, u32[]{:S(2)}, u32[]{:S(2)}) %collective-permute-start.4) | collective-permute-done | bytes 458784 | tf_op jit(solution)/shard_map/ppermute | solution.py:346
  26.2 3.3 %shard_map.56 = f32[8,72,256]{2,1,0:T(8,128)S(1)} custom-call(s32[3]{0:T(128)S(1)} %pad_add_fusion.place, f32[8,64,256]{2,1,0:T(8,128)S(1)} %copy-done, f32[8,64,256]{2,1,0:T(8,128)S(1)} %bitcast.8, f32[8,24,256]{2,1,0:T(8,128)S(1)} %collective-permute-done.strip, f32[8,64,256]{2,1,0:T(8,128)S(1)} %collective-permute-done.1.est_on, ...), custom_call_target="tpu_custom_call" | custom-call | tf_op jit(solution)/shard_map/pallas_call | solution.py:305
  29.6 14.9 %all_to_all.10.parts = f32[8,72,256]{2,1,0:T(8,128)S(1)} all-to-all(f32[8,72,256]{2,1,0:T(8,128)S(1)} %shard_map.56), channel_id=1, replica_groups=mesh['view'=8,'slab'=32,'row'=2] {'view'}, dimensions={0} | all-to-all | bytes 1179648 | tf_op jit(solution)/shard_map/all_to_all | solution.py:370
  44.5 0.6 shard_map.57
  45.1 12.6 %all_to_all.11.field = f32[8,72,256]{2,1,0:T(8,128)S(1)} all-to-all(f32[8,72,256]{2,1,0:T(8,128)S(1)} %shard_map.57), channel_id=1, replica_groups=mesh['view'=8,'slab'=32,'row'=2] {'view'}, dimensions={0} | all-to-all | bytes 1179648 | tf_op jit(solution)/shard_map/all_to_all | solution.py:377
  57.7 6.5 %collective-permute-start.6 = (f32[3,72,256]{2,1,0:T(8,128)S(1)}, f32[3,72,256]{2,1,0:T(8,128)S(1)}, u32[]{:S(2)}, u32[]{:S(2)}) collective-permute-start(f32[3,72,256]{2,1,0:T(8,128)S(1)} %get-tuple-element.21), channel_id=1, source_target_pairs={{2,4},{6,8},{10,12},{14,16},{18,20},{22,24},{26,28},{30,32},{34,36... | collective-permute-start | bytes 663560 | tf_op jit(solution)/shard_map/ppermute | solution.py:380
  64.2 1.9 %collective-permute-start.5 = (f32[3,72,256]{2,1,0:T(8,128)S(1)}, f32[3,72,256]{2,1,0:T(8,128)S(1)}, u32[]{:S(2)}, u32[]{:S(2)}) collective-permute-start(f32[3,72,256]{2,1,0:T(8,128)S(1)} %get-tuple-element.22), channel_id=1, source_target_pairs={{0,2},{2,0},{4,6},{6,4},{8,10},{10,8},{12,14},{14,12},{16,18},{18,... | collective-permute-start | bytes 663560 | tf_op jit(solution)/shard_map/ppermute | solution.py:381
  66.2 1.7 %collective-permute-done.6.off = f32[3,72,256]{2,1,0:T(8,128)S(1)} collective-permute-done((f32[3,72,256]{2,1,0:T(8,128)S(1)}, f32[3,72,256]{2,1,0:T(8,128)S(1)}, u32[]{:S(2)}, u32[]{:S(2)}) %collective-permute-start.6) | collective-permute-done | bytes 221216 | tf_op jit(solution)/shard_map/ppermute | solution.py:380
  67.8 3.6 %shard_map.58 = f32[8,64,256]{2,1,0:T(8,128)} custom-call(s32[3]{0:T(128)S(1)} %pad_add_fusion.place, f32[8,72,256]{2,1,0:T(8,128)S(1)} %all_to_all.11.field, f32[3,72,256]{2,1,0:T(8,128)S(1)} %collective-permute-done.5.on, f32[3,72,256]{2,1,0:T(8,128)S(1)} %collective-permute-done.6.off), custom_call_target="tpu_custom_call" | custom-call | tf_op jit(solution)/shard_map/pallas_call | solution.py:305
  (14 shorter events, 0.1 us)
Async XLA Ops:
  0.0 6.6 %copy-start = (f32[8,64,256]{2,1,0:T(8,128)S(1)}, f32[8,64,256]{2,1,0:T(8,128)}, u32[]{:S(2)}) copy-start(f32[8,64,256]{2,1,0:T(8,128)} %est.3) | copy-start | bytes 1572868
  2.0 12.8 %collective-permute-start = (f32[8,24,256]{2,1,0:T(8,128)S(1)}, f32[8,24,256]{2,1,0:T(8,128)S(1)}, u32[]{:S(2)}, u32[]{:S(2)}) collective-permute-start(f32[8,24,256]{2,1,0:T(8,128)S(1)} %pad_maximum_fusion.2), channel_id=1, source_target_pairs={{0,1},{1,0},{2,3},{3,2},{4,5},{5,4},{6,7},{7,6},{8,9},{9,8},{10,11... | collective-permute-start | bytes 589832 | tf_op jit(solution)/shard_map/ppermute | solution.py:337
  6.6 16.6 %collective-permute-start.2 = (f32[8,64,256]{2,1,0:T(8,128)S(1)}, f32[8,64,256]{2,1,0:T(8,128)S(1)}, u32[]{:S(2)}, u32[]{:S(2)}) collective-permute-start(f32[8,64,256]{2,1,0:T(8,128)S(1)} %copy-done), channel_id=1, source_target_pairs={{2,4},{6,8},{10,12},{14,16},{18,20},{22,24},{26,28},{30,32},{34,36... | collective-permute-start | bytes 1572872 | tf_op jit(solution)/shard_map/ppermute | solution.py:339
  11.0 12.2 %collective-permute-start.1 = (f32[8,64,256]{2,1,0:T(8,128)S(1)}, f32[8,64,256]{2,1,0:T(8,128)S(1)}, u32[]{:S(2)}, u32[]{:S(2)}) collective-permute-start(f32[8,64,256]{2,1,0:T(8,128)S(1)} %copy-done), channel_id=1, source_target_pairs={{0,2},{2,0},{4,6},{6,4},{8,10},{10,8},{12,14},{14,12},{16,18},{18,... | collective-permute-start | bytes 1572872 | tf_op jit(solution)/shard_map/ppermute | solution.py:340
  13.0 0.7 copy-start.4
  14.9 7.2 %copy-start.2 = (s32[1,3]{1,0:T(1,128)S(1)}, s32[1,3]{1,0:T(1,128)}, u32[]{:S(2)}) copy-start(s32[1,3]{1,0:T(1,128)} %band.1) | copy-start | bytes 40
  14.9 7.2 %copy-start.3 = (s32[1,3]{1,0:T(1,128)S(1)}, s32[1,3]{1,0:T(1,128)}, u32[]{:S(2)}) copy-start(s32[1,3]{1,0:T(1,128)} %perm.1) | copy-start | bytes 40
  14.9 11.3 %collective-permute-start.4 = (f32[448,256]{1,0:T(8,128)S(1)}, f32[448,256]{1,0:T(8,128)S(1)}, u32[]{:S(2)}, u32[]{:S(2)}) collective-permute-start(f32[448,256]{1,0:T(8,128)S(1)} %get-tuple-element.25), channel_id=1, source_target_pairs={{2,4},{6,8},{10,12},{14,16},{18,20},{22,24},{26,28},{30,32},{34,36... | collective-permute-start | bytes 1376264 | tf_op jit(solution)/shard_map/ppermute | solution.py:346
  20.1 6.2 %copy-start.1 = (f32[1,8,64,256]{3,2,1,0:T(8,128)S(1)}, f32[1,8,64,256]{3,2,1,0:T(8,128)}, u32[]{:S(2)}) copy-start(f32[1,8,64,256]{3,2,1,0:T(8,128)} %param.5) | copy-start | bytes 1572868
  20.1 6.1 %collective-permute-start.3 = (f32[448,256]{1,0:T(8,128)S(1)}, f32[448,256]{1,0:T(8,128)S(1)}, u32[]{:S(2)}, u32[]{:S(2)}) collective-permute-start(f32[448,256]{1,0:T(8,128)S(1)} %get-tuple-element.26), channel_id=1, source_target_pairs={{0,2},{2,0},{4,6},{6,4},{8,10},{10,8},{12,14},{14,12},{16,18},{18,... | collective-permute-start | bytes 1376264 | tf_op jit(solution)/shard_map/ppermute | solution.py:347
  57.7 10.1 %collective-permute-start.6 = (f32[3,72,256]{2,1,0:T(8,128)S(1)}, f32[3,72,256]{2,1,0:T(8,128)S(1)}, u32[]{:S(2)}, u32[]{:S(2)}) collective-permute-start(f32[3,72,256]{2,1,0:T(8,128)S(1)} %get-tuple-element.21), channel_id=1, source_target_pairs={{2,4},{6,8},{10,12},{14,16},{18,20},{22,24},{26,28},{30,32},{34,36... | collective-permute-start | bytes 663560 | tf_op jit(solution)/shard_map/ppermute | solution.py:380
  64.2 3.6 %collective-permute-start.5 = (f32[3,72,256]{2,1,0:T(8,128)S(1)}, f32[3,72,256]{2,1,0:T(8,128)S(1)}, u32[]{:S(2)}, u32[]{:S(2)}) collective-permute-start(f32[3,72,256]{2,1,0:T(8,128)S(1)} %get-tuple-element.22), channel_id=1, source_target_pairs={{0,2},{2,0},{4,6},{6,4},{8,10},{10,8},{12,14},{14,12},{16,18},{18,... | collective-permute-start | bytes 663560 | tf_op jit(solution)/shard_map/ppermute | solution.py:381

commit v4 on v3

--- a/solution.py
+++ b/solution.py
@@ -31,10 +31,10 @@
     return dot(a_high, b_high) + (dot(a_low, b_high) + dot(a_high, b_low))
 
 
-def weights_kernel(rows, place, band, perm, prof, taps_z, wx_h, wx_l, wy1_h, wy1_l, wy2_h, wy2_l):
+def weights_kernel(rows, place, band, perm, prof, taps_z, wx_h, wx_l, wo_h, wo_l, wr_h, wr_l, wy2_h, wy2_l):
     row = place[2]
-    pitch = wy1_h.shape[0] // 3
-    halo1, halo2 = pitch - rows, pitch - rows - DATA_STRIP
+    pitch = wy2_h.shape[0] // 3
+    used = rows + DATA_STRIP
 
     def taps(axis, shape):
         k = perm[0, axis]
@@ -63,136 +63,162 @@
         taps_z[t] = tap
     banded(2, wx_h.shape, lambda i, j: i - j, lambda i, j: (i >= 0), wx_h, wx_l)
 
-    def plane_of(i):
-        return (i >= pitch).astype(jnp.int32) + (i >= 2 * pitch).astype(jnp.int32)
+    most = wo_h.shape[0]
+
+    def plane_of(i, height):
+        return sum((i >= n * height).astype(jnp.int32) for n in range(1, most // height))
+
+    def within(i, height):
+        return i - height * plane_of(i, height)
 
     def halo_place(i, strip):
-        i = i - pitch * plane_of(i)
         return jnp.where((i >= rows) & (row == 1), i - rows - strip, i)
 
+    def reached(i):
+        return jnp.where(i < 8, i + (rows - 8) * (1 - row), halo_place(i - 8 + rows, DATA_STRIP))
+
     def ascending(i):
-        return i - pitch * plane_of(i) - DATA_STRIP * row
-
-    def same(i, j):
-        return plane_of(i) == plane_of(j)
-
-    def used(i):
-        return i - pitch * plane_of(i) < rows + DATA_STRIP
+        return within(i, pitch) - DATA_STRIP * row
 
     banded(
         1,
-        wy1_h.shape,
-        lambda i, j: halo_place(i, DATA_STRIP) - halo_place(j, EST_STRIP),
-        lambda i, j: same(i, j) & used(i),
-        wy1_h,
-        wy1_l,
+        wo_h.shape,
+        lambda i, j: halo_place(within(i, used), DATA_STRIP) - within(j, rows),
+        lambda i, j: plane_of(i, used) == plane_of(j, rows),
+        wo_h,
+        wo_l,
+    )
+    banded(
+        1,
+        wr_h.shape,
+        lambda i, j: reached(within(i, 16)) - halo_place(within(j, 16) + rows, EST_STRIP),
+        lambda i, j: plane_of(i, 16) == plane_of(j, 16),
+        wr_h,
+        wr_l,
     )
     banded(
         1,
         wy2_h.shape,
-        lambda i, j: ascending(i) - halo_place(j, DATA_STRIP),
-        lambda i, j: same(i, j) & used(i) & used(j),
+        lambda i, j: ascending(i) - halo_place(within(j, pitch), DATA_STRIP),
+        lambda i, j: (plane_of(i, pitch) == plane_of(j, pitch))
+        & (within(i, pitch) < used)
+        & (within(j, pitch) < used),
         wy2_h,
         wy2_l,
     )
 
 
 def blur_z(read, taps_z):
-    total = taps_z[0] * read(WIDTH)
+    taps = [taps_z[t, 0:1, :] for t in range(WIDTH + 1)]
+    total = taps[0] * read(WIDTH)
     for t in range(1, WIDTH + 1):
-        total = total + taps_z[t] * (read(WIDTH - t) + read(WIDTH + t))
+        total = total + taps[t] * (read(WIDTH - t) + read(WIDTH + t))
     return total
 
 
+def blur_yx(x, w_h, w_l, wx_h, wx_l):
+    x_h, x_l = split(x)
+    m_h, m_l = split(dot3(w_h, w_l, x_h, x_l))
+    return dot3(m_h, m_l, wx_h[...], wx_l[...])
+
+
+def own_kernel(place, est, est_off, est_on, taps_z, wx_h, wx_l, wo_h, wo_l, out, flat):
+    planes, rows, lanes = est.shape
+    wide, used, _ = out.shape
+    odd = lax.rem(place[1], 2) == 1
+    group = 256 // rows
+
+    def blur_first(below, above):
+        for p in range(wide):
+            flat[p * rows : (p + 1) * rows, :] = blur_z(
+                lambda t: (below, est, above)[(p + t) // planes][(p + t) % planes], taps_z
+            )
+
+    @pl.when(odd)
+    def _():
+        blur_first(est_on, est_off)
+
+    @pl.when(jnp.logical_not(odd))
+    def _():
+        blur_first(est_off, est_on)
+
+    for p in range(0, wide, group):
+        part = flat[p * rows : (p + group) * rows, :]
+        part = blur_yx(part, wo_h[...], wo_l[...], wx_h, wx_l)
+        out[p : p + group] = part.reshape(group, used, lanes)
+
+
 def views_kernel(
-    slabs, place, est, data, strip, est_on, est_off, on, off,
-    taps_z, wx_h, wx_l, wy1_h, wy1_l, wy2_h, wy2_l, out, flat1, ratio, flat2,
+    slabs, place, partial, data, strip, off, on,
+    taps_z, wx_h, wx_l, wr_h, wr_l, wy2_h, wy2_l, out, rims, ratio, flat,
 ):
-    planes, rows, lanes = est.shape
-    slab = place[1]
+    planes, rows, lanes = data.shape
+    slab, row = place[1], place[2]
     pitch = rows + EST_STRIP
     used = rows + DATA_STRIP
     wide = planes + 2 * WIDTH
-
-    odd = lax.rem(slab, 2) == 1
-
     thick = EST_STRIP + DATA_STRIP
     base = planes * thick
-
-    def blur_first(below, above, strip_below, strip_above):
-        def est_plane(q, first):
-            ref = (below, est, above)[q // planes]
-            return ref[q % planes, first : first + 16, :]
-
-        def est_strip(q):
+    odd = lax.rem(slab, 2) == 1
+
+    def blur_first(below, above):
+        def read(q):
             if q // planes == 1:
                 return strip[q - planes, 0:EST_STRIP, :]
             at = q % planes * thick
-            return (strip_below, strip_above)[q // planes // 2][at : at + EST_STRIP, :]
+            return (below, above)[q // planes // 2][at : at + EST_STRIP, :]
 
         for p in range(wide):
-            for first in range(0, rows, 16):
-                flat1[p * pitch + first : p * pitch + first + 16, :] = blur_z(
-                    lambda t: est_plane(p + t, first), taps_z
-                )
-            flat1[p * pitch + rows : (p + 1) * pitch, :] = blur_z(lambda t: est_strip(p + t), taps_z)
+            rims[p * EST_STRIP : (p + 1) * EST_STRIP, :] = blur_z(lambda t: read(p + t), taps_z)
 
     @pl.when(odd)
     def _():
-        blur_first(est_on, est_off, on, off)
+        blur_first(on, off)
 
     @pl.when(jnp.logical_not(odd))
     def _():
-        blur_first(est_off, est_on, off, on)
-
-    def blur_yx(flat, start, count, w_h, w_l):
-        n = count * pitch
-        x_h, x_l = split(flat[start * pitch : start * pitch + n, :])
-        mid = dot3(w_h[0:n, 0:n], w_l[0:n, 0:n], x_h, x_l)
-        m_h, m_l = split(mid)
-        return dot3(m_h, m_l, wx_h[...], wx_l[...])
-
-    for start in range(0, wide, 3):
-        count = min(3, wide - start)
-        blurred = blur_yx(flat1, start, count, wy1_h, wy1_l)
-        for p in range(start, start + count):
-            own = blurred[(p - start) * pitch : (p - start) * pitch + rows, :]
-            rim = blurred[(p - start) * pitch + rows : (p - start) * pitch + used, :]
-            strip_rows = slice(EST_STRIP, EST_STRIP + DATA_STRIP)
-            if p < WIDTH:
-                top = slice(base + p * rows, base + (p + 1) * rows)
-                low = (planes - WIDTH + p) * thick + EST_STRIP
-                low = slice(low, low + DATA_STRIP)
-                top = jnp.where(odd, on[top, :], off[top, :])
-                low = jnp.where(odd, on[low, :], off[low, :])
-                inside = slab > 0
-            elif p < WIDTH + planes:
-                top, low = data[p - WIDTH], strip[p - WIDTH, strip_rows, :]
-                inside = None
-            else:
-                q = p - WIDTH - planes
-                top = slice(base + q * rows, base + (q + 1) * rows)
-                low = slice(q * thick + EST_STRIP, (q + 1) * thick)
-                top = jnp.where(odd, off[top, :], on[top, :])
-                low = jnp.where(odd, off[low, :], on[low, :])
-                inside = slab < slabs - 1
-            top, low = top / own, low / rim
-            if inside is not None:
-                top, low = jnp.where(inside, top, 0.0), jnp.where(inside, low, 0.0)
-            ratio[p, 0:rows, :] = top
-            ratio[p, rows:used, :] = low
+        blur_first(off, on)
+
+    reached = blur_yx(rims[...], wr_h[...], wr_l[...], wx_h, wx_l).reshape(wide, 16, lanes)
+
+    for p in range(wide):
+        near, far = reached[p, 0:8], reached[p, 8:16]
+        blurred = jnp.concatenate(
+            [
+                partial[p, 0:8, :] + jnp.where(row == 1, near, 0.0),
+                partial[p, 8 : rows - 8, :],
+                partial[p, rows - 8 : rows, :] + jnp.where(row == 0, near, 0.0),
+                partial[p, rows:used, :] + far,
+            ],
+            axis=0,
+        )
+        if WIDTH <= p < WIDTH + planes:
+            top, low = data[p - WIDTH], strip[p - WIDTH, EST_STRIP:thick, :]
+        else:
+            lower = p < WIDTH
+            first, second = (on, off) if lower else (off, on)
+            q = p if lower else p - WIDTH - planes
+            top = slice(base + q * rows, base + (q + 1) * rows)
+            low = (q + planes - WIDTH if lower else q) * thick + EST_STRIP
+            low = slice(low, low + DATA_STRIP)
+            top = jnp.where(odd, first[top, :], second[top, :])
+            low = jnp.where(odd, first[low, :], second[low, :])
+        value = jnp.concatenate([top, low], axis=0) / blurred
+        if p < WIDTH:
+            value = jnp.where(slab > 0, value, 0.0)
+        if p >= WIDTH + planes:
+            value = jnp.where(slab < slabs - 1, value, 0.0)
+        ratio[p] = value
 
     for p in range(planes):
-        for first in range(0, used, 8):
-            flat2[p * pitch + first : p * pitch + first + 8, :] = blur_z(
-                lambda t: ratio[p + t, first : first + 8, :], [taps_z[t, 0:8, :] for t in range(5)]
-            )
-        flat2[p * pitch + used : (p + 1) * pitch, :] = jnp.zeros((pitch - used, lanes), F32)
+        flat[p * pitch : p * pitch + used, :] = blur_z(lambda t: ratio[p + t], taps_z)
+        flat[p * pitch + used : (p + 1) * pitch, :] = jnp.zeros((pitch - used, lanes), F32)
     for start in range(0, planes, 3):
         count = min(3, planes - start)
-        back = blur_yx(flat2, start, count, wy2_h, wy2_l)
-        for p in range(start, start + count):
-            out[p] = back[(p - start) * pitch : (p - start) * pitch + used, :]
+        n = count * pitch
+        part = flat[start * pitch : start * pitch + n, :]
+        part = blur_yx(part, wy2_h[0:n, 0:n], wy2_l[0:n, 0:n], wx_h, wx_l)
+        out[start : start + count] = part.reshape(count, pitch, lanes)[:, :used]
 
 
 def field_kernel(views, rows, place, parts, est, strip, out):
@@ -218,7 +244,7 @@
             out[v] = value
 
 
-def variation_kernel(slabs, rows, place, field, on, off, out, start, first, second):
+def variation_kernel(slabs, rows, place, field, off, on, out, start, first, second):
     planes, used, lanes = field.shape
     slab, row = place[1], place[2]
     half = lanes // 2
@@ -327,6 +353,12 @@
     odd = lax.rem(slab, 2)
 
     first_row, is_odd = row == 0, odd == 1
+    low = data[:WIDTH].reshape(-1, lanes)
+    high = data[planes - WIDTH :].reshape(-1, lanes)
+    rim_off, rim_on = jnp.where(is_odd, high, low), jnp.where(is_odd, low, high)
+    estimate, data, rim_off, rim_on = lax.optimization_barrier(
+        (estimate, data, rim_off, rim_on)
+    )
     edge = jnp.concatenate(
         [
             jnp.where(first_row, estimate[:, rows - EST_STRIP :], estimate[:, :EST_STRIP]),
@@ -338,34 +370,41 @@
     held = lax.optimization_barrier((estimate, edge))[0]
     est_off = lax.ppermute(held, "slab", off_pairs)
     est_on = lax.ppermute(held, "slab", on_pairs)
-    low = data[:WIDTH].reshape(-1, lanes)
-    high = data[planes - WIDTH :].reshape(-1, lanes)
     flat = strip.reshape(-1, lanes)
-    off = jnp.concatenate([flat, jnp.where(is_odd, high, low)], axis=0)
-    on = jnp.concatenate([flat, jnp.where(is_odd, low, high)], axis=0)
+    off = jnp.concatenate([flat, rim_off], axis=0)
+    on = jnp.concatenate([flat, rim_on], axis=0)
     off = lax.ppermute(off, "slab", off_pairs)
     on = lax.ppermute(on, "slab", on_pairs)
 
     pitch, used = rows + EST_STRIP, rows + DATA_STRIP
-    matrices = call(
+    wide, group = planes + 2 * WIDTH, 256 // rows
+    taps_z, wx_h, wx_l, wo_h, wo_l, wr_h, wr_l, wy2_h, wy2_l = call(
         functools.partial(weights_kernel, rows),
         [shape((WIDTH + 1, 16, lanes))]
         + [half((lanes, lanes))] * 2
-        + [half((3 * pitch, 3 * pitch))] * 4,
+        + [half((group * used, group * rows))] * 2
+        + [half((wide * EST_STRIP, wide * EST_STRIP))] * 2
+        + [half((3 * pitch, 3 * pitch))] * 2,
         [],
         place, band, axes_perm, profile,
         scalars=4,
         cost=pl.CostEstimate(flops=COST, bytes_accessed=0, transcendentals=0),
     )
+    partial = call(
+        own_kernel,
+        shape((wide, used, lanes)),
+        [pltpu.VMEM((wide * rows, lanes), F32)],
+        place, estimate, est_off, est_on, taps_z, wx_h, wx_l, wo_h, wo_l,
+    )
     back = call(
         functools.partial(views_kernel, slabs),
         shape((planes, used, lanes)),
         [
-            pltpu.VMEM(((planes + 2 * WIDTH) * pitch, lanes), F32),
-            pltpu.VMEM((planes + 2 * WIDTH, used, lanes), F32),
+            pltpu.VMEM((wide * EST_STRIP, lanes), F32),
+            pltpu.VMEM((wide, used, lanes), F32),
             pltpu.VMEM((planes * pitch, lanes), F32),
         ],
-        place, estimate, data, strip, est_on, est_off, on, off, *matrices,
+        place, partial, data, strip, off, on, taps_z, wx_h, wx_l, wr_h, wr_l, wy2_h, wy2_l,
     )
     parts = lax.all_to_all(back, "view", 0, 0, tiled=True)
     copies = call(
@@ -384,7 +423,7 @@
         functools.partial(variation_kernel, slabs, rows),
         shape((planes, rows, lanes)),
         [deep, deep, deep],
-        place, field, on, off,
+        place, field, off, on,
     )
 
 

time: 71.9 us -> 68.5 us (0.953)
  waiting for transfers between devices: 4.66 us -> 2.18 us
  other arithmetic: 3.19 us -> 1.37 us
  Pallas kernels: 8.62 us -> 10.3 us
    ppermute x1, waiting for transfers between devices: 2.98 us -> 0.5 us  [body(): off = lax.ppermute(off, 'slab', off_pairs)]
    pallas_call x4 -> x5, Pallas kernels: 8.62 us -> 10.3 us  [call(): pl.pallas_call(kernel, out_shape=shapes, in_specs=specs, out_specs=jax.tr...]
    select_n x1, other arithmetic: 1 us -> 0.02 us  [body(): jnp.where(first_row, estimate[:, rows - EST_STRIP:], estimate[:, :EST_STR...]
    select_n x1, other arithmetic: 0.94 us -> 0.01 us  [body(): jnp.where(first_row, data[:, rows - DATA_STRIP:], data[:, :DATA_STRIP])]
    ppermute x1, starting transfers between devices: 6.48 us -> 7.24 us  [body(): off = lax.ppermute(jnp.where(is_odd, high, low), 'slab', off_pairs)]
  transfers between devices with their start and end apart: 7 -> 7, of which waited for: 2 -> 2; matrix products, arithmetic and copies ran while one was open for 2% -> 0% of each run, Pallas kernels for 1% -> 5%
where the time goes in v4:
time: 68.5 us; the launch traced here: 68.2 us
  starting transfers between devices  27.2 us (40%)
  blocking collectives  26.8 us (39%)
  Pallas kernels  10.3 us (15%)
  waiting for transfers between devices  2.18 us (3%)
  other arithmetic  1.37 us (2%)
    all_to_all x1, blocking collectives, body(): parts = lax.all_to_all(back, 'view', 0, 0, tiled=True)  14.3 us
    all_to_all x1, blocking collectives, body(): field = lax.all_to_all(copies, 'view', 0, 0, tiled=True)  12.4 us
    pallas_call x5, Pallas kernels, call(): pl.pallas_call(kernel, out_shape=shapes, in_specs=specs, out_specs=jax.tr...  10.3 us
    ppermute x1, starting transfers between devices, body(): off = lax.ppermute(jnp.where(is_odd, high, low), 'slab', off_pairs)  7.24 us
    ppermute x1, starting transfers between devices, body(): off = lax.ppermute(off, 'slab', off_pairs)  5.14 us
    ppermute x1, starting transfers between devices, body(): strip = lax.ppermute(edge, 'row', [(0, 1), (1, 0)])  4.65 us
    ppermute x1, starting transfers between devices, body(): est_off = lax.ppermute(held, 'slab', off_pairs)  4.39 us
    ppermute x1, starting transfers between devices, body(): on = lax.ppermute(jnp.where(is_odd, low, high), 'slab', on_pairs)  1.92 us
  transfers between devices with their start and end apart: 7, of which 2 were waited for; matrix products, arithmetic and copies ran while one was open for 0% of the time, Pallas kernels for 5%

profile of v4, /device:TPU:193, one launch (start us, length us, event | category | flops | bytes accessed | tf_op | source)
XLA Modules:
  0.0 68.2 jit_solution(15077277879697553431)
XLA Ops:
  0.0 1.2 %slice_select_fusion = (f32[1,4,64,256]{3,2,1,0:T(8,128)S(1)}, f32[1,4,64,256]{3,2,1,0:T(8,128)S(1)}) fusion(f32[1,8,64,256]{3,2,1,0:T(8,128)} %param.5, pred[]{:T(512)S(6)} %eq.6), kind=kLoop, calls=%fused_computation.2 | loop fusion | flops 131072 | bytes 1048577 | tf_op jit(solution)/shard_map/jit(_where)/select_n | solution.py:358
  1.2 0.1 copy-done
  1.3 0.1 copy-done.1
  1.4 4.7 %collective-permute-start.2 = (f32[8,24,256]{2,1,0:T(8,128)S(1)}, f32[8,24,256]{2,1,0:T(8,128)S(1)}, u32[]{:S(2)}, u32[]{:S(2)}) collective-permute-start(f32[8,24,256]{2,1,0:T(8,128)S(1)} %pad_maximum_fusion.2), channel_id=1, source_target_pairs={{0,1},{1,0},{2,3},{3,2},{4,5},{5,4},{6,7},{7,6},{8,9},{9,8},{10,11... | collective-permute-start | bytes 589832 | tf_op jit(solution)/shard_map/ppermute | solution.py:369
  6.1 4.4 %collective-permute-start = (f32[8,64,256]{2,1,0:T(8,128)S(1)}, f32[8,64,256]{2,1,0:T(8,128)S(1)}, u32[]{:S(2)}, u32[]{:S(2)}) collective-permute-start(f32[8,64,256]{2,1,0:T(8,128)S(1)} %copy-done), channel_id=1, source_target_pairs={{2,4},{6,8},{10,12},{14,16},{18,20},{22,24},{26,28},{30,32},{34,36... | collective-permute-start | bytes 1572872 | tf_op jit(solution)/shard_map/ppermute | solution.py:371
  10.5 1.9 %collective-permute-start.1 = (f32[8,64,256]{2,1,0:T(8,128)S(1)}, f32[8,64,256]{2,1,0:T(8,128)S(1)}, u32[]{:S(2)}, u32[]{:S(2)}) collective-permute-start(f32[8,64,256]{2,1,0:T(8,128)S(1)} %copy-done), channel_id=1, source_target_pairs={{0,2},{2,0},{4,6},{6,4},{8,10},{10,8},{12,14},{14,12},{16,18},{18,... | collective-permute-start | bytes 1572872 | tf_op jit(solution)/shard_map/ppermute | solution.py:372
  12.4 0.1 pad_add_fusion.place
  12.5 0.0 collective-permute-done.2.strip
  12.5 0.1 pad_maximum_fusion
  12.6 5.1 %collective-permute-start.3 = (f32[448,256]{1,0:T(8,128)S(1)}, f32[448,256]{1,0:T(8,128)S(1)}, u32[]{:S(2)}, u32[]{:S(2)}) collective-permute-start(f32[448,256]{1,0:T(8,128)S(1)} %get-tuple-element.38), channel_id=1, source_target_pairs={{2,4},{6,8},{10,12},{14,16},{18,20},{22,24},{26,28},{30,32},{34,36... | collective-permute-start | bytes 1376264 | tf_op jit(solution)/shard_map/ppermute | solution.py:376
  17.7 1.9 %collective-permute-start.4 = (f32[448,256]{1,0:T(8,128)S(1)}, f32[448,256]{1,0:T(8,128)S(1)}, u32[]{:S(2)}, u32[]{:S(2)}) collective-permute-start(f32[448,256]{1,0:T(8,128)S(1)} %get-tuple-element.37), channel_id=1, source_target_pairs={{0,2},{2,0},{4,6},{6,4},{8,10},{10,8},{12,14},{14,12},{16,18},{18,... | collective-permute-start | bytes 1376264 | tf_op jit(solution)/shard_map/ppermute | solution.py:377
  19.7 1.3 %shard_map.55 = (f32[5,16,256]{2,1,0:T(8,128)S(1)}, bf16[256,256]{1,0:T(8,128)(2,1)S(1)}, bf16[256,256]{1,0:T(8,128)(2,1)S(1)}, bf16[288,256]{1,0:T(8,128)(2,1)S...) custom-call(s32[3]{0:T(128)S(1)} %pad_add_fusion.place, ...), custom_call_target="tpu_custom_call" | custom-call | flops 20000000000 | tf_op jit(solution)/shard_map/pallas_call | solution.py:331
  20.9 0.0 collective-permute-done.est_off
  20.9 0.0 collective-permute-done.1.est_on
  21.0 2.4 %shard_map.56.partial = f32[16,72,256]{2,1,0:T(8,128)S(1)} custom-call(s32[3]{0:T(128)S(1)} %pad_add_fusion.place, f32[8,64,256]{2,1,0:T(8,128)S(1)} %copy-done, f32[8,64,256]{2,1,0:T(8,128)S(1)} %collective-permute-done.est_off, f32[8,64,256]{2,1,0:T(8,128)S(1)} %collective-permute-done.1.est_on, f32[5,16,256]{2,1,0:T(8,128)S(1)} %get-tuple-element.22.taps_z, ...), custom_call_target="tpu_custom_call" | custom-call | tf_op jit(solution)/shard_map/pallas_call | solution.py:331
  23.4 0.5 collective-permute-done.3.off
  23.9 2.4 %shard_map.57 = f32[8,72,256]{2,1,0:T(8,128)S(1)} custom-call(s32[3]{0:T(128)S(1)} %pad_add_fusion.place, f32[16,72,256]{2,1,0:T(8,128)S(1)} %shard_map.56.partial, f32[8,64,256]{2,1,0:T(8,128)S(1)} %bitcast.8, f32[8,24,256]{2,1,0:T(8,128)S(1)} %collective-permute-done.2.strip, f32[448,256]{1,0:T(8,128)S(1)} %collective-permute-done.3.off, ...), custom_call_target="tpu_custom_call" | custom-call | tf_op jit(solution)/shard_map/pallas_call | solution.py:331
  26.3 14.3 %all_to_all.10.parts = f32[8,72,256]{2,1,0:T(8,128)S(1)} all-to-all(f32[8,72,256]{2,1,0:T(8,128)S(1)} %shard_map.57), channel_id=1, replica_groups=mesh['view'=8,'slab'=32,'row'=2] {'view'}, dimensions={0} | all-to-all | bytes 1179648 | tf_op jit(solution)/shard_map/all_to_all | solution.py:409
  40.6 0.6 shard_map.58
  41.2 12.4 %all_to_all.11.field = f32[8,72,256]{2,1,0:T(8,128)S(1)} all-to-all(f32[8,72,256]{2,1,0:T(8,128)S(1)} %shard_map.58), channel_id=1, replica_groups=mesh['view'=8,'slab'=32,'row'=2] {'view'}, dimensions={0} | all-to-all | bytes 1179648 | tf_op jit(solution)/shard_map/all_to_all | solution.py:416
  53.7 7.2 %collective-permute-start.5 = (f32[3,72,256]{2,1,0:T(8,128)S(1)}, f32[3,72,256]{2,1,0:T(8,128)S(1)}, u32[]{:S(2)}, u32[]{:S(2)}) collective-permute-start(f32[3,72,256]{2,1,0:T(8,128)S(1)} %get-tuple-element.34), channel_id=1, source_target_pairs={{2,4},{6,8},{10,12},{14,16},{18,20},{22,24},{26,28},{30,32},{34,36... | collective-permute-start | bytes 663560 | tf_op jit(solution)/shard_map/ppermute | solution.py:419
  60.9 1.9 %collective-permute-start.6 = (f32[3,72,256]{2,1,0:T(8,128)S(1)}, f32[3,72,256]{2,1,0:T(8,128)S(1)}, u32[]{:S(2)}, u32[]{:S(2)}) collective-permute-start(f32[3,72,256]{2,1,0:T(8,128)S(1)} %get-tuple-element.33), channel_id=1, source_target_pairs={{0,2},{2,0},{4,6},{6,4},{8,10},{10,8},{12,14},{14,12},{16,18},{18,... | collective-permute-start | bytes 663560 | tf_op jit(solution)/shard_map/ppermute | solution.py:420
  62.9 1.7 %collective-permute-done.5.off = f32[3,72,256]{2,1,0:T(8,128)S(1)} collective-permute-done((f32[3,72,256]{2,1,0:T(8,128)S(1)}, f32[3,72,256]{2,1,0:T(8,128)S(1)}, u32[]{:S(2)}, u32[]{:S(2)}) %collective-permute-start.5) | collective-permute-done | bytes 221216 | tf_op jit(solution)/shard_map/ppermute | solution.py:419
  64.5 3.6 %shard_map.59 = f32[8,64,256]{2,1,0:T(8,128)} custom-call(s32[3]{0:T(128)S(1)} %pad_add_fusion.place, f32[8,72,256]{2,1,0:T(8,128)S(1)} %all_to_all.11.field, f32[3,72,256]{2,1,0:T(8,128)S(1)} %collective-permute-done.5.off, f32[3,72,256]{2,1,0:T(8,128)S(1)} %collective-permute-done.6.on), custom_call_target="tpu_custom_call" | custom-call | tf_op jit(solution)/shard_map/pallas_call | solution.py:331
  (15 shorter events, 0.1 us)
Async XLA Ops:
  0.0 1.4 %copy-start.1 = (f32[1,8,64,256]{3,2,1,0:T(8,128)S(1)}, f32[1,8,64,256]{3,2,1,0:T(8,128)}, u32[]{:S(2)}) copy-start(f32[1,8,64,256]{3,2,1,0:T(8,128)} %param.5) | copy-start | bytes 1572868
  0.0 1.3 %copy-start = (f32[8,64,256]{2,1,0:T(8,128)S(1)}, f32[8,64,256]{2,1,0:T(8,128)}, u32[]{:S(2)}) copy-start(f32[8,64,256]{2,1,0:T(8,128)} %est.1) | copy-start | bytes 1572868
  0.0 12.4 %copy-start.4 = (f32[1,3,5]{2,0,1:T(1,128)S(1)}, f32[1,3,5]{2,0,1:T(1,128)}, u32[]{:S(2)}) copy-start(f32[1,3,5]{2,0,1:T(1,128)} %param.7) | copy-start | bytes 184
  1.4 18.3 %copy-start.2 = (s32[1,3]{1,0:T(1,128)S(1)}, s32[1,3]{1,0:T(1,128)}, u32[]{:S(2)}) copy-start(s32[1,3]{1,0:T(1,128)} %band.1) | copy-start | bytes 40
  1.4 18.3 %copy-start.3 = (s32[1,3]{1,0:T(1,128)S(1)}, s32[1,3]{1,0:T(1,128)}, u32[]{:S(2)}) copy-start(s32[1,3]{1,0:T(1,128)} %perm.1) | copy-start | bytes 40
  1.4 11.1 %collective-permute-start.2 = (f32[8,24,256]{2,1,0:T(8,128)S(1)}, f32[8,24,256]{2,1,0:T(8,128)S(1)}, u32[]{:S(2)}, u32[]{:S(2)}) collective-permute-start(f32[8,24,256]{2,1,0:T(8,128)S(1)} %pad_maximum_fusion.2), channel_id=1, source_target_pairs={{0,1},{1,0},{2,3},{3,2},{4,5},{5,4},{6,7},{7,6},{8,9},{9,8},{10,11... | collective-permute-start | bytes 589832 | tf_op jit(solution)/shard_map/ppermute | solution.py:369
  6.1 14.9 %collective-permute-start = (f32[8,64,256]{2,1,0:T(8,128)S(1)}, f32[8,64,256]{2,1,0:T(8,128)S(1)}, u32[]{:S(2)}, u32[]{:S(2)}) collective-permute-start(f32[8,64,256]{2,1,0:T(8,128)S(1)} %copy-done), channel_id=1, source_target_pairs={{2,4},{6,8},{10,12},{14,16},{18,20},{22,24},{26,28},{30,32},{34,36... | collective-permute-start | bytes 1572872 | tf_op jit(solution)/shard_map/ppermute | solution.py:371
  10.5 10.5 %collective-permute-start.1 = (f32[8,64,256]{2,1,0:T(8,128)S(1)}, f32[8,64,256]{2,1,0:T(8,128)S(1)}, u32[]{:S(2)}, u32[]{:S(2)}) collective-permute-start(f32[8,64,256]{2,1,0:T(8,128)S(1)} %copy-done), channel_id=1, source_target_pairs={{0,2},{2,0},{4,6},{6,4},{8,10},{10,8},{12,14},{14,12},{16,18},{18,... | collective-permute-start | bytes 1572872 | tf_op jit(solution)/shard_map/ppermute | solution.py:372
  12.6 11.3 %collective-permute-start.3 = (f32[448,256]{1,0:T(8,128)S(1)}, f32[448,256]{1,0:T(8,128)S(1)}, u32[]{:S(2)}, u32[]{:S(2)}) collective-permute-start(f32[448,256]{1,0:T(8,128)S(1)} %get-tuple-element.38), channel_id=1, source_target_pairs={{2,4},{6,8},{10,12},{14,16},{18,20},{22,24},{26,28},{30,32},{34,36... | collective-permute-start | bytes 1376264 | tf_op jit(solution)/shard_map/ppermute | solution.py:376
  17.7 6.2 %collective-permute-start.4 = (f32[448,256]{1,0:T(8,128)S(1)}, f32[448,256]{1,0:T(8,128)S(1)}, u32[]{:S(2)}, u32[]{:S(2)}) collective-permute-start(f32[448,256]{1,0:T(8,128)S(1)} %get-tuple-element.37), channel_id=1, source_target_pairs={{0,2},{2,0},{4,6},{6,4},{8,10},{10,8},{12,14},{14,12},{16,18},{18,... | collective-permute-start | bytes 1376264 | tf_op jit(solution)/shard_map/ppermute | solution.py:377
  53.7 10.9 %collective-permute-start.5 = (f32[3,72,256]{2,1,0:T(8,128)S(1)}, f32[3,72,256]{2,1,0:T(8,128)S(1)}, u32[]{:S(2)}, u32[]{:S(2)}) collective-permute-start(f32[3,72,256]{2,1,0:T(8,128)S(1)} %get-tuple-element.34), channel_id=1, source_target_pairs={{2,4},{6,8},{10,12},{14,16},{18,20},{22,24},{26,28},{30,32},{34,36... | collective-permute-start | bytes 663560 | tf_op jit(solution)/shard_map/ppermute | solution.py:419
  60.9 3.6 %collective-permute-start.6 = (f32[3,72,256]{2,1,0:T(8,128)S(1)}, f32[3,72,256]{2,1,0:T(8,128)S(1)}, u32[]{:S(2)}, u32[]{:S(2)}) collective-permute-start(f32[3,72,256]{2,1,0:T(8,128)S(1)} %get-tuple-element.33), channel_id=1, source_target_pairs={{0,2},{2,0},{4,6},{6,4},{8,10},{10,8},{12,14},{14,12},{16,18},{18,... | collective-permute-start | bytes 663560 | tf_op jit(solution)/shard_map/ppermute | solution.py:420

commit v5 on v4

--- a/solution.py
+++ b/solution.py
@@ -31,8 +31,8 @@
     return dot(a_high, b_high) + (dot(a_low, b_high) + dot(a_high, b_low))
 
 
-def weights_kernel(rows, place, band, perm, prof, taps_z, wx_h, wx_l, wo_h, wo_l, wr_h, wr_l, wy2_h, wy2_l):
-    row = place[2]
+def weights_kernel(rows, band, perm, prof, taps_z, wx_h, wx_l, wo_h, wo_l, wr_h, wr_l, wy2_h, wy2_l):
+    row = lax.axis_index("row")
     pitch = wy2_h.shape[0] // 3
     used = rows + DATA_STRIP
 
@@ -45,64 +45,61 @@
             total = total + 2.0 * part
         return [jnp.full(shape, part, F32) / jnp.full(shape, total, F32) for part in parts]
 
-    def banded(axis, shape, distance, keep, high, low):
-        small = (8, shape[1])
+    def banded(axis, shape, row_place, column_place, high, low):
+        pieces = taps(axis, (8, shape[1]))
+        column = column_place(lax.broadcasted_iota(jnp.int32, (8, shape[1]), 1))
         for start in range(0, shape[0], 16):
-            pieces = []
-            for t, tap in enumerate(taps(axis, small)):
-                pieces.append(jnp.concatenate([tap, tap], axis=0))
-            i = start + lax.broadcasted_iota(jnp.int32, (16, shape[1]), 0)
-            j = lax.broadcasted_iota(jnp.int32, (16, shape[1]), 1)
-            d = jnp.abs(distance(i, j))
-            value = jnp.zeros((16, shape[1]), F32)
-            for t in range(WIDTH + 1):
-                value = jnp.where((d == t) & keep(i, j), pieces[t], value)
-            high[start : start + 16, :], low[start : start + 16, :] = split(value)
+            parts = []
+            for first in (start, start + 8):
+                line = row_place(first + lax.broadcasted_iota(jnp.int32, (8, 128), 0))
+                line = jnp.concatenate([line] * 2, axis=1)[:, : shape[1]]
+                d = jnp.abs(line - column)
+                value = jnp.where(d == 0, pieces[0], 0.0)
+                for t in range(1, WIDTH + 1):
+                    value = jnp.where(d == t, pieces[t], value)
+                parts.append(split(value))
+            high[start : start + 16, :] = jnp.concatenate([p[0] for p in parts], axis=0)
+            low[start : start + 16, :] = jnp.concatenate([p[1] for p in parts], axis=0)
 
     for t, tap in enumerate(taps(0, taps_z.shape[1:])):
         taps_z[t] = tap
-    banded(2, wx_h.shape, lambda i, j: i - j, lambda i, j: (i >= 0), wx_h, wx_l)
+    banded(2, wx_h.shape, lambda i: i, lambda j: j, wx_h, wx_l)
 
     most = wo_h.shape[0]
 
-    def plane_of(i, height):
-        return sum((i >= n * height).astype(jnp.int32) for n in range(1, most // height))
-
-    def within(i, height):
-        return i - height * plane_of(i, height)
+    def placed(i, height, place_within):
+        plane = sum((i >= n * height).astype(jnp.int32) for n in range(1, most // height))
+        return plane * 4096 + place_within(i - height * plane)
 
     def halo_place(i, strip):
         return jnp.where((i >= rows) & (row == 1), i - rows - strip, i)
 
     def reached(i):
         return jnp.where(i < 8, i + (rows - 8) * (1 - row), halo_place(i - 8 + rows, DATA_STRIP))
-
-    def ascending(i):
-        return within(i, pitch) - DATA_STRIP * row
 
     banded(
         1,
         wo_h.shape,
-        lambda i, j: halo_place(within(i, used), DATA_STRIP) - within(j, rows),
-        lambda i, j: plane_of(i, used) == plane_of(j, rows),
+        lambda i: placed(i, used, lambda k: halo_place(k, DATA_STRIP)),
+        lambda j: placed(j, rows, lambda k: k),
         wo_h,
         wo_l,
     )
     banded(
         1,
         wr_h.shape,
-        lambda i, j: reached(within(i, 16)) - halo_place(within(j, 16) + rows, EST_STRIP),
-        lambda i, j: plane_of(i, 16) == plane_of(j, 16),
+        lambda i: placed(i, EST_STRIP, reached),
+        lambda j: placed(j, EST_STRIP, lambda k: halo_place(k + rows, EST_STRIP)),
         wr_h,
         wr_l,
     )
     banded(
         1,
         wy2_h.shape,
-        lambda i, j: ascending(i) - halo_place(within(j, pitch), DATA_STRIP),
-        lambda i, j: (plane_of(i, pitch) == plane_of(j, pitch))
-        & (within(i, pitch) < used)
-        & (within(j, pitch) < used),
+        lambda i: placed(i, pitch, lambda k: jnp.where(k < used, k - DATA_STRIP * row, 1024)),
+        lambda j: placed(
+            j, pitch, lambda k: jnp.where(k < used, halo_place(k, DATA_STRIP), 2048)
+        ),
         wy2_h,
         wy2_l,
     )
@@ -122,38 +119,42 @@
     return dot3(m_h, m_l, wx_h[...], wx_l[...])
 
 
-def own_kernel(place, est, est_off, est_on, taps_z, wx_h, wx_l, wo_h, wo_l, out, flat):
+def own_kernel(est, data, est_off, est_on, taps_z, wx_h, wx_l, wo_h, wo_l, out, ratio):
     planes, rows, lanes = est.shape
     wide, used, _ = out.shape
-    odd = lax.rem(place[1], 2) == 1
+    odd = lax.rem(lax.axis_index("slab"), 2) == 1
     group = 256 // rows
 
-    def blur_first(below, above):
-        for p in range(wide):
-            flat[p * rows : (p + 1) * rows, :] = blur_z(
-                lambda t: (below, est, above)[(p + t) // planes][(p + t) % planes], taps_z
-            )
+    def work(below, above):
+        mids = []
+        for start in range(0, wide, group):
+            part = [
+                blur_z(lambda t: (below, est, above)[(p + t) // planes][(p + t) % planes], taps_z)
+                for p in range(start, start + group)
+            ]
+            x_h, x_l = split(jnp.concatenate(part, axis=0))
+            mids.append(split(dot3(wo_h[...], wo_l[...], x_h, x_l)))
+        m_h = jnp.concatenate([m[0] for m in mids], axis=0)
+        m_l = jnp.concatenate([m[1] for m in mids], axis=0)
+        blurred = dot3(m_h, m_l, wx_h[...], wx_l[...]).reshape(wide, used, lanes)
+        out[...] = blurred
+        ratio[...] = data[:, 8 : rows - 8, :] / blurred[WIDTH : WIDTH + planes, 8 : rows - 8]
 
     @pl.when(odd)
     def _():
-        blur_first(est_on, est_off)
+        work(est_on, est_off)
 
     @pl.when(jnp.logical_not(odd))
     def _():
-        blur_first(est_off, est_on)
-
-    for p in range(0, wide, group):
-        part = flat[p * rows : (p + group) * rows, :]
-        part = blur_yx(part, wo_h[...], wo_l[...], wx_h, wx_l)
-        out[p : p + group] = part.reshape(group, used, lanes)
+        work(est_off, est_on)
 
 
 def views_kernel(
-    slabs, place, partial, data, strip, off, on,
+    slabs, partial, inner, data, strip, off, on,
     taps_z, wx_h, wx_l, wr_h, wr_l, wy2_h, wy2_l, out, rims, ratio, flat,
 ):
     planes, rows, lanes = data.shape
-    slab, row = place[1], place[2]
+    slab, row = lax.axis_index("slab"), lax.axis_index("row")
     pitch = rows + EST_STRIP
     used = rows + DATA_STRIP
     wide = planes + 2 * WIDTH
@@ -179,50 +180,59 @@
     def _():
         blur_first(off, on)
 
+    mids = []
     reached = blur_yx(rims[...], wr_h[...], wr_l[...], wx_h, wx_l).reshape(wide, 16, lanes)
 
-    for p in range(wide):
-        near, far = reached[p, 0:8], reached[p, 8:16]
-        blurred = jnp.concatenate(
-            [
-                partial[p, 0:8, :] + jnp.where(row == 1, near, 0.0),
-                partial[p, 8 : rows - 8, :],
-                partial[p, rows - 8 : rows, :] + jnp.where(row == 0, near, 0.0),
-                partial[p, rows:used, :] + far,
-            ],
-            axis=0,
+    def touched(low, high):
+        near = reached[low:high, 0:8]
+        return (
+            partial[low:high, 0:8, :] + jnp.where(row == 1, near, 0.0),
+            partial[low:high, rows - 8 : rows, :] + jnp.where(row == 0, near, 0.0),
+            partial[low:high, rows:used, :] + reached[low:high, 8:16],
         )
-        if WIDTH <= p < WIDTH + planes:
-            top, low = data[p - WIDTH], strip[p - WIDTH, EST_STRIP:thick, :]
-        else:
-            lower = p < WIDTH
-            first, second = (on, off) if lower else (off, on)
-            q = p if lower else p - WIDTH - planes
+
+    def beyond(lower):
+        first, second = (on, off) if lower else (off, on)
+        low = 0 if lower else WIDTH + planes
+        start, end, last = touched(low, low + WIDTH)
+        blurred = jnp.concatenate([start, partial[low : low + WIDTH, 8 : rows - 8, :], end, last], axis=1)
+        tops, lows = [], []
+        for q in range(WIDTH):
             top = slice(base + q * rows, base + (q + 1) * rows)
-            low = (q + planes - WIDTH if lower else q) * thick + EST_STRIP
-            low = slice(low, low + DATA_STRIP)
-            top = jnp.where(odd, first[top, :], second[top, :])
-            low = jnp.where(odd, first[low, :], second[low, :])
-        value = jnp.concatenate([top, low], axis=0) / blurred
-        if p < WIDTH:
-            value = jnp.where(slab > 0, value, 0.0)
-        if p >= WIDTH + planes:
-            value = jnp.where(slab < slabs - 1, value, 0.0)
-        ratio[p] = value
-
-    for p in range(planes):
-        flat[p * pitch : p * pitch + used, :] = blur_z(lambda t: ratio[p + t], taps_z)
-        flat[p * pitch + used : (p + 1) * pitch, :] = jnp.zeros((pitch - used, lanes), F32)
-    for start in range(0, planes, 3):
-        count = min(3, planes - start)
-        n = count * pitch
-        part = flat[start * pitch : start * pitch + n, :]
-        part = blur_yx(part, wy2_h[0:n, 0:n], wy2_l[0:n, 0:n], wx_h, wx_l)
-        out[start : start + count] = part.reshape(count, pitch, lanes)[:, :used]
-
-
-def field_kernel(views, rows, place, parts, est, strip, out):
-    view, row = place[0], place[2]
+            at = (q + planes - WIDTH if lower else q) * thick + EST_STRIP
+            at = slice(at, at + DATA_STRIP)
+            tops.append(jnp.where(odd, first[top, :], second[top, :])[None])
+            lows.append(jnp.where(odd, first[at, :], second[at, :])[None])
+        value = [jnp.concatenate(tops, axis=0), jnp.concatenate(lows, axis=0)]
+        value = jnp.concatenate(value, axis=1) / blurred
+        inside = slab > 0 if lower else slab < slabs - 1
+        ratio[low : low + WIDTH] = jnp.where(inside, value, 0.0)
+
+    def second_blur(low, high):
+        for p in range(low, high):
+            flat[p * pitch : p * pitch + used, :] = blur_z(lambda t: ratio[p + t], taps_z)
+            flat[p * pitch + used : (p + 1) * pitch, :] = jnp.zeros((pitch - used, lanes), F32)
+        n = (high - low) * pitch
+        x_h, x_l = split(flat[low * pitch : low * pitch + n, :])
+        return split(dot3(wy2_h[0:n, 0:n], wy2_l[0:n, 0:n], x_h, x_l))
+
+    beyond(True)
+    ends = [data[:, 0:8, :], data[:, rows - 8 : rows, :], strip[:, EST_STRIP:thick, :]]
+    ends = jnp.concatenate(ends, axis=1) / jnp.concatenate(touched(WIDTH, WIDTH + planes), axis=1)
+    own = slice(WIDTH, WIDTH + planes)
+    ratio[own, 0:8, :] = ends[:, 0:8]
+    ratio[own, 8 : rows - 8, :] = inner[...]
+    ratio[own, rows - 8 : used, :] = ends[:, 8:24]
+    mids = [second_blur(0, 2), second_blur(2, 4)]
+    beyond(False)
+    mids += [second_blur(4, 6), second_blur(6, 8)]
+    m_h = jnp.concatenate([m[0] for m in mids], axis=0)
+    m_l = jnp.concatenate([m[1] for m in mids], axis=0)
+    out[...] = dot3(m_h, m_l, wx_h[...], wx_l[...]).reshape(planes, pitch, lanes)[:, :used]
+
+
+def field_kernel(views, rows, parts, est, strip, out):
+    view, row = lax.axis_index("view"), lax.axis_index("row")
     total = parts[0]
     for v in range(1, views):
         total = total + parts[v]
@@ -244,9 +254,9 @@
             out[v] = value
 
 
-def variation_kernel(slabs, rows, place, field, off, on, out, start, first, second):
+def variation_kernel(slabs, rows, field, off, on, out, start, first, second):
     planes, used, lanes = field.shape
-    slab, row = place[1], place[2]
+    slab, row = lax.axis_index("slab"), lax.axis_index("row")
     half = lanes // 2
     odd = lax.rem(slab, 2)
     start[pl.ds(odd * (planes + TV_HALO), TV_HALO)] = off[...]
@@ -326,7 +336,7 @@
     out[...] = first[TV_HALO : TV_HALO + planes, pl.ds(skip, rows), :]
 
 
-def call(kernel, shapes, scratch, *args, cost=None, scalars=1):
+def call(kernel, shapes, scratch, *args, cost=None, scalars=0):
     specs = [SMEM if i < scalars else VMEM for i in range(len(args))]
     return pl.pallas_call(
         kernel,
@@ -343,8 +353,7 @@
     data = data[0]
     planes, rows, lanes = estimate.shape
     views, slabs = lax.axis_size("view"), lax.axis_size("slab")
-    view, slab, row = lax.axis_index("view"), lax.axis_index("slab"), lax.axis_index("row")
-    place = jnp.stack([view, slab, row]).astype(jnp.int32)
+    slab, row = lax.axis_index("slab"), lax.axis_index("row")
     shape = functools.partial(jax.ShapeDtypeStruct, dtype=F32)
     half = functools.partial(jax.ShapeDtypeStruct, dtype=BF16)
     off_pairs = [(i, i + 1) for i in range(1, slabs - 1, 2)]
@@ -386,15 +395,15 @@
         + [half((wide * EST_STRIP, wide * EST_STRIP))] * 2
         + [half((3 * pitch, 3 * pitch))] * 2,
         [],
-        place, band, axes_perm, profile,
-        scalars=4,
+        band, axes_perm, profile,
+        scalars=3,
         cost=pl.CostEstimate(flops=COST, bytes_accessed=0, transcendentals=0),
     )
-    partial = call(
+    partial, inner = call(
         own_kernel,
-        shape((wide, used, lanes)),
-        [pltpu.VMEM((wide * rows, lanes), F32)],
-        place, estimate, est_off, est_on, taps_z, wx_h, wx_l, wo_h, wo_l,
+        [shape((wide, used, lanes)), shape((planes, rows - 16, lanes))],
+        [],
+        estimate, data, est_off, est_on, taps_z, wx_h, wx_l, wo_h, wo_l,
     )
     back = call(
         functools.partial(views_kernel, slabs),
@@ -404,14 +413,14 @@
             pltpu.VMEM((wide, used, lanes), F32),
             pltpu.VMEM((planes * pitch, lanes), F32),
         ],
-        place, partial, data, strip, off, on, taps_z, wx_h, wx_l, wr_h, wr_l, wy2_h, wy2_l,
+        partial, inner, data, strip, off, on, taps_z, wx_h, wx_l, wr_h, wr_l, wy2_h, wy2_l,
     )
     parts = lax.all_to_all(back, "view", 0, 0, tiled=True)
     copies = call(
         functools.partial(field_kernel, views, rows),
         shape((views, used, lanes)),
         [],
-        place, parts, estimate, strip,
+        parts, estimate, strip,
     )
     field = lax.all_to_all(copies, "view", 0, 0, tiled=True)
     reach = planes - TV_HALO
@@ -423,7 +432,7 @@
         functools.partial(variation_kernel, slabs, rows),
         shape((planes, rows, lanes)),
         [deep, deep, deep],
-        place, field, off, on,
+        field, off, on,
     )
 
 

time: 68.5 us -> 66.7 us (0.974)
  Pallas kernels: 10.3 us -> 7.73 us
  blocking collectives: 26.8 us -> 28.1 us
  starting transfers between devices: 27.2 us -> 25.9 us
  waiting for transfers between devices: 2.18 us -> 2.99 us
    pallas_call x5, Pallas kernels: 10.3 us -> 7.73 us  [call(): pl.pallas_call(kernel, out_shape=shapes, in_specs=specs, out_specs=jax.tr...]
    ppermute x1, starting transfers between devices: 7.24 us -> 5.93 us  [body(): off = lax.ppermute(jnp.where(is_odd, high, low), 'slab', off_pairs)]
    all_to_all x1, blocking collectives: 14.3 us -> 15.4 us  [body(): parts = lax.all_to_all(back, 'view', 0, 0, tiled=True)]
    ppermute x1, waiting for transfers between devices: 0.5 us -> 1.3 us  [body(): off = lax.ppermute(off, 'slab', off_pairs)]
  transfers between devices with their start and end apart: 7 -> 7, of which waited for: 2 -> 2; matrix products, arithmetic and copies ran while one was open for 0% -> 0% of each run, Pallas kernels for 5% -> 4%
where the time goes in v5:
time: 66.7 us; the launch traced here: 66.3 us
  blocking collectives  28.1 us (42%)
  starting transfers between devices  25.9 us (39%)
  Pallas kernels  7.73 us (12%)
  waiting for transfers between devices  2.99 us (4%)
  other arithmetic  1.29 us (2%)
    all_to_all x1, blocking collectives, body(): parts = lax.all_to_all(back, 'view', 0, 0, tiled=True)  15.4 us
    all_to_all x1, blocking collectives, body(): field = lax.all_to_all(copies, 'view', 0, 0, tiled=True)  12.7 us
    pallas_call x5, Pallas kernels, call(): pl.pallas_call(kernel, out_shape=shapes, in_specs=specs, out_specs=jax.tr...  7.73 us
    ppermute x1, starting transfers between devices, body(): off = lax.ppermute(jnp.where(is_odd, high, low), 'slab', off_pairs)  5.93 us
    ppermute x1, starting transfers between devices, body(): off = lax.ppermute(off, 'slab', off_pairs)  5.14 us
    ppermute x1, starting transfers between devices, body(): strip = lax.ppermute(edge, 'row', [(0, 1), (1, 0)])  4.65 us
    ppermute x1, starting transfers between devices, body(): est_off = lax.ppermute(held, 'slab', off_pairs)  4.39 us
    ppermute x1, starting transfers between devices, body(): on = lax.ppermute(jnp.where(is_odd, low, high), 'slab', on_pairs)  1.92 us
  transfers between devices with their start and end apart: 7, of which 2 were waited for; matrix products, arithmetic and copies ran while one was open for 0% of the time, Pallas kernels for 4%

profile of v5, /device:TPU:193, one launch (start us, length us, event | category | flops | bytes accessed | tf_op | source)
XLA Modules:
  0.0 66.3 jit_solution(15805225739286376761)
XLA Ops:
  0.0 1.2 %slice_select_fusion = (f32[1,4,64,256]{3,2,1,0:T(8,128)S(1)}, f32[1,4,64,256]{3,2,1,0:T(8,128)S(1)}) fusion(f32[1,8,64,256]{3,2,1,0:T(8,128)} %param.5, pred[]{:T(512)S(6)} %eq.6), kind=kLoop, calls=%fused_computation.2 | loop fusion | flops 131072 | bytes 1048577 | tf_op jit(solution)/shard_map/jit(_where)/select_n | solution.py:367
  1.2 0.1 copy-done.1
  1.3 0.1 copy-done
  1.4 4.7 %collective-permute-start.2 = (f32[8,24,256]{2,1,0:T(8,128)S(1)}, f32[8,24,256]{2,1,0:T(8,128)S(1)}, u32[]{:S(2)}, u32[]{:S(2)}) collective-permute-start(f32[8,24,256]{2,1,0:T(8,128)S(1)} %pad_maximum_fusion.2), channel_id=1, source_target_pairs={{0,1},{1,0},{2,3},{3,2},{4,5},{5,4},{6,7},{7,6},{8,9},{9,8},{10,11... | collective-permute-start | bytes 589832 | tf_op jit(solution)/shard_map/ppermute | solution.py:378
  6.1 4.4 %collective-permute-start = (f32[8,64,256]{2,1,0:T(8,128)S(1)}, f32[8,64,256]{2,1,0:T(8,128)S(1)}, u32[]{:S(2)}, u32[]{:S(2)}) collective-permute-start(f32[8,64,256]{2,1,0:T(8,128)S(1)} %copy-done.1), channel_id=1, source_target_pairs={{2,4},{6,8},{10,12},{14,16},{18,20},{22,24},{26,28},{30,32},{34,36... | collective-permute-start | bytes 1572872 | tf_op jit(solution)/shard_map/ppermute | solution.py:380
  10.5 1.9 %collective-permute-start.1 = (f32[8,64,256]{2,1,0:T(8,128)S(1)}, f32[8,64,256]{2,1,0:T(8,128)S(1)}, u32[]{:S(2)}, u32[]{:S(2)}) collective-permute-start(f32[8,64,256]{2,1,0:T(8,128)S(1)} %copy-done.1), channel_id=1, source_target_pairs={{0,2},{2,0},{4,6},{6,4},{8,10},{10,8},{12,14},{14,12},{16,18},{18,... | collective-permute-start | bytes 1572872 | tf_op jit(solution)/shard_map/ppermute | solution.py:381
  12.4 0.0 collective-permute-done.2.strip
  12.4 0.1 pad_maximum_fusion
  12.5 5.1 %collective-permute-start.3 = (f32[448,256]{1,0:T(8,128)S(1)}, f32[448,256]{1,0:T(8,128)S(1)}, u32[]{:S(2)}, u32[]{:S(2)}) collective-permute-start(f32[448,256]{1,0:T(8,128)S(1)} %get-tuple-element.42), channel_id=1, source_target_pairs={{2,4},{6,8},{10,12},{14,16},{18,20},{22,24},{26,28},{30,32},{34,36... | collective-permute-start | bytes 1376264 | tf_op jit(solution)/shard_map/ppermute | solution.py:385
  17.6 1.9 %collective-permute-start.4 = (f32[448,256]{1,0:T(8,128)S(1)}, f32[448,256]{1,0:T(8,128)S(1)}, u32[]{:S(2)}, u32[]{:S(2)}) collective-permute-start(f32[448,256]{1,0:T(8,128)S(1)} %get-tuple-element.41), channel_id=1, source_target_pairs={{0,2},{2,0},{4,6},{6,4},{8,10},{10,8},{12,14},{14,12},{16,18},{18,... | collective-permute-start | bytes 1376264 | tf_op jit(solution)/shard_map/ppermute | solution.py:386
  19.6 1.3 %shard_map.55 = (f32[5,16,256]{2,1,0:T(8,128)S(1)}, bf16[256,256]{1,0:T(8,128)(2,1)S(1)}, bf16[256,256]{1,0:T(8,128)(2,1)S(1)}, bf16[288,256]{1,0:T(8,128)(2,1)S...) custom-call(s32[1,3]{1,0:T(1,128)S(1)} %copy-done.2, ...), custom_call_target="tpu_custom_call" | custom-call | flops 20000000000 | tf_op jit(solution)/shard_map/pallas_call | solution.py:341
  20.9 0.0 collective-permute-done.est_off
  20.9 1.6 %shard_map.56 = (f32[16,72,256]{2,1,0:T(8,128)S(1)}, f32[8,48,256]{2,1,0:T(8,128)S(1)}) custom-call(f32[8,64,256]{2,1,0:T(8,128)S(1)} %copy-done.1, f32[8,64,256]{2,1,0:T(8,128)S(1)} %bitcast.5, f32[8,64,256]{2,1,0:T(8,128)S(1)} %collective-permute-done.est_off, f32[8,64,256]{2,1,0:T(8,128)S(1)} %collective-permute-done.1.est_on, ...), custom_call_target="tpu_custom_call" | custom-call | tf_op jit(solution)/shard_map/pallas_call | solution.py:341
  22.5 1.3 %collective-permute-done.3.off = f32[448,256]{1,0:T(8,128)S(1)} collective-permute-done((f32[448,256]{1,0:T(8,128)S(1)}, f32[448,256]{1,0:T(8,128)S(1)}, u32[]{:S(2)}, u32[]{:S(2)}) %collective-permute-start.3) | collective-permute-done | bytes 458784 | tf_op jit(solution)/shard_map/ppermute | solution.py:385
  23.8 0.0 collective-permute-done.4.on
  23.8 1.6 %shard_map.57 = f32[8,72,256]{2,1,0:T(8,128)S(1)} custom-call(f32[16,72,256]{2,1,0:T(8,128)S(1)} %get-tuple-element.29.partial, f32[8,48,256]{2,1,0:T(8,128)S(1)} %get-tuple-element.30.inner, f32[8,64,256]{2,1,0:T(8,128)S(1)} %bitcast.6, f32[8,24,256]{2,1,0:T(8,128)S(1)} %collective-permute-done.2.strip, f32[448,256]{1,0:T(8,128)S(1)} %collective-permute-done.3.off, ...), custom_call_target="tpu_custom_call" | custom-call | tf_op jit(solution)/shard_map/pallas_call | solution.py:341
  25.4 15.4 %all_to_all.10.parts = f32[8,72,256]{2,1,0:T(8,128)S(1)} all-to-all(f32[8,72,256]{2,1,0:T(8,128)S(1)} %shard_map.57), channel_id=1, replica_groups=mesh['view'=8,'slab'=32,'row'=2] {'view'}, dimensions={0} | all-to-all | bytes 1179648 | tf_op jit(solution)/shard_map/all_to_all | solution.py:418
  40.8 0.1 shard_map.58
  40.9 12.7 %all_to_all.11.field = f32[8,72,256]{2,1,0:T(8,128)S(1)} all-to-all(f32[8,72,256]{2,1,0:T(8,128)S(1)} %shard_map.58), channel_id=1, replica_groups=mesh['view'=8,'slab'=32,'row'=2] {'view'}, dimensions={0} | all-to-all | bytes 1179648 | tf_op jit(solution)/shard_map/all_to_all | solution.py:425
  53.6 5.9 %collective-permute-start.5 = (f32[3,72,256]{2,1,0:T(8,128)S(1)}, f32[3,72,256]{2,1,0:T(8,128)S(1)}, u32[]{:S(2)}, u32[]{:S(2)}) collective-permute-start(f32[3,72,256]{2,1,0:T(8,128)S(1)} %get-tuple-element.38), channel_id=1, source_target_pairs={{2,4},{6,8},{10,12},{14,16},{18,20},{22,24},{26,28},{30,32},{34,36... | collective-permute-start | bytes 663560 | tf_op jit(solution)/shard_map/ppermute | solution.py:428
  59.5 1.9 %collective-permute-start.6 = (f32[3,72,256]{2,1,0:T(8,128)S(1)}, f32[3,72,256]{2,1,0:T(8,128)S(1)}, u32[]{:S(2)}, u32[]{:S(2)}) collective-permute-start(f32[3,72,256]{2,1,0:T(8,128)S(1)} %get-tuple-element.37), channel_id=1, source_target_pairs={{0,2},{2,0},{4,6},{6,4},{8,10},{10,8},{12,14},{14,12},{16,18},{18,... | collective-permute-start | bytes 663560 | tf_op jit(solution)/shard_map/ppermute | solution.py:429
  61.5 1.7 %collective-permute-done.5.off = f32[3,72,256]{2,1,0:T(8,128)S(1)} collective-permute-done((f32[3,72,256]{2,1,0:T(8,128)S(1)}, f32[3,72,256]{2,1,0:T(8,128)S(1)}, u32[]{:S(2)}, u32[]{:S(2)}) %collective-permute-start.5) | collective-permute-done | bytes 221216 | tf_op jit(solution)/shard_map/ppermute | solution.py:428
  63.2 0.0 collective-permute-done.6.on
  63.2 3.2 %shard_map.59 = f32[8,64,256]{2,1,0:T(8,128)} custom-call(f32[8,72,256]{2,1,0:T(8,128)S(1)} %all_to_all.11.field, f32[3,72,256]{2,1,0:T(8,128)S(1)} %collective-permute-done.5.off, f32[3,72,256]{2,1,0:T(8,128)S(1)} %collective-permute-done.6.on), custom_call_target="tpu_custom_call" | custom-call | tf_op jit(solution)/shard_map/pallas_call | solution.py:341
  (14 shorter events, 0.1 us)
Async XLA Ops:
  0.0 1.4 %copy-start = (f32[1,8,64,256]{3,2,1,0:T(8,128)S(1)}, f32[1,8,64,256]{3,2,1,0:T(8,128)}, u32[]{:S(2)}) copy-start(f32[1,8,64,256]{3,2,1,0:T(8,128)} %param.5) | copy-start | bytes 1572868
  0.0 1.3 %copy-start.1 = (f32[8,64,256]{2,1,0:T(8,128)S(1)}, f32[8,64,256]{2,1,0:T(8,128)}, u32[]{:S(2)}) copy-start(f32[8,64,256]{2,1,0:T(8,128)} %est.1) | copy-start | bytes 1572868
  0.0 12.4 %copy-start.4 = (f32[1,3,5]{2,0,1:T(1,128)S(1)}, f32[1,3,5]{2,0,1:T(1,128)}, u32[]{:S(2)}) copy-start(f32[1,3,5]{2,0,1:T(1,128)} %param.7) | copy-start | bytes 184
  1.4 18.2 %copy-start.2 = (s32[1,3]{1,0:T(1,128)S(1)}, s32[1,3]{1,0:T(1,128)}, u32[]{:S(2)}) copy-start(s32[1,3]{1,0:T(1,128)} %band.1) | copy-start | bytes 40
  1.4 18.2 %copy-start.3 = (s32[1,3]{1,0:T(1,128)S(1)}, s32[1,3]{1,0:T(1,128)}, u32[]{:S(2)}) copy-start(s32[1,3]{1,0:T(1,128)} %perm.1) | copy-start | bytes 40
  1.4 11.0 %collective-permute-start.2 = (f32[8,24,256]{2,1,0:T(8,128)S(1)}, f32[8,24,256]{2,1,0:T(8,128)S(1)}, u32[]{:S(2)}, u32[]{:S(2)}) collective-permute-start(f32[8,24,256]{2,1,0:T(8,128)S(1)} %pad_maximum_fusion.2), channel_id=1, source_target_pairs={{0,1},{1,0},{2,3},{3,2},{4,5},{5,4},{6,7},{7,6},{8,9},{9,8},{10,11... | collective-permute-start | bytes 589832 | tf_op jit(solution)/shard_map/ppermute | solution.py:378
  6.1 14.8 %collective-permute-start = (f32[8,64,256]{2,1,0:T(8,128)S(1)}, f32[8,64,256]{2,1,0:T(8,128)S(1)}, u32[]{:S(2)}, u32[]{:S(2)}) collective-permute-start(f32[8,64,256]{2,1,0:T(8,128)S(1)} %copy-done.1), channel_id=1, source_target_pairs={{2,4},{6,8},{10,12},{14,16},{18,20},{22,24},{26,28},{30,32},{34,36... | collective-permute-start | bytes 1572872 | tf_op jit(solution)/shard_map/ppermute | solution.py:380
  10.5 10.4 %collective-permute-start.1 = (f32[8,64,256]{2,1,0:T(8,128)S(1)}, f32[8,64,256]{2,1,0:T(8,128)S(1)}, u32[]{:S(2)}, u32[]{:S(2)}) collective-permute-start(f32[8,64,256]{2,1,0:T(8,128)S(1)} %copy-done.1), channel_id=1, source_target_pairs={{0,2},{2,0},{4,6},{6,4},{8,10},{10,8},{12,14},{14,12},{16,18},{18,... | collective-permute-start | bytes 1572872 | tf_op jit(solution)/shard_map/ppermute | solution.py:381
  12.5 11.3 %collective-permute-start.3 = (f32[448,256]{1,0:T(8,128)S(1)}, f32[448,256]{1,0:T(8,128)S(1)}, u32[]{:S(2)}, u32[]{:S(2)}) collective-permute-start(f32[448,256]{1,0:T(8,128)S(1)} %get-tuple-element.42), channel_id=1, source_target_pairs={{2,4},{6,8},{10,12},{14,16},{18,20},{22,24},{26,28},{30,32},{34,36... | collective-permute-start | bytes 1376264 | tf_op jit(solution)/shard_map/ppermute | solution.py:385
  17.6 6.2 %collective-permute-start.4 = (f32[448,256]{1,0:T(8,128)S(1)}, f32[448,256]{1,0:T(8,128)S(1)}, u32[]{:S(2)}, u32[]{:S(2)}) collective-permute-start(f32[448,256]{1,0:T(8,128)S(1)} %get-tuple-element.41), channel_id=1, source_target_pairs={{0,2},{2,0},{4,6},{6,4},{8,10},{10,8},{12,14},{14,12},{16,18},{18,... | collective-permute-start | bytes 1376264 | tf_op jit(solution)/shard_map/ppermute | solution.py:386
  53.6 9.5 %collective-permute-start.5 = (f32[3,72,256]{2,1,0:T(8,128)S(1)}, f32[3,72,256]{2,1,0:T(8,128)S(1)}, u32[]{:S(2)}, u32[]{:S(2)}) collective-permute-start(f32[3,72,256]{2,1,0:T(8,128)S(1)} %get-tuple-element.38), channel_id=1, source_target_pairs={{2,4},{6,8},{10,12},{14,16},{18,20},{22,24},{26,28},{30,32},{34,36... | collective-permute-start | bytes 663560 | tf_op jit(solution)/shard_map/ppermute | solution.py:428
  59.5 3.6 %collective-permute-start.6 = (f32[3,72,256]{2,1,0:T(8,128)S(1)}, f32[3,72,256]{2,1,0:T(8,128)S(1)}, u32[]{:S(2)}, u32[]{:S(2)}) collective-permute-start(f32[3,72,256]{2,1,0:T(8,128)S(1)} %get-tuple-element.37), channel_id=1, source_target_pairs={{0,2},{2,0},{4,6},{6,4},{8,10},{10,8},{12,14},{14,12},{16,18},{18,... | collective-permute-start | bytes 663560 | tf_op jit(solution)/shard_map/ppermute | solution.py:429

commit v6 on v5

--- a/solution.py
+++ b/solution.py
@@ -150,7 +150,7 @@
 
 
 def views_kernel(
-    slabs, partial, inner, data, strip, off, on,
+    slabs, partial, inner, data, strip, est_off, off, on,
     taps_z, wx_h, wx_l, wr_h, wr_l, wy2_h, wy2_l, out, rims, ratio, flat,
 ):
     planes, rows, lanes = data.shape
@@ -166,8 +166,10 @@
         def read(q):
             if q // planes == 1:
                 return strip[q - planes, 0:EST_STRIP, :]
+            if (below, above)[q // planes // 2] is off:
+                return off[q % planes, 0:EST_STRIP, :]
             at = q % planes * thick
-            return (below, above)[q // planes // 2][at : at + EST_STRIP, :]
+            return on[at : at + EST_STRIP, :]
 
         for p in range(wide):
             rims[p * EST_STRIP : (p + 1) * EST_STRIP, :] = blur_z(lambda t: read(p + t), taps_z)
@@ -192,17 +194,17 @@
         )
 
     def beyond(lower):
-        first, second = (on, off) if lower else (off, on)
+        next_chip = jnp.logical_not(odd) if lower else odd
         low = 0 if lower else WIDTH + planes
         start, end, last = touched(low, low + WIDTH)
         blurred = jnp.concatenate([start, partial[low : low + WIDTH, 8 : rows - 8, :], end, last], axis=1)
         tops, lows = [], []
         for q in range(WIDTH):
-            top = slice(base + q * rows, base + (q + 1) * rows)
-            at = (q + planes - WIDTH if lower else q) * thick + EST_STRIP
-            at = slice(at, at + DATA_STRIP)
-            tops.append(jnp.where(odd, first[top, :], second[top, :])[None])
-            lows.append(jnp.where(odd, first[at, :], second[at, :])[None])
+            k = q + planes - WIDTH if lower else q
+            top = on[base + q * rows : base + (q + 1) * rows, :]
+            last_rows = on[k * thick + EST_STRIP : (k + 1) * thick, :]
+            tops.append(jnp.where(next_chip, est_off[planes + q], top)[None])
+            lows.append(jnp.where(next_chip, off[k, EST_STRIP:thick, :], last_rows)[None])
         value = [jnp.concatenate(tops, axis=0), jnp.concatenate(lows, axis=0)]
         value = jnp.concatenate(value, axis=1) / blurred
         inside = slab > 0 if lower else slab < slabs - 1
@@ -377,11 +379,12 @@
     )
     strip = lax.ppermute(edge, "row", [(0, 1), (1, 0)])
     held = lax.optimization_barrier((estimate, edge))[0]
-    est_off = lax.ppermute(held, "slab", off_pairs)
+    far = jnp.concatenate([held, rim_off.reshape(WIDTH, rows, lanes)], axis=0)
+    held, far = lax.optimization_barrier((held, far))
+    est_off = lax.ppermute(far, "slab", off_pairs)
     est_on = lax.ppermute(held, "slab", on_pairs)
-    flat = strip.reshape(-1, lanes)
-    off = jnp.concatenate([flat, rim_off], axis=0)
-    on = jnp.concatenate([flat, rim_on], axis=0)
+    on = jnp.concatenate([strip.reshape(-1, lanes), rim_on], axis=0)
+    off = strip
     off = lax.ppermute(off, "slab", off_pairs)
     on = lax.ppermute(on, "slab", on_pairs)
 
@@ -413,7 +416,7 @@
             pltpu.VMEM((wide, used, lanes), F32),
             pltpu.VMEM((planes * pitch, lanes), F32),
         ],
-        partial, inner, data, strip, off, on, taps_z, wx_h, wx_l, wr_h, wr_l, wy2_h, wy2_l,
+        partial, inner, data, strip, est_off, off, on, taps_z, wx_h, wx_l, wr_h, wr_l, wy2_h, wy2_l,
     )
     parts = lax.all_to_all(back, "view", 0, 0, tiled=True)
     copies = call(

time: 66.7 us -> 65.7 us (0.985)
  waiting for transfers between devices: 2.99 us -> 2.16 us
    ppermute x1, waiting for transfers between devices: 1.3 us -> 0.47 us  [body(): off = lax.ppermute(off, 'slab', off_pairs)]
where the time goes in v6:
time: 65.7 us; the launch traced here: 65.3 us
  blocking collectives  27.8 us (42%)
  starting transfers between devices  26 us (40%)
  Pallas kernels  7.67 us (12%)
  waiting for transfers between devices  2.16 us (3%)
  other arithmetic  1.34 us (2%)
    all_to_all x1, blocking collectives, body(): parts = lax.all_to_all(back, 'view', 0, 0, tiled=True)  15.1 us
    all_to_all x1, blocking collectives, body(): field = lax.all_to_all(copies, 'view', 0, 0, tiled=True)  12.7 us
    pallas_call x5, Pallas kernels, call(): pl.pallas_call(kernel, out_shape=shapes, in_specs=specs, out_specs=jax.tr...  7.67 us
    ppermute x1, starting transfers between devices, body(): off = lax.ppermute(jnp.where(is_odd, high, low), 'slab', off_pairs)  6.02 us
    ppermute x1, starting transfers between devices, body(): off = lax.ppermute(off, 'slab', off_pairs)  4.65 us
    ppermute x1, starting transfers between devices, body(): strip = lax.ppermute(edge, 'row', [(0, 1), (1, 0)])  4.65 us
    ppermute x1, starting transfers between devices, body(): est_off = lax.ppermute(far, 'slab', off_pairs)  4.39 us
    ppermute x1, starting transfers between devices, body(): on = lax.ppermute(on, 'slab', on_pairs)  2.41 us
  transfers between devices with their start and end apart: 7, of which 2 were waited for; matrix products, arithmetic and copies ran while one was open for 0% of the time, Pallas kernels for 4%

profile of v6, /device:TPU:193, one launch (start us, length us, event | category | flops | bytes accessed | tf_op | source)
XLA Modules:
  0.0 65.3 jit_solution(16372319958281488377)
XLA Ops:
  0.0 1.2 %slice_select_fusion = (f32[1,4,64,256]{3,2,1,0:T(8,128)S(1)}, f32[1,4,64,256]{3,2,1,0:T(8,128)S(1)}) fusion(f32[1,8,64,256]{3,2,1,0:T(8,128)} %param.5, pred[]{:T(512)S(6)} %eq.6), kind=kLoop, calls=%fused_computation.2 | loop fusion | flops 131072 | bytes 1048577 | tf_op jit(solution)/shard_map/jit(_where)/select_n | solution.py:369
  1.2 0.1 copy-done
  1.3 0.1 copy-done.1
  1.4 4.7 %collective-permute-start.2 = (f32[8,24,256]{2,1,0:T(8,128)S(1)}, f32[8,24,256]{2,1,0:T(8,128)S(1)}, u32[]{:S(2)}, u32[]{:S(2)}) collective-permute-start(f32[8,24,256]{2,1,0:T(8,128)S(1)} %pad_maximum_fusion.2), channel_id=1, source_target_pairs={{0,1},{1,0},{2,3},{3,2},{4,5},{5,4},{6,7},{7,6},{8,9},{9,8},{10,11... | collective-permute-start | bytes 589832 | tf_op jit(solution)/shard_map/ppermute | solution.py:380
  6.1 0.0 copy-start.2
  6.1 0.0 copy-start.3
  6.1 0.1 pad_maximum_fusion
  6.2 4.4 %collective-permute-start = (f32[12,64,256]{2,1,0:T(8,128)S(1)}, f32[12,64,256]{2,1,0:T(8,128)S(1)}, u32[]{:S(2)}, u32[]{:S(2)}) collective-permute-start(f32[12,64,256]{2,1,0:T(8,128)S(1)} %pad_maximum_fusion), channel_id=1, source_target_pairs={{2,4},{6,8},{10,12},{14,16},{18,20},{22,24},{26,28},{30,32},{34,36... | collective-permute-start | bytes 2359304 | tf_op jit(solution)/shard_map/ppermute | solution.py:384
  10.6 1.9 %collective-permute-start.1 = (f32[8,64,256]{2,1,0:T(8,128)S(1)}, f32[8,64,256]{2,1,0:T(8,128)S(1)}, u32[]{:S(2)}, u32[]{:S(2)}) collective-permute-start(f32[8,64,256]{2,1,0:T(8,128)S(1)} %copy-done), channel_id=1, source_target_pairs={{0,2},{2,0},{4,6},{6,4},{8,10},{10,8},{12,14},{14,12},{16,18},{18,... | collective-permute-start | bytes 1572872 | tf_op jit(solution)/shard_map/ppermute | solution.py:385
  12.6 2.4 %collective-permute-start.4 = (f32[448,256]{1,0:T(8,128)S(1)}, f32[448,256]{1,0:T(8,128)S(1)}, u32[]{:S(2)}, u32[]{:S(2)}) collective-permute-start(f32[448,256]{1,0:T(8,128)S(1)} %pad_maximum_fusion.1), channel_id=1, source_target_pairs={{0,2},{2,0},{4,6},{6,4},{8,10},{10,8},{12,14},{14,12},{16,18},{18,... | collective-permute-start | bytes 1376264 | tf_op jit(solution)/shard_map/ppermute | solution.py:389
  15.0 4.7 %collective-permute-start.3 = (f32[8,24,256]{2,1,0:T(8,128)S(1)}, f32[8,24,256]{2,1,0:T(8,128)S(1)}, u32[]{:S(2)}, u32[]{:S(2)}) collective-permute-start(f32[8,24,256]{2,1,0:T(8,128)S(1)} %collective-permute-done.2.strip), channel_id=1, source_target_pairs={{2,4},{6,8},{10,12},{14,16},{18,20},{22,24},{26,28},{30,32},{34,36... | collective-permute-start | bytes 589832 | tf_op jit(solution)/shard_map/ppermute | solution.py:388
  19.7 1.3 %shard_map.55 = (f32[5,16,256]{2,1,0:T(8,128)S(1)}, bf16[256,256]{1,0:T(8,128)(2,1)S(1)}, bf16[256,256]{1,0:T(8,128)(2,1)S(1)}, bf16[288,256]{1,0:T(8,128)(2,1)S...) custom-call(s32[1,3]{1,0:T(1,128)S(1)} %copy-done.2, ...), custom_call_target="tpu_custom_call" | custom-call | flops 20000000000 | tf_op jit(solution)/shard_map/pallas_call | solution.py:343
  20.9 0.0 collective-permute-done.1.est_on
  21.0 1.5 %shard_map.56 = (f32[16,72,256]{2,1,0:T(8,128)S(1)}, f32[8,48,256]{2,1,0:T(8,128)S(1)}) custom-call(f32[8,64,256]{2,1,0:T(8,128)S(1)} %copy-done, f32[8,64,256]{2,1,0:T(8,128)S(1)} %bitcast.6, f32[12,64,256]{2,1,0:T(8,128)S(1)} %collective-permute-done.est_off, f32[8,64,256]{2,1,0:T(8,128)S(1)} %collective-permute-done.1.est_on, ...), custom_call_target="tpu_custom_call" | custom-call | tf_op jit(solution)/shard_map/pallas_call | solution.py:343
  22.5 0.5 collective-permute-done.3.off
  23.0 0.0 collective-permute-done.4.on
  23.0 1.6 %shard_map.57 = f32[8,72,256]{2,1,0:T(8,128)S(1)} custom-call(f32[16,72,256]{2,1,0:T(8,128)S(1)} %get-tuple-element.34.partial, f32[8,48,256]{2,1,0:T(8,128)S(1)} %get-tuple-element.35.inner, f32[8,64,256]{2,1,0:T(8,128)S(1)} %bitcast.7, f32[8,24,256]{2,1,0:T(8,128)S(1)} %collective-permute-done.2.strip, f32[12,64,256]{2,1,0:T(8,128)S(1)} %collective-permute-done.est_off, ...), custom_call_target="tpu_custom_call" | custom-call | tf_op jit(solution)/shard_map/pallas_call | solution.py:343
  24.6 15.1 %all_to_all.10.parts = f32[8,72,256]{2,1,0:T(8,128)S(1)} all-to-all(f32[8,72,256]{2,1,0:T(8,128)S(1)} %shard_map.57), channel_id=1, replica_groups=mesh['view'=8,'slab'=32,'row'=2] {'view'}, dimensions={0} | all-to-all | bytes 1179648 | tf_op jit(solution)/shard_map/all_to_all | solution.py:421
  39.7 0.1 shard_map.58
  39.7 12.7 %all_to_all.11.field = f32[8,72,256]{2,1,0:T(8,128)S(1)} all-to-all(f32[8,72,256]{2,1,0:T(8,128)S(1)} %shard_map.58), channel_id=1, replica_groups=mesh['view'=8,'slab'=32,'row'=2] {'view'}, dimensions={0} | all-to-all | bytes 1179648 | tf_op jit(solution)/shard_map/all_to_all | solution.py:428
  52.5 6.0 %collective-permute-start.5 = (f32[3,72,256]{2,1,0:T(8,128)S(1)}, f32[3,72,256]{2,1,0:T(8,128)S(1)}, u32[]{:S(2)}, u32[]{:S(2)}) collective-permute-start(f32[3,72,256]{2,1,0:T(8,128)S(1)} %get-tuple-element.42), channel_id=1, source_target_pairs={{2,4},{6,8},{10,12},{14,16},{18,20},{22,24},{26,28},{30,32},{34,36... | collective-permute-start | bytes 663560 | tf_op jit(solution)/shard_map/ppermute | solution.py:431
  58.5 1.9 %collective-permute-start.6 = (f32[3,72,256]{2,1,0:T(8,128)S(1)}, f32[3,72,256]{2,1,0:T(8,128)S(1)}, u32[]{:S(2)}, u32[]{:S(2)}) collective-permute-start(f32[3,72,256]{2,1,0:T(8,128)S(1)} %get-tuple-element.41), channel_id=1, source_target_pairs={{0,2},{2,0},{4,6},{6,4},{8,10},{10,8},{12,14},{14,12},{16,18},{18,... | collective-permute-start | bytes 663560 | tf_op jit(solution)/shard_map/ppermute | solution.py:432
  60.5 1.7 %collective-permute-done.5.off = f32[3,72,256]{2,1,0:T(8,128)S(1)} collective-permute-done((f32[3,72,256]{2,1,0:T(8,128)S(1)}, f32[3,72,256]{2,1,0:T(8,128)S(1)}, u32[]{:S(2)}, u32[]{:S(2)}) %collective-permute-start.5) | collective-permute-done | bytes 221216 | tf_op jit(solution)/shard_map/ppermute | solution.py:431
  62.1 3.2 %shard_map.59 = f32[8,64,256]{2,1,0:T(8,128)} custom-call(f32[8,72,256]{2,1,0:T(8,128)S(1)} %all_to_all.11.field, f32[3,72,256]{2,1,0:T(8,128)S(1)} %collective-permute-done.5.off, f32[3,72,256]{2,1,0:T(8,128)S(1)} %collective-permute-done.6.on), custom_call_target="tpu_custom_call" | custom-call | tf_op jit(solution)/shard_map/pallas_call | solution.py:343
  (15 shorter events, 0.1 us)
Async XLA Ops:
  0.0 1.4 %copy-start.1 = (f32[1,8,64,256]{3,2,1,0:T(8,128)S(1)}, f32[1,8,64,256]{3,2,1,0:T(8,128)}, u32[]{:S(2)}) copy-start(f32[1,8,64,256]{3,2,1,0:T(8,128)} %param.5) | copy-start | bytes 1572868
  0.0 1.3 %copy-start = (f32[8,64,256]{2,1,0:T(8,128)S(1)}, f32[8,64,256]{2,1,0:T(8,128)}, u32[]{:S(2)}) copy-start(f32[8,64,256]{2,1,0:T(8,128)} %est.1) | copy-start | bytes 1572868
  1.4 11.1 %copy-start.4 = (f32[1,3,5]{2,0,1:T(1,128)S(1)}, f32[1,3,5]{2,0,1:T(1,128)}, u32[]{:S(2)}) copy-start(f32[1,3,5]{2,0,1:T(1,128)} %param.7) | copy-start | bytes 184
  1.4 11.1 %collective-permute-start.2 = (f32[8,24,256]{2,1,0:T(8,128)S(1)}, f32[8,24,256]{2,1,0:T(8,128)S(1)}, u32[]{:S(2)}, u32[]{:S(2)}) collective-permute-start(f32[8,24,256]{2,1,0:T(8,128)S(1)} %pad_maximum_fusion.2), channel_id=1, source_target_pairs={{0,1},{1,0},{2,3},{3,2},{4,5},{5,4},{6,7},{7,6},{8,9},{9,8},{10,11... | collective-permute-start | bytes 589832 | tf_op jit(solution)/shard_map/ppermute | solution.py:380
  6.1 13.6 %copy-start.2 = (s32[1,3]{1,0:T(1,128)S(1)}, s32[1,3]{1,0:T(1,128)}, u32[]{:S(2)}) copy-start(s32[1,3]{1,0:T(1,128)} %band.1) | copy-start | bytes 40
  6.1 13.6 %copy-start.3 = (s32[1,3]{1,0:T(1,128)S(1)}, s32[1,3]{1,0:T(1,128)}, u32[]{:S(2)}) copy-start(s32[1,3]{1,0:T(1,128)} %perm.1) | copy-start | bytes 40
  6.2 14.8 %collective-permute-start = (f32[12,64,256]{2,1,0:T(8,128)S(1)}, f32[12,64,256]{2,1,0:T(8,128)S(1)}, u32[]{:S(2)}, u32[]{:S(2)}) collective-permute-start(f32[12,64,256]{2,1,0:T(8,128)S(1)} %pad_maximum_fusion), channel_id=1, source_target_pairs={{2,4},{6,8},{10,12},{14,16},{18,20},{22,24},{26,28},{30,32},{34,36... | collective-permute-start | bytes 2359304 | tf_op jit(solution)/shard_map/ppermute | solution.py:384
  10.6 10.4 %collective-permute-start.1 = (f32[8,64,256]{2,1,0:T(8,128)S(1)}, f32[8,64,256]{2,1,0:T(8,128)S(1)}, u32[]{:S(2)}, u32[]{:S(2)}) collective-permute-start(f32[8,64,256]{2,1,0:T(8,128)S(1)} %copy-done), channel_id=1, source_target_pairs={{0,2},{2,0},{4,6},{6,4},{8,10},{10,8},{12,14},{14,12},{16,18},{18,... | collective-permute-start | bytes 1572872 | tf_op jit(solution)/shard_map/ppermute | solution.py:385
  12.6 10.4 %collective-permute-start.4 = (f32[448,256]{1,0:T(8,128)S(1)}, f32[448,256]{1,0:T(8,128)S(1)}, u32[]{:S(2)}, u32[]{:S(2)}) collective-permute-start(f32[448,256]{1,0:T(8,128)S(1)} %pad_maximum_fusion.1), channel_id=1, source_target_pairs={{0,2},{2,0},{4,6},{6,4},{8,10},{10,8},{12,14},{14,12},{16,18},{18,... | collective-permute-start | bytes 1376264 | tf_op jit(solution)/shard_map/ppermute | solution.py:389
  15.0 8.0 %collective-permute-start.3 = (f32[8,24,256]{2,1,0:T(8,128)S(1)}, f32[8,24,256]{2,1,0:T(8,128)S(1)}, u32[]{:S(2)}, u32[]{:S(2)}) collective-permute-start(f32[8,24,256]{2,1,0:T(8,128)S(1)} %collective-permute-done.2.strip), channel_id=1, source_target_pairs={{2,4},{6,8},{10,12},{14,16},{18,20},{22,24},{26,28},{30,32},{34,36... | collective-permute-start | bytes 589832 | tf_op jit(solution)/shard_map/ppermute | solution.py:388
  52.5 9.6 %collective-permute-start.5 = (f32[3,72,256]{2,1,0:T(8,128)S(1)}, f32[3,72,256]{2,1,0:T(8,128)S(1)}, u32[]{:S(2)}, u32[]{:S(2)}) collective-permute-start(f32[3,72,256]{2,1,0:T(8,128)S(1)} %get-tuple-element.42), channel_id=1, source_target_pairs={{2,4},{6,8},{10,12},{14,16},{18,20},{22,24},{26,28},{30,32},{34,36... | collective-permute-start | bytes 663560 | tf_op jit(solution)/shard_map/ppermute | solution.py:431
  58.5 3.6 %collective-permute-start.6 = (f32[3,72,256]{2,1,0:T(8,128)S(1)}, f32[3,72,256]{2,1,0:T(8,128)S(1)}, u32[]{:S(2)}, u32[]{:S(2)}) collective-permute-start(f32[3,72,256]{2,1,0:T(8,128)S(1)} %get-tuple-element.41), channel_id=1, source_target_pairs={{0,2},{2,0},{4,6},{6,4},{8,10},{10,8},{12,14},{14,12},{16,18},{18,... | collective-permute-start | bytes 663560 | tf_op jit(solution)/shard_map/ppermute | solution.py:432

commit v7 on v6

--- a/solution.py
+++ b/solution.py
@@ -159,17 +159,15 @@
     used = rows + DATA_STRIP
     wide = planes + 2 * WIDTH
     thick = EST_STRIP + DATA_STRIP
-    base = planes * thick
+    base = planes * EST_STRIP + WIDTH * DATA_STRIP
     odd = lax.rem(slab, 2) == 1
 
     def blur_first(below, above):
         def read(q):
             if q // planes == 1:
                 return strip[q - planes, 0:EST_STRIP, :]
-            if (below, above)[q // planes // 2] is off:
-                return off[q % planes, 0:EST_STRIP, :]
-            at = q % planes * thick
-            return on[at : at + EST_STRIP, :]
+            at = q % planes * EST_STRIP
+            return (below, above)[q // planes // 2][at : at + EST_STRIP, :]
 
         for p in range(wide):
             rims[p * EST_STRIP : (p + 1) * EST_STRIP, :] = blur_z(lambda t: read(p + t), taps_z)
@@ -200,11 +198,11 @@
         blurred = jnp.concatenate([start, partial[low : low + WIDTH, 8 : rows - 8, :], end, last], axis=1)
         tops, lows = [], []
         for q in range(WIDTH):
-            k = q + planes - WIDTH if lower else q
             top = on[base + q * rows : base + (q + 1) * rows, :]
-            last_rows = on[k * thick + EST_STRIP : (k + 1) * thick, :]
+            at = planes * EST_STRIP + q * DATA_STRIP
+            at = slice(at, at + DATA_STRIP)
             tops.append(jnp.where(next_chip, est_off[planes + q], top)[None])
-            lows.append(jnp.where(next_chip, off[k, EST_STRIP:thick, :], last_rows)[None])
+            lows.append(jnp.where(next_chip, off[at, :], on[at, :])[None])
         value = [jnp.concatenate(tops, axis=0), jnp.concatenate(lows, axis=0)]
         value = jnp.concatenate(value, axis=1) / blurred
         inside = slab > 0 if lower else slab < slabs - 1
@@ -256,7 +254,7 @@
             out[v] = value
 
 
-def variation_kernel(slabs, rows, field, off, on, out, start, first, second):
+def variation_kernel(slabs, rows, field, off, on, out, start, first, second, sems):
     planes, used, lanes = field.shape
     slab, row = lax.axis_index("slab"), lax.axis_index("row")
     half = lanes // 2
@@ -315,7 +313,7 @@
                 f_x.append(g_x * scale)
         return now, f_x, f_y, f_z
 
-    def one_pass(source, low, high, group, target):
+    def one_pass(source, low, high, group, target, then=None):
         before = flux(source, low - 1, 1, True)[3]
         for z in range(low, high, group):
             count = min(group, high - z)
@@ -328,23 +326,37 @@
                 spread = (f_z[h] - below) + (f_y[h] - last_y(f_y[h])) + (f_x[h] - side[h])
                 target[z : z + count, :, h * half : (h + 1) * half] = masked(now[h] + TAU * spread, z)
             before = [f[count - 1 : count] for f in f_z]
+            if then is not None:
+                then(z, count)
 
     deep = planes + 2 * TV_HALO
-    groups = (4, 5, 4)
+    groups = (4, 5, 3)
     one_pass(start, 1, deep - 1, groups[0], first)
     one_pass(first, 2, deep - 2, groups[1], second)
-    one_pass(second, 3, deep - 3, groups[2], first)
     skip = pl.multiple_of(row * (used - rows), 8)
-    out[...] = first[TV_HALO : TV_HALO + planes, pl.ds(skip, rows), :]
-
-
-def call(kernel, shapes, scratch, *args, cost=None, scalars=0):
+    copies = []
+
+    def leave(z, count):
+        copy = pltpu.make_async_copy(
+            first.at[z : z + count, pl.ds(skip, rows), :],
+            out.at[z - TV_HALO : z - TV_HALO + count],
+            sems.at[len(copies)],
+        )
+        copy.start()
+        copies.append(copy)
+
+    one_pass(second, TV_HALO, deep - TV_HALO, groups[2], first, leave)
+    for copy in copies:
+        copy.wait()
+
+
+def call(kernel, shapes, scratch, *args, cost=None, scalars=0, target=VMEM):
     specs = [SMEM if i < scalars else VMEM for i in range(len(args))]
     return pl.pallas_call(
         kernel,
         out_shape=shapes,
         in_specs=specs,
-        out_specs=jax.tree.map(lambda _: VMEM, shapes),
+        out_specs=jax.tree.map(lambda _: target, shapes),
         scratch_shapes=scratch,
         cost_estimate=cost,
         compiler_params=pltpu.CompilerParams(vmem_limit_bytes=16 * 2**20),
@@ -383,8 +395,11 @@
     held, far = lax.optimization_barrier((held, far))
     est_off = lax.ppermute(far, "slab", off_pairs)
     est_on = lax.ppermute(held, "slab", on_pairs)
-    on = jnp.concatenate([strip.reshape(-1, lanes), rim_on], axis=0)
-    off = strip
+    parts = [strip[:, :EST_STRIP].reshape(-1, lanes)]
+    first = strip[:WIDTH, EST_STRIP:].reshape(-1, lanes)
+    last = strip[planes - WIDTH :, EST_STRIP:].reshape(-1, lanes)
+    off = jnp.concatenate(parts + [jnp.where(is_odd, last, first)], axis=0)
+    on = jnp.concatenate(parts + [jnp.where(is_odd, first, last), rim_on], axis=0)
     off = lax.ppermute(off, "slab", off_pairs)
     on = lax.ppermute(on, "slab", on_pairs)
 
@@ -434,8 +449,9 @@
     return call(
         functools.partial(variation_kernel, slabs, rows),
         shape((planes, rows, lanes)),
-        [deep, deep, deep],
+        [deep, deep, deep, pltpu.SemaphoreType.DMA((4,))],
         field, off, on,
+        target=pl.BlockSpec(memory_space=pl.ANY),
     )
 
 

time: 65.7 us -> 65.2 us (level)
  no operation moved by 1% of the time
where the time goes in v7:
time: 65.2 us; the launch traced here: 64.8 us
  blocking collectives  27.8 us (43%)
  starting transfers between devices  26 us (40%)
  Pallas kernels  7.48 us (11%)
  waiting for transfers between devices  1.81 us (3%)
  other arithmetic  1.36 us (2%)
    all_to_all x1, blocking collectives, body(): parts = lax.all_to_all(back, 'view', 0, 0, tiled=True)  15.1 us
    all_to_all x1, blocking collectives, body(): field = lax.all_to_all(copies, 'view', 0, 0, tiled=True)  12.7 us
    pallas_call x5, Pallas kernels, call(): pl.pallas_call(kernel, out_shape=shapes, in_specs=specs, out_specs=jax.tr...  7.48 us
    ppermute x1, starting transfers between devices, body(): off = lax.ppermute(jnp.where(is_odd, high, low), 'slab', off_pairs)  6.02 us
    ppermute x1, starting transfers between devices, body(): off = lax.ppermute(off, 'slab', off_pairs)  4.65 us
    ppermute x1, starting transfers between devices, body(): strip = lax.ppermute(edge, 'row', [(0, 1), (1, 0)])  4.65 us
    ppermute x1, starting transfers between devices, body(): est_off = lax.ppermute(far, 'slab', off_pairs)  4.39 us
    ppermute x1, starting transfers between devices, body(): on = lax.ppermute(on, 'slab', on_pairs)  2.41 us
  transfers between devices with their start and end apart: 7, of which 2 were waited for; matrix products, arithmetic and copies ran while one was open for 0% of the time, Pallas kernels for 4%

profile of v7, /device:TPU:193, one launch (start us, length us, event | category | flops | bytes accessed | tf_op | source)
XLA Modules:
  0.0 64.8 jit_solution(16426400905788009394)
XLA Ops:
  0.0 1.2 %slice_select_fusion = (f32[1,4,64,256]{3,2,1,0:T(8,128)S(1)}, f32[1,4,64,256]{3,2,1,0:T(8,128)S(1)}) fusion(f32[1,8,64,256]{3,2,1,0:T(8,128)} %param.5, pred[]{:T(512)S(6)} %eq.6), kind=kLoop, calls=%fused_computation.2 | loop fusion | flops 131072 | bytes 1048577 | tf_op jit(solution)/shard_map/jit(_where)/select_n | solution.py:381
  1.2 0.1 copy-done
  1.3 0.1 copy-done.1
  1.4 4.7 %collective-permute-start.2 = (f32[8,24,256]{2,1,0:T(8,128)S(1)}, f32[8,24,256]{2,1,0:T(8,128)S(1)}, u32[]{:S(2)}, u32[]{:S(2)}) collective-permute-start(f32[8,24,256]{2,1,0:T(8,128)S(1)} %pad_maximum_fusion.2), channel_id=1, source_target_pairs={{0,1},{1,0},{2,3},{3,2},{4,5},{5,4},{6,7},{7,6},{8,9},{9,8},{10,11... | collective-permute-start | bytes 589832 | tf_op jit(solution)/shard_map/ppermute | solution.py:392
  6.1 0.1 pad_maximum_fusion
  6.1 0.0 copy-start.2
  6.1 0.0 copy-start.3
  6.2 4.4 %collective-permute-start = (f32[12,64,256]{2,1,0:T(8,128)S(1)}, f32[12,64,256]{2,1,0:T(8,128)S(1)}, u32[]{:S(2)}, u32[]{:S(2)}) collective-permute-start(f32[12,64,256]{2,1,0:T(8,128)S(1)} %pad_maximum_fusion), channel_id=1, source_target_pairs={{2,4},{6,8},{10,12},{14,16},{18,20},{22,24},{26,28},{30,32},{34,36... | collective-permute-start | bytes 2359304 | tf_op jit(solution)/shard_map/ppermute | solution.py:396
  10.6 1.9 %collective-permute-start.1 = (f32[8,64,256]{2,1,0:T(8,128)S(1)}, f32[8,64,256]{2,1,0:T(8,128)S(1)}, u32[]{:S(2)}, u32[]{:S(2)}) collective-permute-start(f32[8,64,256]{2,1,0:T(8,128)S(1)} %copy-done), channel_id=1, source_target_pairs={{0,2},{2,0},{4,6},{6,4},{8,10},{10,8},{12,14},{14,12},{16,18},{18,... | collective-permute-start | bytes 1572872 | tf_op jit(solution)/shard_map/ppermute | solution.py:397
  12.5 0.0 collective-permute-done.2.strip
  12.6 2.4 %collective-permute-start.4 = (f32[416,256]{1,0:T(8,128)S(1)}, f32[416,256]{1,0:T(8,128)S(1)}, u32[]{:S(2)}, u32[]{:S(2)}) collective-permute-start(f32[416,256]{1,0:T(8,128)S(1)} %pad_maximum_fusion.1), channel_id=1, source_target_pairs={{0,2},{2,0},{4,6},{6,4},{8,10},{10,8},{12,14},{14,12},{16,18},{18,... | collective-permute-start | bytes 1277960 | tf_op jit(solution)/shard_map/ppermute | solution.py:404
  15.0 4.7 %collective-permute-start.3 = (f32[160,256]{1,0:T(8,128)S(1)}, f32[160,256]{1,0:T(8,128)S(1)}, u32[]{:S(2)}, u32[]{:S(2)}) collective-permute-start(f32[160,256]{1,0:T(8,128)S(1)} %pad_maximum_fusion.3), channel_id=1, source_target_pairs={{2,4},{6,8},{10,12},{14,16},{18,20},{22,24},{26,28},{30,32},{34,36... | collective-permute-start | bytes 491528 | tf_op jit(solution)/shard_map/ppermute | solution.py:403
  19.7 1.3 %shard_map.55 = (f32[5,16,256]{2,1,0:T(8,128)S(1)}, bf16[256,256]{1,0:T(8,128)(2,1)S(1)}, bf16[256,256]{1,0:T(8,128)(2,1)S(1)}, bf16[288,256]{1,0:T(8,128)(2,1)S...) custom-call(s32[1,3]{1,0:T(1,128)S(1)} %copy-done.2, ...), custom_call_target="tpu_custom_call" | custom-call | flops 20000000000 | tf_op jit(solution)/shard_map/pallas_call | solution.py:355
  21.0 0.0 collective-permute-done.1.est_on
  21.0 1.5 %shard_map.56 = (f32[16,72,256]{2,1,0:T(8,128)S(1)}, f32[8,48,256]{2,1,0:T(8,128)S(1)}) custom-call(f32[8,64,256]{2,1,0:T(8,128)S(1)} %copy-done, f32[8,64,256]{2,1,0:T(8,128)S(1)} %bitcast.10, f32[12,64,256]{2,1,0:T(8,128)S(1)} %collective-permute-done.est_off, f32[8,64,256]{2,1,0:T(8,128)S(1)} %collective-permute-done.1.est_on, ...), custom_call_target="tpu_custom_call" | custom-call | tf_op jit(solution)/shard_map/pallas_call | solution.py:355
  22.6 0.1 collective-permute-done.3.off
  22.7 1.6 %shard_map.57 = f32[8,72,256]{2,1,0:T(8,128)S(1)} custom-call(f32[16,72,256]{2,1,0:T(8,128)S(1)} %get-tuple-element.34.partial, f32[8,48,256]{2,1,0:T(8,128)S(1)} %get-tuple-element.35.inner, f32[8,64,256]{2,1,0:T(8,128)S(1)} %bitcast.11, f32[8,24,256]{2,1,0:T(8,128)S(1)} %collective-permute-done.2.strip, f32[12,64,256]{2,1,0:T(8,128)S(1)} %collective-permute-done.est_off, ...), custom_call_target="tpu_custom_call" | custom-call | tf_op jit(solution)/shard_map/pallas_call | solution.py:355
  24.3 15.1 %all_to_all.10.parts = f32[8,72,256]{2,1,0:T(8,128)S(1)} all-to-all(f32[8,72,256]{2,1,0:T(8,128)S(1)} %shard_map.57), channel_id=1, replica_groups=mesh['view'=8,'slab'=32,'row'=2] {'view'}, dimensions={0} | all-to-all | bytes 1179648 | tf_op jit(solution)/shard_map/all_to_all | solution.py:436
  39.4 0.1 shard_map.58
  39.5 12.7 %all_to_all.11.field = f32[8,72,256]{2,1,0:T(8,128)S(1)} all-to-all(f32[8,72,256]{2,1,0:T(8,128)S(1)} %shard_map.58), channel_id=1, replica_groups=mesh['view'=8,'slab'=32,'row'=2] {'view'}, dimensions={0} | all-to-all | bytes 1179648 | tf_op jit(solution)/shard_map/all_to_all | solution.py:443
  52.2 6.0 %collective-permute-start.5 = (f32[3,72,256]{2,1,0:T(8,128)S(1)}, f32[3,72,256]{2,1,0:T(8,128)S(1)}, u32[]{:S(2)}, u32[]{:S(2)}) collective-permute-start(f32[3,72,256]{2,1,0:T(8,128)S(1)} %get-tuple-element.42), channel_id=1, source_target_pairs={{2,4},{6,8},{10,12},{14,16},{18,20},{22,24},{26,28},{30,32},{34,36... | collective-permute-start | bytes 663560 | tf_op jit(solution)/shard_map/ppermute | solution.py:446
  58.2 1.9 %collective-permute-start.6 = (f32[3,72,256]{2,1,0:T(8,128)S(1)}, f32[3,72,256]{2,1,0:T(8,128)S(1)}, u32[]{:S(2)}, u32[]{:S(2)}) collective-permute-start(f32[3,72,256]{2,1,0:T(8,128)S(1)} %get-tuple-element.41), channel_id=1, source_target_pairs={{0,2},{2,0},{4,6},{6,4},{8,10},{10,8},{12,14},{14,12},{16,18},{18,... | collective-permute-start | bytes 663560 | tf_op jit(solution)/shard_map/ppermute | solution.py:447
  60.2 1.7 %collective-permute-done.5.off = f32[3,72,256]{2,1,0:T(8,128)S(1)} collective-permute-done((f32[3,72,256]{2,1,0:T(8,128)S(1)}, f32[3,72,256]{2,1,0:T(8,128)S(1)}, u32[]{:S(2)}, u32[]{:S(2)}) %collective-permute-start.5) | collective-permute-done | bytes 221216 | tf_op jit(solution)/shard_map/ppermute | solution.py:446
  61.8 3.0 %shard_map.59 = f32[8,64,256]{2,1,0:T(8,128)} custom-call(f32[8,72,256]{2,1,0:T(8,128)S(1)} %all_to_all.11.field, f32[3,72,256]{2,1,0:T(8,128)S(1)} %collective-permute-done.5.off, f32[3,72,256]{2,1,0:T(8,128)S(1)} %collective-permute-done.6.on), custom_call_target="tpu_custom_call" | custom-call | tf_op jit(solution)/shard_map/pallas_call | solution.py:355
  (18 shorter events, 0.2 us)
Async XLA Ops:
  0.0 1.4 %copy-start.1 = (f32[1,8,64,256]{3,2,1,0:T(8,128)S(1)}, f32[1,8,64,256]{3,2,1,0:T(8,128)}, u32[]{:S(2)}) copy-start(f32[1,8,64,256]{3,2,1,0:T(8,128)} %param.5) | copy-start | bytes 1572868
  0.0 1.3 %copy-start = (f32[8,64,256]{2,1,0:T(8,128)S(1)}, f32[8,64,256]{2,1,0:T(8,128)}, u32[]{:S(2)}) copy-start(f32[8,64,256]{2,1,0:T(8,128)} %est.1) | copy-start | bytes 1572868
  1.4 11.1 %copy-start.4 = (f32[1,3,5]{2,0,1:T(1,128)S(1)}, f32[1,3,5]{2,0,1:T(1,128)}, u32[]{:S(2)}) copy-start(f32[1,3,5]{2,0,1:T(1,128)} %param.7) | copy-start | bytes 184
  1.4 11.1 %collective-permute-start.2 = (f32[8,24,256]{2,1,0:T(8,128)S(1)}, f32[8,24,256]{2,1,0:T(8,128)S(1)}, u32[]{:S(2)}, u32[]{:S(2)}) collective-permute-start(f32[8,24,256]{2,1,0:T(8,128)S(1)} %pad_maximum_fusion.2), channel_id=1, source_target_pairs={{0,1},{1,0},{2,3},{3,2},{4,5},{5,4},{6,7},{7,6},{8,9},{9,8},{10,11... | collective-permute-start | bytes 589832 | tf_op jit(solution)/shard_map/ppermute | solution.py:392
  6.1 13.6 %copy-start.2 = (s32[1,3]{1,0:T(1,128)S(1)}, s32[1,3]{1,0:T(1,128)}, u32[]{:S(2)}) copy-start(s32[1,3]{1,0:T(1,128)} %band.1) | copy-start | bytes 40
  6.1 13.5 %copy-start.3 = (s32[1,3]{1,0:T(1,128)S(1)}, s32[1,3]{1,0:T(1,128)}, u32[]{:S(2)}) copy-start(s32[1,3]{1,0:T(1,128)} %perm.1) | copy-start | bytes 40
  6.2 14.8 %collective-permute-start = (f32[12,64,256]{2,1,0:T(8,128)S(1)}, f32[12,64,256]{2,1,0:T(8,128)S(1)}, u32[]{:S(2)}, u32[]{:S(2)}) collective-permute-start(f32[12,64,256]{2,1,0:T(8,128)S(1)} %pad_maximum_fusion), channel_id=1, source_target_pairs={{2,4},{6,8},{10,12},{14,16},{18,20},{22,24},{26,28},{30,32},{34,36... | collective-permute-start | bytes 2359304 | tf_op jit(solution)/shard_map/ppermute | solution.py:396
  10.6 10.4 %collective-permute-start.1 = (f32[8,64,256]{2,1,0:T(8,128)S(1)}, f32[8,64,256]{2,1,0:T(8,128)S(1)}, u32[]{:S(2)}, u32[]{:S(2)}) collective-permute-start(f32[8,64,256]{2,1,0:T(8,128)S(1)} %copy-done), channel_id=1, source_target_pairs={{0,2},{2,0},{4,6},{6,4},{8,10},{10,8},{12,14},{14,12},{16,18},{18,... | collective-permute-start | bytes 1572872 | tf_op jit(solution)/shard_map/ppermute | solution.py:397
  12.6 10.1 %collective-permute-start.4 = (f32[416,256]{1,0:T(8,128)S(1)}, f32[416,256]{1,0:T(8,128)S(1)}, u32[]{:S(2)}, u32[]{:S(2)}) collective-permute-start(f32[416,256]{1,0:T(8,128)S(1)} %pad_maximum_fusion.1), channel_id=1, source_target_pairs={{0,2},{2,0},{4,6},{6,4},{8,10},{10,8},{12,14},{14,12},{16,18},{18,... | collective-permute-start | bytes 1277960 | tf_op jit(solution)/shard_map/ppermute | solution.py:404
  15.0 7.6 %collective-permute-start.3 = (f32[160,256]{1,0:T(8,128)S(1)}, f32[160,256]{1,0:T(8,128)S(1)}, u32[]{:S(2)}, u32[]{:S(2)}) collective-permute-start(f32[160,256]{1,0:T(8,128)S(1)} %pad_maximum_fusion.3), channel_id=1, source_target_pairs={{2,4},{6,8},{10,12},{14,16},{18,20},{22,24},{26,28},{30,32},{34,36... | collective-permute-start | bytes 491528 | tf_op jit(solution)/shard_map/ppermute | solution.py:403
  52.2 9.6 %collective-permute-start.5 = (f32[3,72,256]{2,1,0:T(8,128)S(1)}, f32[3,72,256]{2,1,0:T(8,128)S(1)}, u32[]{:S(2)}, u32[]{:S(2)}) collective-permute-start(f32[3,72,256]{2,1,0:T(8,128)S(1)} %get-tuple-element.42), channel_id=1, source_target_pairs={{2,4},{6,8},{10,12},{14,16},{18,20},{22,24},{26,28},{30,32},{34,36... | collective-permute-start | bytes 663560 | tf_op jit(solution)/shard_map/ppermute | solution.py:446
  58.2 3.6 %collective-permute-start.6 = (f32[3,72,256]{2,1,0:T(8,128)S(1)}, f32[3,72,256]{2,1,0:T(8,128)S(1)}, u32[]{:S(2)}, u32[]{:S(2)}) collective-permute-start(f32[3,72,256]{2,1,0:T(8,128)S(1)} %get-tuple-element.41), channel_id=1, source_target_pairs={{0,2},{2,0},{4,6},{6,4},{8,10},{10,8},{12,14},{14,12},{16,18},{18,... | collective-permute-start | bytes 663560 | tf_op jit(solution)/shard_map/ppermute | solution.py:447

commit v8 on v7

--- a/solution.py
+++ b/solution.py
@@ -214,7 +214,8 @@
             flat[p * pitch + used : (p + 1) * pitch, :] = jnp.zeros((pitch - used, lanes), F32)
         n = (high - low) * pitch
         x_h, x_l = split(flat[low * pitch : low * pitch + n, :])
-        return split(dot3(wy2_h[0:n, 0:n], wy2_l[0:n, 0:n], x_h, x_l))
+        mid = dot3(wy2_h[0:n, 0:n], wy2_l[0:n, 0:n], x_h, x_l).reshape(high - low, pitch, lanes)
+        return split(mid[:, :used].reshape(-1, lanes))
 
     beyond(True)
     ends = [data[:, 0:8, :], data[:, rows - 8 : rows, :], strip[:, EST_STRIP:thick, :]]
@@ -228,7 +229,7 @@
     mids += [second_blur(4, 6), second_blur(6, 8)]
     m_h = jnp.concatenate([m[0] for m in mids], axis=0)
     m_l = jnp.concatenate([m[1] for m in mids], axis=0)
-    out[...] = dot3(m_h, m_l, wx_h[...], wx_l[...]).reshape(planes, pitch, lanes)[:, :used]
+    out[...] = dot3(m_h, m_l, wx_h[...], wx_l[...]).reshape(planes, used, lanes)
 
 
 def field_kernel(views, rows, parts, est, strip, out):

time: 65.2 us -> 65.2 us (level)
  the two profiles are of different devices: /device:TPU:193 before, /device:TPU:65 now
where the time goes in v8:
time: 65.2 us; the launch traced here: 64.8 us
  blocking collectives  27.8 us (43%)
  starting transfers between devices  26 us (40%)
  Pallas kernels  7.45 us (11%)
  waiting for transfers between devices  1.8 us (3%)
  other arithmetic  1.36 us (2%)
    all_to_all x1, blocking collectives, body(): parts = lax.all_to_all(back, 'view', 0, 0, tiled=True)  15.1 us
    all_to_all x1, blocking collectives, body(): field = lax.all_to_all(copies, 'view', 0, 0, tiled=True)  12.7 us
    pallas_call x5, Pallas kernels, call(): pl.pallas_call(kernel, out_shape=shapes, in_specs=specs, out_specs=jax.tr...  7.45 us
    ppermute x1, starting transfers between devices, body(): off = lax.ppermute(jnp.where(is_odd, high, low), 'slab', off_pairs)  6.02 us
    ppermute x1, starting transfers between devices, body(): off = lax.ppermute(off, 'slab', off_pairs)  4.65 us
    ppermute x1, starting transfers between devices, body(): strip = lax.ppermute(edge, 'row', [(0, 1), (1, 0)])  4.65 us
    ppermute x1, starting transfers between devices, body(): est_off = lax.ppermute(far, 'slab', off_pairs)  4.39 us
    ppermute x1, starting transfers between devices, body(): on = lax.ppermute(on, 'slab', on_pairs)  2.41 us
  transfers between devices with their start and end apart: 7, of which 2 were waited for; matrix products, arithmetic and copies ran while one was open for 0% of the time, Pallas kernels for 4%

profile of v8, /device:TPU:65, one launch (start us, length us, event | category | flops | bytes accessed | tf_op | source)
XLA Modules:
  0.0 64.8 jit_solution(1521093081523807204)
XLA Ops:
  0.0 1.2 %slice_select_fusion = (f32[1,4,64,256]{3,2,1,0:T(8,128)S(1)}, f32[1,4,64,256]{3,2,1,0:T(8,128)S(1)}) fusion(f32[1,8,64,256]{3,2,1,0:T(8,128)} %param.5, pred[]{:T(512)S(6)} %eq.6), kind=kLoop, calls=%fused_computation.2 | loop fusion | flops 131072 | bytes 1048577 | tf_op jit(solution)/shard_map/jit(_where)/select_n | solution.py:382
  1.2 0.1 copy-done
  1.3 0.1 copy-done.1
  1.4 4.7 %collective-permute-start.2 = (f32[8,24,256]{2,1,0:T(8,128)S(1)}, f32[8,24,256]{2,1,0:T(8,128)S(1)}, u32[]{:S(2)}, u32[]{:S(2)}) collective-permute-start(f32[8,24,256]{2,1,0:T(8,128)S(1)} %pad_maximum_fusion.2), channel_id=1, source_target_pairs={{0,1},{1,0},{2,3},{3,2},{4,5},{5,4},{6,7},{7,6},{8,9},{9,8},{10,11... | collective-permute-start | bytes 589832 | tf_op jit(solution)/shard_map/ppermute | solution.py:393
  6.1 0.1 pad_maximum_fusion
  6.1 0.0 copy-start.2
  6.1 0.0 copy-start.3
  6.2 4.4 %collective-permute-start = (f32[12,64,256]{2,1,0:T(8,128)S(1)}, f32[12,64,256]{2,1,0:T(8,128)S(1)}, u32[]{:S(2)}, u32[]{:S(2)}) collective-permute-start(f32[12,64,256]{2,1,0:T(8,128)S(1)} %pad_maximum_fusion), channel_id=1, source_target_pairs={{2,4},{6,8},{10,12},{14,16},{18,20},{22,24},{26,28},{30,32},{34,36... | collective-permute-start | bytes 2359304 | tf_op jit(solution)/shard_map/ppermute | solution.py:397
  10.6 1.9 %collective-permute-start.1 = (f32[8,64,256]{2,1,0:T(8,128)S(1)}, f32[8,64,256]{2,1,0:T(8,128)S(1)}, u32[]{:S(2)}, u32[]{:S(2)}) collective-permute-start(f32[8,64,256]{2,1,0:T(8,128)S(1)} %copy-done), channel_id=1, source_target_pairs={{0,2},{2,0},{4,6},{6,4},{8,10},{10,8},{12,14},{14,12},{16,18},{18,... | collective-permute-start | bytes 1572872 | tf_op jit(solution)/shard_map/ppermute | solution.py:398
  12.6 2.4 %collective-permute-start.4 = (f32[416,256]{1,0:T(8,128)S(1)}, f32[416,256]{1,0:T(8,128)S(1)}, u32[]{:S(2)}, u32[]{:S(2)}) collective-permute-start(f32[416,256]{1,0:T(8,128)S(1)} %pad_maximum_fusion.1), channel_id=1, source_target_pairs={{0,2},{2,0},{4,6},{6,4},{8,10},{10,8},{12,14},{14,12},{16,18},{18,... | collective-permute-start | bytes 1277960 | tf_op jit(solution)/shard_map/ppermute | solution.py:405
  15.0 4.7 %collective-permute-start.3 = (f32[160,256]{1,0:T(8,128)S(1)}, f32[160,256]{1,0:T(8,128)S(1)}, u32[]{:S(2)}, u32[]{:S(2)}) collective-permute-start(f32[160,256]{1,0:T(8,128)S(1)} %pad_maximum_fusion.3), channel_id=1, source_target_pairs={{2,4},{6,8},{10,12},{14,16},{18,20},{22,24},{26,28},{30,32},{34,36... | collective-permute-start | bytes 491528 | tf_op jit(solution)/shard_map/ppermute | solution.py:404
  19.7 1.3 %shard_map.55 = (f32[5,16,256]{2,1,0:T(8,128)S(1)}, bf16[256,256]{1,0:T(8,128)(2,1)S(1)}, bf16[256,256]{1,0:T(8,128)(2,1)S(1)}, bf16[288,256]{1,0:T(8,128)(2,1)S...) custom-call(s32[1,3]{1,0:T(1,128)S(1)} %copy-done.2, ...), custom_call_target="tpu_custom_call" | custom-call | flops 20000000000 | tf_op jit(solution)/shard_map/pallas_call | solution.py:356
  21.0 0.0 collective-permute-done.1.est_on
  21.0 1.5 %shard_map.56 = (f32[16,72,256]{2,1,0:T(8,128)S(1)}, f32[8,48,256]{2,1,0:T(8,128)S(1)}) custom-call(f32[8,64,256]{2,1,0:T(8,128)S(1)} %copy-done, f32[8,64,256]{2,1,0:T(8,128)S(1)} %bitcast.10, f32[12,64,256]{2,1,0:T(8,128)S(1)} %collective-permute-done.est_off, f32[8,64,256]{2,1,0:T(8,128)S(1)} %collective-permute-done.1.est_on, ...), custom_call_target="tpu_custom_call" | custom-call | tf_op jit(solution)/shard_map/pallas_call | solution.py:356
  22.6 0.1 collective-permute-done.3.off
  22.7 0.0 collective-permute-done.4.on
  22.7 1.6 %shard_map.57 = f32[8,72,256]{2,1,0:T(8,128)S(1)} custom-call(f32[16,72,256]{2,1,0:T(8,128)S(1)} %get-tuple-element.34.partial, f32[8,48,256]{2,1,0:T(8,128)S(1)} %get-tuple-element.35.inner, f32[8,64,256]{2,1,0:T(8,128)S(1)} %bitcast.11, f32[8,24,256]{2,1,0:T(8,128)S(1)} %collective-permute-done.2.strip, f32[12,64,256]{2,1,0:T(8,128)S(1)} %collective-permute-done.est_off, ...), custom_call_target="tpu_custom_call" | custom-call | tf_op jit(solution)/shard_map/pallas_call | solution.py:356
  24.3 15.1 %all_to_all.10.parts = f32[8,72,256]{2,1,0:T(8,128)S(1)} all-to-all(f32[8,72,256]{2,1,0:T(8,128)S(1)} %shard_map.57), channel_id=1, replica_groups=mesh['view'=8,'slab'=32,'row'=2] {'view'}, dimensions={0} | all-to-all | bytes 1179648 | tf_op jit(solution)/shard_map/all_to_all | solution.py:437
  39.4 0.1 shard_map.58
  39.5 12.7 %all_to_all.11.field = f32[8,72,256]{2,1,0:T(8,128)S(1)} all-to-all(f32[8,72,256]{2,1,0:T(8,128)S(1)} %shard_map.58), channel_id=1, replica_groups=mesh['view'=8,'slab'=32,'row'=2] {'view'}, dimensions={0} | all-to-all | bytes 1179648 | tf_op jit(solution)/shard_map/all_to_all | solution.py:444
  52.2 6.0 %collective-permute-start.5 = (f32[3,72,256]{2,1,0:T(8,128)S(1)}, f32[3,72,256]{2,1,0:T(8,128)S(1)}, u32[]{:S(2)}, u32[]{:S(2)}) collective-permute-start(f32[3,72,256]{2,1,0:T(8,128)S(1)} %get-tuple-element.42), channel_id=1, source_target_pairs={{2,4},{6,8},{10,12},{14,16},{18,20},{22,24},{26,28},{30,32},{34,36... | collective-permute-start | bytes 663560 | tf_op jit(solution)/shard_map/ppermute | solution.py:447
  58.2 1.9 %collective-permute-start.6 = (f32[3,72,256]{2,1,0:T(8,128)S(1)}, f32[3,72,256]{2,1,0:T(8,128)S(1)}, u32[]{:S(2)}, u32[]{:S(2)}) collective-permute-start(f32[3,72,256]{2,1,0:T(8,128)S(1)} %get-tuple-element.41), channel_id=1, source_target_pairs={{0,2},{2,0},{4,6},{6,4},{8,10},{10,8},{12,14},{14,12},{16,18},{18,... | collective-permute-start | bytes 663560 | tf_op jit(solution)/shard_map/ppermute | solution.py:448
  60.1 1.7 %collective-permute-done.5.off = f32[3,72,256]{2,1,0:T(8,128)S(1)} collective-permute-done((f32[3,72,256]{2,1,0:T(8,128)S(1)}, f32[3,72,256]{2,1,0:T(8,128)S(1)}, u32[]{:S(2)}, u32[]{:S(2)}) %collective-permute-start.5) | collective-permute-done | bytes 221216 | tf_op jit(solution)/shard_map/ppermute | solution.py:447
  61.8 3.0 %shard_map.59 = f32[8,64,256]{2,1,0:T(8,128)} custom-call(f32[8,72,256]{2,1,0:T(8,128)S(1)} %all_to_all.11.field, f32[3,72,256]{2,1,0:T(8,128)S(1)} %collective-permute-done.5.off, f32[3,72,256]{2,1,0:T(8,128)S(1)} %collective-permute-done.6.on), custom_call_target="tpu_custom_call" | custom-call | tf_op jit(solution)/shard_map/pallas_call | solution.py:356
  (18 shorter events, 0.2 us)
Async XLA Ops:
  0.0 1.4 %copy-start.1 = (f32[1,8,64,256]{3,2,1,0:T(8,128)S(1)}, f32[1,8,64,256]{3,2,1,0:T(8,128)}, u32[]{:S(2)}) copy-start(f32[1,8,64,256]{3,2,1,0:T(8,128)} %param.5) | copy-start | bytes 1572868
  0.0 1.3 %copy-start = (f32[8,64,256]{2,1,0:T(8,128)S(1)}, f32[8,64,256]{2,1,0:T(8,128)}, u32[]{:S(2)}) copy-start(f32[8,64,256]{2,1,0:T(8,128)} %est.1) | copy-start | bytes 1572868
  1.4 11.1 %copy-start.4 = (f32[1,3,5]{2,0,1:T(1,128)S(1)}, f32[1,3,5]{2,0,1:T(1,128)}, u32[]{:S(2)}) copy-start(f32[1,3,5]{2,0,1:T(1,128)} %param.7) | copy-start | bytes 184
  1.4 11.1 %collective-permute-start.2 = (f32[8,24,256]{2,1,0:T(8,128)S(1)}, f32[8,24,256]{2,1,0:T(8,128)S(1)}, u32[]{:S(2)}, u32[]{:S(2)}) collective-permute-start(f32[8,24,256]{2,1,0:T(8,128)S(1)} %pad_maximum_fusion.2), channel_id=1, source_target_pairs={{0,1},{1,0},{2,3},{3,2},{4,5},{5,4},{6,7},{7,6},{8,9},{9,8},{10,11... | collective-permute-start | bytes 589832 | tf_op jit(solution)/shard_map/ppermute | solution.py:393
  6.1 13.6 %copy-start.2 = (s32[1,3]{1,0:T(1,128)S(1)}, s32[1,3]{1,0:T(1,128)}, u32[]{:S(2)}) copy-start(s32[1,3]{1,0:T(1,128)} %band.1) | copy-start | bytes 40
  6.1 13.5 %copy-start.3 = (s32[1,3]{1,0:T(1,128)S(1)}, s32[1,3]{1,0:T(1,128)}, u32[]{:S(2)}) copy-start(s32[1,3]{1,0:T(1,128)} %perm.1) | copy-start | bytes 40
  6.2 14.8 %collective-permute-start = (f32[12,64,256]{2,1,0:T(8,128)S(1)}, f32[12,64,256]{2,1,0:T(8,128)S(1)}, u32[]{:S(2)}, u32[]{:S(2)}) collective-permute-start(f32[12,64,256]{2,1,0:T(8,128)S(1)} %pad_maximum_fusion), channel_id=1, source_target_pairs={{2,4},{6,8},{10,12},{14,16},{18,20},{22,24},{26,28},{30,32},{34,36... | collective-permute-start | bytes 2359304 | tf_op jit(solution)/shard_map/ppermute | solution.py:397
  10.6 10.4 %collective-permute-start.1 = (f32[8,64,256]{2,1,0:T(8,128)S(1)}, f32[8,64,256]{2,1,0:T(8,128)S(1)}, u32[]{:S(2)}, u32[]{:S(2)}) collective-permute-start(f32[8,64,256]{2,1,0:T(8,128)S(1)} %copy-done), channel_id=1, source_target_pairs={{0,2},{2,0},{4,6},{6,4},{8,10},{10,8},{12,14},{14,12},{16,18},{18,... | collective-permute-start | bytes 1572872 | tf_op jit(solution)/shard_map/ppermute | solution.py:398
  12.6 10.1 %collective-permute-start.4 = (f32[416,256]{1,0:T(8,128)S(1)}, f32[416,256]{1,0:T(8,128)S(1)}, u32[]{:S(2)}, u32[]{:S(2)}) collective-permute-start(f32[416,256]{1,0:T(8,128)S(1)} %pad_maximum_fusion.1), channel_id=1, source_target_pairs={{0,2},{2,0},{4,6},{6,4},{8,10},{10,8},{12,14},{14,12},{16,18},{18,... | collective-permute-start | bytes 1277960 | tf_op jit(solution)/shard_map/ppermute | solution.py:405
  15.0 7.6 %collective-permute-start.3 = (f32[160,256]{1,0:T(8,128)S(1)}, f32[160,256]{1,0:T(8,128)S(1)}, u32[]{:S(2)}, u32[]{:S(2)}) collective-permute-start(f32[160,256]{1,0:T(8,128)S(1)} %pad_maximum_fusion.3), channel_id=1, source_target_pairs={{2,4},{6,8},{10,12},{14,16},{18,20},{22,24},{26,28},{30,32},{34,36... | collective-permute-start | bytes 491528 | tf_op jit(solution)/shard_map/ppermute | solution.py:404
  52.2 9.6 %collective-permute-start.5 = (f32[3,72,256]{2,1,0:T(8,128)S(1)}, f32[3,72,256]{2,1,0:T(8,128)S(1)}, u32[]{:S(2)}, u32[]{:S(2)}) collective-permute-start(f32[3,72,256]{2,1,0:T(8,128)S(1)} %get-tuple-element.42), channel_id=1, source_target_pairs={{2,4},{6,8},{10,12},{14,16},{18,20},{22,24},{26,28},{30,32},{34,36... | collective-permute-start | bytes 663560 | tf_op jit(solution)/shard_map/ppermute | solution.py:447
  58.2 3.6 %collective-permute-start.6 = (f32[3,72,256]{2,1,0:T(8,128)S(1)}, f32[3,72,256]{2,1,0:T(8,128)S(1)}, u32[]{:S(2)}, u32[]{:S(2)}) collective-permute-start(f32[3,72,256]{2,1,0:T(8,128)S(1)} %get-tuple-element.41), channel_id=1, source_target_pairs={{0,2},{2,0},{4,6},{6,4},{8,10},{10,8},{12,14},{14,12},{16,18},{18,... | collective-permute-start | bytes 663560 | tf_op jit(solution)/shard_map/ppermute | solution.py:448

commit v9 on v7

--- a/solution.py
+++ b/solution.py
@@ -330,7 +330,7 @@
                 then(z, count)
 
     deep = planes + 2 * TV_HALO
-    groups = (4, 5, 3)
+    groups = (6, 5, 3)
     one_pass(start, 1, deep - 1, groups[0], first)
     one_pass(first, 2, deep - 2, groups[1], second)
     skip = pl.multiple_of(row * (used - rows), 8)

time: 65.2 us -> 65.2 us (level)
  no operation moved by 1% of the time
where the time goes in v9:
time: 65.2 us; the launch traced here: 64.8 us
  blocking collectives  27.8 us (43%)
  starting transfers between devices  26 us (40%)
  Pallas kernels  7.5 us (12%)
  waiting for transfers between devices  1.81 us (3%)
  other arithmetic  1.36 us (2%)
    all_to_all x1, blocking collectives, body(): parts = lax.all_to_all(back, 'view', 0, 0, tiled=True)  15.1 us
    all_to_all x1, blocking collectives, body(): field = lax.all_to_all(copies, 'view', 0, 0, tiled=True)  12.7 us
    pallas_call x5, Pallas kernels, call(): pl.pallas_call(kernel, out_shape=shapes, in_specs=specs, out_specs=jax.tr...  7.5 us
    ppermute x1, starting transfers between devices, body(): off = lax.ppermute(jnp.where(is_odd, high, low), 'slab', off_pairs)  6.02 us
    ppermute x1, starting transfers between devices, body(): off = lax.ppermute(off, 'slab', off_pairs)  4.65 us
    ppermute x1, starting transfers between devices, body(): strip = lax.ppermute(edge, 'row', [(0, 1), (1, 0)])  4.65 us
    ppermute x1, starting transfers between devices, body(): est_off = lax.ppermute(far, 'slab', off_pairs)  4.39 us
    ppermute x1, starting transfers between devices, body(): on = lax.ppermute(on, 'slab', on_pairs)  2.41 us
  transfers between devices with their start and end apart: 7, of which 2 were waited for; matrix products, arithmetic and copies ran while one was open for 0% of the time, Pallas kernels for 4%

profile of v9, /device:TPU:193, one launch (start us, length us, event | category | flops | bytes accessed | tf_op | source)
XLA Modules:
  0.0 64.8 jit_solution(14001932803818408962)
XLA Ops:
  0.0 1.2 %slice_select_fusion = (f32[1,4,64,256]{3,2,1,0:T(8,128)S(1)}, f32[1,4,64,256]{3,2,1,0:T(8,128)S(1)}) fusion(f32[1,8,64,256]{3,2,1,0:T(8,128)} %param.5, pred[]{:T(512)S(6)} %eq.6), kind=kLoop, calls=%fused_computation.2 | loop fusion | flops 131072 | bytes 1048577 | tf_op jit(solution)/shard_map/jit(_where)/select_n | solution.py:381
  1.2 0.1 copy-done
  1.3 0.1 copy-done.1
  1.4 4.7 %collective-permute-start.2 = (f32[8,24,256]{2,1,0:T(8,128)S(1)}, f32[8,24,256]{2,1,0:T(8,128)S(1)}, u32[]{:S(2)}, u32[]{:S(2)}) collective-permute-start(f32[8,24,256]{2,1,0:T(8,128)S(1)} %pad_maximum_fusion.2), channel_id=1, source_target_pairs={{0,1},{1,0},{2,3},{3,2},{4,5},{5,4},{6,7},{7,6},{8,9},{9,8},{10,11... | collective-permute-start | bytes 589832 | tf_op jit(solution)/shard_map/ppermute | solution.py:392
  6.1 0.1 pad_maximum_fusion
  6.1 0.0 copy-start.2
  6.1 0.0 copy-start.3
  6.2 4.4 %collective-permute-start = (f32[12,64,256]{2,1,0:T(8,128)S(1)}, f32[12,64,256]{2,1,0:T(8,128)S(1)}, u32[]{:S(2)}, u32[]{:S(2)}) collective-permute-start(f32[12,64,256]{2,1,0:T(8,128)S(1)} %pad_maximum_fusion), channel_id=1, source_target_pairs={{2,4},{6,8},{10,12},{14,16},{18,20},{22,24},{26,28},{30,32},{34,36... | collective-permute-start | bytes 2359304 | tf_op jit(solution)/shard_map/ppermute | solution.py:396
  10.6 1.9 %collective-permute-start.1 = (f32[8,64,256]{2,1,0:T(8,128)S(1)}, f32[8,64,256]{2,1,0:T(8,128)S(1)}, u32[]{:S(2)}, u32[]{:S(2)}) collective-permute-start(f32[8,64,256]{2,1,0:T(8,128)S(1)} %copy-done), channel_id=1, source_target_pairs={{0,2},{2,0},{4,6},{6,4},{8,10},{10,8},{12,14},{14,12},{16,18},{18,... | collective-permute-start | bytes 1572872 | tf_op jit(solution)/shard_map/ppermute | solution.py:397
  12.5 0.0 collective-permute-done.2.strip
  12.6 2.4 %collective-permute-start.4 = (f32[416,256]{1,0:T(8,128)S(1)}, f32[416,256]{1,0:T(8,128)S(1)}, u32[]{:S(2)}, u32[]{:S(2)}) collective-permute-start(f32[416,256]{1,0:T(8,128)S(1)} %pad_maximum_fusion.1), channel_id=1, source_target_pairs={{0,2},{2,0},{4,6},{6,4},{8,10},{10,8},{12,14},{14,12},{16,18},{18,... | collective-permute-start | bytes 1277960 | tf_op jit(solution)/shard_map/ppermute | solution.py:404
  15.0 4.7 %collective-permute-start.3 = (f32[160,256]{1,0:T(8,128)S(1)}, f32[160,256]{1,0:T(8,128)S(1)}, u32[]{:S(2)}, u32[]{:S(2)}) collective-permute-start(f32[160,256]{1,0:T(8,128)S(1)} %pad_maximum_fusion.3), channel_id=1, source_target_pairs={{2,4},{6,8},{10,12},{14,16},{18,20},{22,24},{26,28},{30,32},{34,36... | collective-permute-start | bytes 491528 | tf_op jit(solution)/shard_map/ppermute | solution.py:403
  19.7 1.3 %shard_map.55 = (f32[5,16,256]{2,1,0:T(8,128)S(1)}, bf16[256,256]{1,0:T(8,128)(2,1)S(1)}, bf16[256,256]{1,0:T(8,128)(2,1)S(1)}, bf16[288,256]{1,0:T(8,128)(2,1)S...) custom-call(s32[1,3]{1,0:T(1,128)S(1)} %copy-done.2, ...), custom_call_target="tpu_custom_call" | custom-call | flops 20000000000 | tf_op jit(solution)/shard_map/pallas_call | solution.py:355
  21.0 0.0 collective-permute-done.1.est_on
  21.0 1.5 %shard_map.56 = (f32[16,72,256]{2,1,0:T(8,128)S(1)}, f32[8,48,256]{2,1,0:T(8,128)S(1)}) custom-call(f32[8,64,256]{2,1,0:T(8,128)S(1)} %copy-done, f32[8,64,256]{2,1,0:T(8,128)S(1)} %bitcast.10, f32[12,64,256]{2,1,0:T(8,128)S(1)} %collective-permute-done.est_off, f32[8,64,256]{2,1,0:T(8,128)S(1)} %collective-permute-done.1.est_on, ...), custom_call_target="tpu_custom_call" | custom-call | tf_op jit(solution)/shard_map/pallas_call | solution.py:355
  22.6 0.1 collective-permute-done.3.off
  22.7 1.6 %shard_map.57 = f32[8,72,256]{2,1,0:T(8,128)S(1)} custom-call(f32[16,72,256]{2,1,0:T(8,128)S(1)} %get-tuple-element.34.partial, f32[8,48,256]{2,1,0:T(8,128)S(1)} %get-tuple-element.35.inner, f32[8,64,256]{2,1,0:T(8,128)S(1)} %bitcast.11, f32[8,24,256]{2,1,0:T(8,128)S(1)} %collective-permute-done.2.strip, f32[12,64,256]{2,1,0:T(8,128)S(1)} %collective-permute-done.est_off, ...), custom_call_target="tpu_custom_call" | custom-call | tf_op jit(solution)/shard_map/pallas_call | solution.py:355
  24.3 15.1 %all_to_all.10.parts = f32[8,72,256]{2,1,0:T(8,128)S(1)} all-to-all(f32[8,72,256]{2,1,0:T(8,128)S(1)} %shard_map.57), channel_id=1, replica_groups=mesh['view'=8,'slab'=32,'row'=2] {'view'}, dimensions={0} | all-to-all | bytes 1179648 | tf_op jit(solution)/shard_map/all_to_all | solution.py:436
  39.4 0.1 shard_map.58
  39.5 12.7 %all_to_all.11.field = f32[8,72,256]{2,1,0:T(8,128)S(1)} all-to-all(f32[8,72,256]{2,1,0:T(8,128)S(1)} %shard_map.58), channel_id=1, replica_groups=mesh['view'=8,'slab'=32,'row'=2] {'view'}, dimensions={0} | all-to-all | bytes 1179648 | tf_op jit(solution)/shard_map/all_to_all | solution.py:443
  52.2 6.0 %collective-permute-start.5 = (f32[3,72,256]{2,1,0:T(8,128)S(1)}, f32[3,72,256]{2,1,0:T(8,128)S(1)}, u32[]{:S(2)}, u32[]{:S(2)}) collective-permute-start(f32[3,72,256]{2,1,0:T(8,128)S(1)} %get-tuple-element.42), channel_id=1, source_target_pairs={{2,4},{6,8},{10,12},{14,16},{18,20},{22,24},{26,28},{30,32},{34,36... | collective-permute-start | bytes 663560 | tf_op jit(solution)/shard_map/ppermute | solution.py:446
  58.2 1.9 %collective-permute-start.6 = (f32[3,72,256]{2,1,0:T(8,128)S(1)}, f32[3,72,256]{2,1,0:T(8,128)S(1)}, u32[]{:S(2)}, u32[]{:S(2)}) collective-permute-start(f32[3,72,256]{2,1,0:T(8,128)S(1)} %get-tuple-element.41), channel_id=1, source_target_pairs={{0,2},{2,0},{4,6},{6,4},{8,10},{10,8},{12,14},{14,12},{16,18},{18,... | collective-permute-start | bytes 663560 | tf_op jit(solution)/shard_map/ppermute | solution.py:447
  60.2 1.7 %collective-permute-done.5.off = f32[3,72,256]{2,1,0:T(8,128)S(1)} collective-permute-done((f32[3,72,256]{2,1,0:T(8,128)S(1)}, f32[3,72,256]{2,1,0:T(8,128)S(1)}, u32[]{:S(2)}, u32[]{:S(2)}) %collective-permute-start.5) | collective-permute-done | bytes 221216 | tf_op jit(solution)/shard_map/ppermute | solution.py:446
  61.8 3.0 %shard_map.59 = f32[8,64,256]{2,1,0:T(8,128)} custom-call(f32[8,72,256]{2,1,0:T(8,128)S(1)} %all_to_all.11.field, f32[3,72,256]{2,1,0:T(8,128)S(1)} %collective-permute-done.5.off, f32[3,72,256]{2,1,0:T(8,128)S(1)} %collective-permute-done.6.on), custom_call_target="tpu_custom_call" | custom-call | tf_op jit(solution)/shard_map/pallas_call | solution.py:355
  (18 shorter events, 0.2 us)
Async XLA Ops:
  0.0 1.4 %copy-start.1 = (f32[1,8,64,256]{3,2,1,0:T(8,128)S(1)}, f32[1,8,64,256]{3,2,1,0:T(8,128)}, u32[]{:S(2)}) copy-start(f32[1,8,64,256]{3,2,1,0:T(8,128)} %param.5) | copy-start | bytes 1572868
  0.0 1.3 %copy-start = (f32[8,64,256]{2,1,0:T(8,128)S(1)}, f32[8,64,256]{2,1,0:T(8,128)}, u32[]{:S(2)}) copy-start(f32[8,64,256]{2,1,0:T(8,128)} %est.1) | copy-start | bytes 1572868
  1.4 11.1 %copy-start.4 = (f32[1,3,5]{2,0,1:T(1,128)S(1)}, f32[1,3,5]{2,0,1:T(1,128)}, u32[]{:S(2)}) copy-start(f32[1,3,5]{2,0,1:T(1,128)} %param.7) | copy-start | bytes 184
  1.4 11.1 %collective-permute-start.2 = (f32[8,24,256]{2,1,0:T(8,128)S(1)}, f32[8,24,256]{2,1,0:T(8,128)S(1)}, u32[]{:S(2)}, u32[]{:S(2)}) collective-permute-start(f32[8,24,256]{2,1,0:T(8,128)S(1)} %pad_maximum_fusion.2), channel_id=1, source_target_pairs={{0,1},{1,0},{2,3},{3,2},{4,5},{5,4},{6,7},{7,6},{8,9},{9,8},{10,11... | collective-permute-start | bytes 589832 | tf_op jit(solution)/shard_map/ppermute | solution.py:392
  6.1 13.6 %copy-start.2 = (s32[1,3]{1,0:T(1,128)S(1)}, s32[1,3]{1,0:T(1,128)}, u32[]{:S(2)}) copy-start(s32[1,3]{1,0:T(1,128)} %band.1) | copy-start | bytes 40
  6.1 13.5 %copy-start.3 = (s32[1,3]{1,0:T(1,128)S(1)}, s32[1,3]{1,0:T(1,128)}, u32[]{:S(2)}) copy-start(s32[1,3]{1,0:T(1,128)} %perm.1) | copy-start | bytes 40
  6.2 14.8 %collective-permute-start = (f32[12,64,256]{2,1,0:T(8,128)S(1)}, f32[12,64,256]{2,1,0:T(8,128)S(1)}, u32[]{:S(2)}, u32[]{:S(2)}) collective-permute-start(f32[12,64,256]{2,1,0:T(8,128)S(1)} %pad_maximum_fusion), channel_id=1, source_target_pairs={{2,4},{6,8},{10,12},{14,16},{18,20},{22,24},{26,28},{30,32},{34,36... | collective-permute-start | bytes 2359304 | tf_op jit(solution)/shard_map/ppermute | solution.py:396
  10.6 10.4 %collective-permute-start.1 = (f32[8,64,256]{2,1,0:T(8,128)S(1)}, f32[8,64,256]{2,1,0:T(8,128)S(1)}, u32[]{:S(2)}, u32[]{:S(2)}) collective-permute-start(f32[8,64,256]{2,1,0:T(8,128)S(1)} %copy-done), channel_id=1, source_target_pairs={{0,2},{2,0},{4,6},{6,4},{8,10},{10,8},{12,14},{14,12},{16,18},{18,... | collective-permute-start | bytes 1572872 | tf_op jit(solution)/shard_map/ppermute | solution.py:397
  12.6 10.1 %collective-permute-start.4 = (f32[416,256]{1,0:T(8,128)S(1)}, f32[416,256]{1,0:T(8,128)S(1)}, u32[]{:S(2)}, u32[]{:S(2)}) collective-permute-start(f32[416,256]{1,0:T(8,128)S(1)} %pad_maximum_fusion.1), channel_id=1, source_target_pairs={{0,2},{2,0},{4,6},{6,4},{8,10},{10,8},{12,14},{14,12},{16,18},{18,... | collective-permute-start | bytes 1277960 | tf_op jit(solution)/shard_map/ppermute | solution.py:404
  15.0 7.6 %collective-permute-start.3 = (f32[160,256]{1,0:T(8,128)S(1)}, f32[160,256]{1,0:T(8,128)S(1)}, u32[]{:S(2)}, u32[]{:S(2)}) collective-permute-start(f32[160,256]{1,0:T(8,128)S(1)} %pad_maximum_fusion.3), channel_id=1, source_target_pairs={{2,4},{6,8},{10,12},{14,16},{18,20},{22,24},{26,28},{30,32},{34,36... | collective-permute-start | bytes 491528 | tf_op jit(solution)/shard_map/ppermute | solution.py:403
  52.2 9.6 %collective-permute-start.5 = (f32[3,72,256]{2,1,0:T(8,128)S(1)}, f32[3,72,256]{2,1,0:T(8,128)S(1)}, u32[]{:S(2)}, u32[]{:S(2)}) collective-permute-start(f32[3,72,256]{2,1,0:T(8,128)S(1)} %get-tuple-element.42), channel_id=1, source_target_pairs={{2,4},{6,8},{10,12},{14,16},{18,20},{22,24},{26,28},{30,32},{34,36... | collective-permute-start | bytes 663560 | tf_op jit(solution)/shard_map/ppermute | solution.py:446
  58.2 3.6 %collective-permute-start.6 = (f32[3,72,256]{2,1,0:T(8,128)S(1)}, f32[3,72,256]{2,1,0:T(8,128)S(1)}, u32[]{:S(2)}, u32[]{:S(2)}) collective-permute-start(f32[3,72,256]{2,1,0:T(8,128)S(1)} %get-tuple-element.41), channel_id=1, source_target_pairs={{0,2},{2,0},{4,6},{6,4},{8,10},{10,8},{12,14},{14,12},{16,18},{18,... | collective-permute-start | bytes 663560 | tf_op jit(solution)/shard_map/ppermute | solution.py:447
